TPU v7x, 1024 devices: a whole 4x8x16 slice. The times are simulated.
1024 devices in a mesh: seq: 32 (over z, core), exp: 8 (over y), head: 4 (over x).
Axes of the slice: x: 4, y: 8, z: 16, core: 2. Of those that a mesh axis runs over, the one named last changes fastest.
Arguments:
- resid: bfloat16 [4096, 4096], P('seq'), may hold values from -6 to 6
- grad_out: bfloat16 [4096, 4096], P('seq'), may hold values from -6 to 6
- norm_gain: bfloat16 [4096], replicated, may hold values from 0.25 to 1.75
- expert_ids: int32 [4096, 2], P('seq'), may hold values from 0 to 7, all different within a row; in each aligned block of 32 rows (0 to 31, 32 to 63, ...) at most 12 rows name the same one
- route_weights: float32 [4096, 2], P('seq'), may hold values from 0.2 to 1
- w_gate: bfloat16 [8, 4096, 6400], P('exp', None, 'seq'), may hold values from -0.09375 to 0.09375
- w_up: bfloat16 [8, 4096, 6400], P('exp', None, 'seq'), may hold values from -0.09375 to 0.09375
- w_down: bfloat16 [8, 6400, 4096], P('exp', 'seq'), may hold values from -0.078125 to 0.078125
- w_out: bfloat16 [4096, 4096], P(('exp', 'head')), may hold values from -0.09375 to 0.09375
- queries: bfloat16 [4096, 4096], P('seq', ('exp', 'head')), may hold values from -18 to 18
- keys: bfloat16 [4096, 4096], P('seq', ('exp', 'head')), may hold values from -6 to 6
- values: bfloat16 [4096, 4096], P('seq', ('exp', 'head')), may hold values from -6 to 6
Outputs:
- grad_resid: bfloat16 [4096, 4096], P(('seq', 'head'))
- query_grad: bfloat16 [4096, 4096], P('seq', ('exp', 'head'))
Inputs may be any that keep to these rules, and one draw needn't show every extreme that they name: `expert_ids`: each row names two different experts. In each aligned block of 32 rows no expert is named by more than 12 rows, a bound that some block reaches.
All inputs are finite; a program needn't handle non-finite values.
Results may differ from a plain program's by a relative error of at most 0.0085.
Values may be sent and summed in bfloat16 or wider, within the bound.
No kernel may reach another device: no remote copies, remote signals or barrier semaphores. Data moves between devices by JAX's collectives and lax.ppermute only.
A program may use at most 64 MiB of HBM per device.

v0:
```python
import jax
import jax.numpy as jnp
from jax import lax
from jax.sharding import PartitionSpec as P

HD = 128


EPSILON = 1e-05


def norm_back(resid_rows, grad_rows, norm_gain, expert_grad):
    resid_full = resid_rows.astype(jnp.float32)
    inv_rms = lax.rsqrt(jnp.mean(resid_full * resid_full, axis=-1, keepdims=True) + EPSILON)
    scaled_grad = norm_gain.astype(jnp.float32) * expert_grad
    cubed = inv_rms * inv_rms * inv_rms
    mean_term = jnp.mean(scaled_grad * resid_full, axis=-1, keepdims=True)
    return (
        grad_rows.astype(jnp.float32) + inv_rms * scaled_grad - resid_full * cubed * mean_term
    ).astype(jnp.bfloat16)


def per_device(
    resid,
    grad_out,
    norm_gain,
    expert_ids,
    route_weights,
    w_gate,
    w_up,
    w_down,
    w_out,
    queries,
    keys,
    values,
):
    tok_rows = resid.shape[0]
    width = resid.shape[1]
    head_count = lax.axis_size("head")
    exp_count = lax.axis_size("exp")
    quarter = tok_rows // head_count
    local_experts = w_gate.shape[0]
    capacity = 3 * quarter // (local_experts * exp_count)
    seq_index = lax.axis_index("seq")
    exp_index = lax.axis_index("exp")
    head_index = lax.axis_index("head")
    row_first = head_index * quarter
    resid_part = lax.dynamic_slice_in_dim(resid, row_first, quarter, 0)
    grad_part = lax.dynamic_slice_in_dim(grad_out, row_first, quarter, 0)
    ids_part = lax.dynamic_slice_in_dim(expert_ids, row_first, quarter, 0)
    weights_part = lax.dynamic_slice_in_dim(route_weights, row_first, quarter, 0)
    resid_full = resid_part.astype(jnp.float32)
    inv_rms = lax.rsqrt(jnp.mean(resid_full * resid_full, axis=-1, keepdims=True) + EPSILON)
    normed = (resid_full * inv_rms * norm_gain.astype(jnp.float32)).astype(jnp.bfloat16)
    grad_full = grad_part.astype(jnp.float32)
    slot_ids = lax.broadcasted_iota(jnp.int32, (capacity, quarter), 0)
    contract = (((1,), (1,)), ((), ()))
    expert = exp_index * local_experts + 0
    matched = ids_part == expert
    routed = jnp.any(matched, axis=1)
    weight = jnp.sum(jnp.where(matched, weights_part, 0.0), axis=1)
    position = jnp.cumsum(routed.astype(jnp.int32)) - 1
    select = (position[None, :] == slot_ids) & routed[None, :]
    select_mat = select.astype(jnp.bfloat16)
    slot_in = jnp.dot(select_mat, normed, preferred_element_type=jnp.float32).astype(jnp.bfloat16)
    scaled = (weight[:, None] * grad_full).astype(jnp.bfloat16)
    slot_grad = jnp.dot(select_mat, scaled, preferred_element_type=jnp.float32).astype(jnp.bfloat16)
    gate_mat = w_gate[0]
    up_mat = w_up[0]
    down_mat = w_down[0]
    rows_in = lax.all_gather(slot_in, "seq", axis=0, tiled=True)
    rows_grad = lax.all_gather(slot_grad, "seq", axis=0, tiled=True)
    gate_val = jnp.dot(rows_in, gate_mat, preferred_element_type=jnp.float32)
    up_val = jnp.dot(rows_in, up_mat, preferred_element_type=jnp.float32)
    hidden_grad = lax.dot_general(rows_grad, down_mat, contract, preferred_element_type=jnp.float32)
    sigma = jax.nn.sigmoid(gate_val)
    gate_grad = (hidden_grad * up_val * sigma * (1.0 + gate_val * (1.0 - sigma))).astype(
        jnp.bfloat16
    )
    up_grad = (hidden_grad * gate_val * sigma).astype(jnp.bfloat16)
    all_slots = lax.dot_general(gate_grad, gate_mat, contract, preferred_element_type=jnp.float32)
    all_slots = all_slots + lax.dot_general(
        up_grad, up_mat, contract, preferred_element_type=jnp.float32
    )
    slots_back = lax.psum_scatter(all_slots, "seq", scatter_dimension=0, tiled=True)
    local_sum = jnp.dot(select.astype(jnp.float32).T, slots_back, precision=lax.Precision.HIGHEST)
    share = quarter // exp_count
    summed = lax.psum_scatter(local_sum, "exp", scatter_dimension=0, tiled=True)
    share_first = exp_index * share
    resid_share = lax.dynamic_slice_in_dim(resid_part, share_first, share, 0)
    grad_share_in = lax.dynamic_slice_in_dim(grad_part, share_first, share, 0)
    grad_share = norm_back(resid_share, grad_share_in, norm_gain, summed)
    gathered = lax.all_gather(grad_share, ("exp", "head"), axis=0, tiled=True)
    full_grad = (
        gathered.reshape(exp_count, head_count, share, width)
        .transpose(1, 0, 2, 3)
        .reshape(tok_rows, width)
    )
    grad_quarter = lax.dynamic_slice_in_dim(full_grad, row_first, quarter, 0)
    heads_here = queries.shape[1] // HD
    attn_grad = lax.dot_general(
        full_grad, w_out, contract, preferred_element_type=jnp.float32
    ).astype(jnp.bfloat16)
    query_three = queries.reshape(tok_rows, heads_here, HD)
    attn_three = attn_grad.reshape(tok_rows, heads_here, HD)
    query_pos = seq_index * tok_rows + jnp.arange(tok_rows, dtype=jnp.int32)
    scale = HD ** (-0.5)
    highest = lax.Precision.HIGHEST
    start_max = jnp.full((heads_here, tok_rows), -1e30, jnp.float32)
    run_max = start_max
    key_piece = lax.all_gather(keys, "seq", axis=0, tiled=True)
    value_piece = lax.all_gather(values, "seq", axis=0, tiled=True)
    key_count = key_piece.shape[0]
    key_three = key_piece.reshape(key_count, heads_here, HD)
    value_three = value_piece.reshape(key_count, heads_here, HD)
    scores = (
        jnp.einsum("qhd,khd->hqk", query_three, key_three, preferred_element_type=jnp.float32)
        * scale
    )
    key_pos = jnp.arange(key_count, dtype=jnp.int32)
    allowed = (key_pos[None, :] <= query_pos[:, None])[None, :, :]
    scores = jnp.where(allowed, scores, -1e30)
    new_max = jnp.maximum(run_max, jnp.max(scores, axis=-1))
    expo_vals = jnp.where(allowed, jnp.exp(scores - new_max[:, :, None]), 0.0)
    prob_grad = jnp.einsum(
        "qhd,khd->hqk", attn_three, value_three, preferred_element_type=jnp.float32
    )
    key_full = key_three.astype(jnp.float32)
    value_full = value_three.astype(jnp.float32)
    run_sum = jnp.sum(expo_vals, axis=-1)
    acc_val = jnp.einsum("hqk,khd->hqd", expo_vals, value_full, precision=highest)
    acc_mix = jnp.einsum("hqk,khd->hqd", expo_vals * prob_grad, key_full, precision=highest)
    acc_key = jnp.einsum("hqk,khd->hqd", expo_vals, key_full, precision=highest)
    run_max, run_sum, acc_val, acc_mix, acc_key = (new_max, run_sum, acc_val, acc_mix, acc_key)
    output = acc_val / run_sum[:, :, None]
    attn_heads = attn_three.astype(jnp.float32).transpose(1, 0, 2)
    delta = jnp.sum(attn_heads * output, axis=-1, keepdims=True)
    query_heads = scale * (acc_mix - delta * acc_key) / run_sum[:, :, None]
    query_grad = (
        query_heads.transpose(1, 0, 2).reshape(tok_rows, heads_here * HD).astype(jnp.bfloat16)
    )
    return (grad_quarter, query_grad)


def solution(mesh):
    in_specs = (
        P("seq", None),
        P("seq", None),
        P(),
        P("seq", None),
        P("seq", None),
        P("exp", None, "seq"),
        P("exp", None, "seq"),
        P("exp", "seq", None),
        P(("exp", "head"), None),
        P("seq", ("exp", "head")),
        P("seq", ("exp", "head")),
        P("seq", ("exp", "head")),
    )
    out_specs = (P(("seq", "head"), None), P("seq", ("exp", "head")))
    return jax.shard_map(
        per_device, mesh=mesh, in_specs=in_specs, out_specs=out_specs, check_vma=False
    )
```

profile of v0, /device:TPU:1, one launch (start us, length us, event | category | flops | bytes accessed | tf_op | source)
XLA Modules:
  0.0 739.4 jit_solution(4306651578538725658)
XLA Ops:
  7.2 0.9 fusion.73
  8.4 0.8 fusion.70
  9.2 1.8 fusion.2
  11.1 0.7 convert_element_type.68
  11.8 1.1 fusion.33
  12.9 1.9 fusion.3
  14.8 83.4 %all-gather.13.cloned.1.call-done = bf16[32,12,4096]{2,1,0:T(8,128)(2,1)} async-done(((bf16[1,12,4096]{2,1,0:T(8,128)(2,1)}), bf16[32,12,4096]{2,1,0:T(8,128)(2,1)}) %all-gather.13.cloned.1.call-update) | async-done | bytes 3145744 | tf_op jit(solution)/shard_map/all_gather | solution.py:72
  98.3 5.6 reshape.143
  103.8 3.6 fusion.11
  107.4 67.6 %all-gather.15.cloned.1.call-done = bf16[32,12,4096]{2,1,0:T(8,128)(2,1)} async-done(((bf16[1,12,4096]{2,1,0:T(8,128)(2,1)}), bf16[32,12,4096]{2,1,0:T(8,128)(2,1)}) %all-gather.15.cloned.1.call-update) | async-done | bytes 3145744 | tf_op jit(solution)/shard_map/all_gather | solution.py:71
  175.0 5.6 reshape.145
  180.6 3.6 fusion.6
  184.2 7.5 %fusion.4 = f32[384,4096]{1,0:T(8,128)} fusion(bf16[1,4096,200]{1,2,0:T(8,128)(2,1)} %param.17, f32[384,200]{0,1:T(8,128)S(1)} %fusion.11, bf16[384,4096]{1,0:T(8,128)(2,1)} %reshape.145, bf16[1,4096,200]{1,2,0:T(8,128)(2,1)S(1)} %copy-done, f32[384,200]{0,1:T(8,128)S(1)} %fusion.6), kind=kOutput, calls=%fused_computation.10 | convolution fusion | flops 1259059200 | bytes 13328384 | tf_op jit(solution)/shard_map/dot_general | solution.py:81
  191.7 6.5 convolution_add_fusion
  198.2 60.2 %fusion = f32[16,4096]{1,0:T(8,128)S(1)} fusion(f32[384,4096]{1,0:T(8,128)} %convolution_add_fusion), kind=kCustom, calls=%all-reduce-scatter | all-reduce-scatter fusion | flops 2097153 | bytes 6557696
  258.4 2.2 collective-permute-start
  260.6 1.3 collective-permute-start.1
  261.9 4.7 collective-permute-start.7
  266.7 5.4 collective-permute-start.2
  272.1 4.5 collective-permute-start.3
  276.7 26.6 %collective-permute-start.4 = (f32[16,4096]{1,0:T(8,128)S(1)}, f32[16,4096]{1,0:T(8,128)S(1)}, u32[]{:S(2)}, u32[]{:S(2)}) collective-permute-start(f32[16,4096]{1,0:T(8,128)S(1)} %fusion), channel_id=1, source_target_pairs={{0,160},{32,192},{64,224},{96,256},{128,288},{160,320},{192,352},{... | collective-permute-start | bytes 786440
  303.2 2.8 collective-permute-start.5
  306.0 8.1 %collective-permute-start.6 = (f32[16,4096]{1,0:T(8,128)S(1)}, f32[16,4096]{1,0:T(8,128)}, u32[]{:S(2)}, u32[]{:S(2)}) collective-permute-start(f32[16,4096]{1,0:T(8,128)S(1)} %fusion), channel_id=1, source_target_pairs={{0,224},{32,256},{64,288},{96,320},{128,352},{160,384},{192,416},{... | collective-permute-start | bytes 786440
  314.2 1.3 dynamic-slice.6
  316.1 1.6 collective-permute-done.6
  317.8 22.0 %concatenate = f32[140,4096]{1,0:T(8,128)} concatenate(f32[12,4096]{1,0:T(8,128)S(1)} %collective-permute-done.7, f32[16,4096]{1,0:T(8,128)} %collective-permute-done.6, f32[16,4096]{1,0:T(8,128)} %collective-permute-done.5, f32[16,4096]{1,0:T(8,128)S(1)} %collective-permute-done.4, f32[16,4096]{1,0:T(8,128)S(1)} %collective-permute-done.3, ...), dimensions={0} | concatenate | bytes 4587520
  339.8 2.2 fusion.40
  342.1 0.5 all-gather.9.cloned.1.call-update
  342.7 1.3 dynamic-slice.2
  344.6 127.7 %all-reduce.5.cloned.1.call-done = f32[32,4096]{1,0:T(8,128)} async-done(((f32[32,4096]{1,0:T(8,128)}), f32[32,4096]{1,0:T(8,128)}) %all-reduce.5.cloned.1.call-update) | async-done | bytes 524304
  472.3 1.2 fusion.49
  473.5 1.8 fusion.54
  475.5 0.3 all-gather.11.cloned.1.call-update
  475.9 78.0 %all-gather.9.cloned.1.call-done = bf16[4096,128]{1,0:T(8,128)(2,1)} async-done(((bf16[128,128]{1,0:T(8,128)(2,1)}), bf16[4096,128]{1,0:T(8,128)(2,1)}) %all-gather.9.cloned.1.call-update) | async-done | bytes 1048592 | tf_op jit(solution)/shard_map/all_gather | solution.py:111
  553.9 1.8 fusion.75
  555.7 1.3 copy-done.1
  557.1 0.6 fusion.74
  557.7 85.8 %all-gather.17.cloned.1.call-done = bf16[32,4,4096]{2,1,0:T(4,128)(2,1)} async-done(((bf16[1,4,4096]{2,1,0:T(4,128)(2,1)}), bf16[32,4,4096]{2,1,0:T(4,128)(2,1)}) %all-gather.17.cloned.1.call-update) | async-done | bytes 1048592 | tf_op jit(solution)/shard_map/all_gather | solution.py:93
  643.5 2.9 copy.25
  646.4 1.3 reshape.140
  647.7 1.7 convolution_convert_fusion.2
  649.4 0.7 constant_dynamic-slice_fusion
  650.1 73.8 %all-gather.11.cloned.1.call-done = bf16[4096,128]{1,0:T(8,128)(2,1)} async-done(((bf16[128,128]{1,0:T(8,128)(2,1)}), bf16[4096,128]{1,0:T(8,128)(2,1)}) %all-gather.11.cloned.1.call-update) | async-done | bytes 1048592 | tf_op jit(solution)/shard_map/all_gather | solution.py:112
  723.9 2.8 convolution_multiply_fusion
  726.7 1.8 fusion.32
  728.6 1.4 fusion.76
  730.0 1.8 fusion.31
  731.8 0.7 copy.28
  (37 shorter events, 0.9 us)
Async XLA Ops:
  7.2 177.0 %copy-start = (bf16[1,4096,200]{1,2,0:T(8,128)(2,1)S(1)}, bf16[1,4096,200]{1,2,0:T(8,128)(2,1)}, u32[]{:S(2)}) copy-start(bf16[1,4096,200]{1,2,0:T(8,128)(2,1)} %param.18) | copy-start | bytes 4915204
  7.2 91.1 %all-gather.13.cloned.1.call-start = ((), (), s32[]{:S(2)}) async-start(), calls=%async_computation.2 | async-start | bytes 4325376 | tf_op jit(solution)/shard_map/all_gather | solution.py:72
  11.0 164.0 %all-gather.15.cloned.1.call-start = ((), (), s32[]{:S(2)}) async-start(), calls=%async_computation.3 | async-start | bytes 4325376 | tf_op jit(solution)/shard_map/all_gather | solution.py:71
  14.8 457.5 %all-reduce.5.cloned.1.call-start = ((), (), s32[]{:S(2)}) async-start(), calls=%async_computation.5 | async-start | bytes 1048576
  258.4 44.8 %collective-permute-start = (f32[16,4096]{1,0:T(8,128)S(1)}, f32[16,4096]{1,0:T(8,128)S(1)}, u32[]{:S(2)}, u32[]{:S(2)}) collective-permute-start(f32[16,4096]{1,0:T(8,128)S(1)} %fusion), channel_id=1, source_target_pairs={{0,32},{32,64},{64,96},{96,128},{128,160},{160,192},{192,224},{224... | collective-permute-start | bytes 786440
  260.6 45.5 %collective-permute-start.1 = (f32[16,4096]{1,0:T(8,128)S(1)}, f32[16,4096]{1,0:T(8,128)S(1)}, u32[]{:S(2)}, u32[]{:S(2)}) collective-permute-start(f32[16,4096]{1,0:T(8,128)S(1)} %fusion), channel_id=1, source_target_pairs={{0,64},{32,96},{64,128},{96,160},{128,192},{160,224},{192,256},{22... | collective-permute-start | bytes 786440
  261.9 14.7 %collective-permute-start.7 = (f32[12,4096]{1,0:T(8,128)S(1)}, f32[12,4096]{1,0:T(8,128)S(1)}, u32[]{:S(2)}, u32[]{:S(2)}) collective-permute-start(f32[12,4096]{1,0:T(8,128)S(1)} %slice), channel_id=1, source_target_pairs={{0,256},{32,288},{64,320},{96,352},{128,384},{160,416},{192,448},{... | collective-permute-start | bytes 589832
  266.7 49.4 %collective-permute-start.2 = (f32[16,4096]{1,0:T(8,128)S(1)}, f32[16,4096]{1,0:T(8,128)S(1)}, u32[]{:S(2)}, u32[]{:S(2)}) collective-permute-start(f32[16,4096]{1,0:T(8,128)S(1)} %fusion), channel_id=1, source_target_pairs={{0,96},{32,128},{64,160},{96,192},{128,224},{160,256},{192,288},{2... | collective-permute-start | bytes 786440
  272.1 44.0 %collective-permute-start.3 = (f32[16,4096]{1,0:T(8,128)S(1)}, f32[16,4096]{1,0:T(8,128)S(1)}, u32[]{:S(2)}, u32[]{:S(2)}) collective-permute-start(f32[16,4096]{1,0:T(8,128)S(1)} %fusion), channel_id=1, source_target_pairs={{0,128},{32,160},{64,192},{96,224},{128,256},{160,288},{192,320},{... | collective-permute-start | bytes 786440
  276.7 39.5 %collective-permute-start.4 = (f32[16,4096]{1,0:T(8,128)S(1)}, f32[16,4096]{1,0:T(8,128)S(1)}, u32[]{:S(2)}, u32[]{:S(2)}) collective-permute-start(f32[16,4096]{1,0:T(8,128)S(1)} %fusion), channel_id=1, source_target_pairs={{0,160},{32,192},{64,224},{96,256},{128,288},{160,320},{192,352},{... | collective-permute-start | bytes 786440
  303.2 12.9 %collective-permute-start.5 = (f32[16,4096]{1,0:T(8,128)S(1)}, f32[16,4096]{1,0:T(8,128)}, u32[]{:S(2)}, u32[]{:S(2)}) collective-permute-start(f32[16,4096]{1,0:T(8,128)S(1)} %fusion), channel_id=1, source_target_pairs={{0,192},{32,224},{64,256},{96,288},{128,320},{160,352},{192,384},{... | collective-permute-start | bytes 786440
  306.0 11.7 %collective-permute-start.6 = (f32[16,4096]{1,0:T(8,128)S(1)}, f32[16,4096]{1,0:T(8,128)}, u32[]{:S(2)}, u32[]{:S(2)}) collective-permute-start(f32[16,4096]{1,0:T(8,128)S(1)} %fusion), channel_id=1, source_target_pairs={{0,224},{32,256},{64,288},{96,320},{128,352},{160,384},{192,416},{... | collective-permute-start | bytes 786440
  316.1 237.8 %copy-start.5 = (bf16[128,128]{1,0:T(8,128)(2,1)S(1)}, bf16[128,128]{1,0:T(8,128)(2,1)}, u32[]{:S(2)}) copy-start(bf16[128,128]{1,0:T(8,128)(2,1)} %param.21) | copy-start | bytes 98308
  342.1 211.8 %all-gather.9.cloned.1.call-start = ((), (), s32[]{:S(2)}) async-start(), calls=%async_computation | async-start | bytes 1081344 | tf_op jit(solution)/shard_map/all_gather | solution.py:111
  342.6 300.9 %all-gather.17.cloned.1.call-start = ((), (), s32[]{:S(2)}) async-start(), calls=%async_computation.4 | async-start | bytes 1081344 | tf_op jit(solution)/shard_map/all_gather | solution.py:93
  475.3 248.6 %all-gather.11.cloned.1.call-start = ((), (), s32[]{:S(2)}) async-start(), calls=%async_computation.1 | async-start | bytes 1081344 | tf_op jit(solution)/shard_map/all_gather | solution.py:112
  555.7 1.4 copy-start.1
  723.9 2.8 copy-start.2
  723.9 2.8 copy-start.4
  726.7 1.8 copy-start.3
Sparse Core Ops, SparseCore 0:
  11.3 86.9 all-gather.12
  101.0 74.0 all-gather.14
  342.2 130.1 all-reduce.4
  475.3 78.6 all-gather.8
  559.4 84.0 all-gather.16
  646.4 77.4 all-gather.10
where the time goes:
time: 741 us; the launch traced here: 739 us
  waiting for transfers between devices  519 us (70%)
  blocking collectives  60.2 us (8%)
  starting transfers between devices  56.1 us (8%)
  local copies, waits for them, and re-layouts  42.9 us (6%)
  matrix products  38.3 us (5%)
  between operations  15.7 us (2%)
    unnamed x15, waiting for transfers between devices  130 us
    all_gather x1, waiting for transfers between devices, per_device(): gathered = lax.all_gather(grad_share, ('exp', 'head'), axis=0, tiled=True)  85.8 us
    all_gather x1, waiting for transfers between devices, per_device(): rows_grad = lax.all_gather(slot_grad, 'seq', axis=0, tiled=True)  83.4 us
    all_gather x1, waiting for transfers between devices, per_device(): key_piece = lax.all_gather(keys, 'seq', axis=0, tiled=True)  78 us
    all_gather x1, waiting for transfers between devices, per_device(): value_piece = lax.all_gather(values, 'seq', axis=0, tiled=True)  73.8 us
    all_gather x1, waiting for transfers between devices, per_device(): rows_in = lax.all_gather(slot_in, 'seq', axis=0, tiled=True)  67.6 us
    unnamed x1, blocking collectives  60.2 us
    unnamed x9, starting transfers between devices  55.7 us
  transfers between devices with their start and end apart: 14, of which 7 were waited for; matrix products, arithmetic and copies ran while one was open for 4% of the time, Pallas kernels for 0%

commit v1 on v0

--- a/solution.py
+++ b/solution.py
@@ -59,7 +59,9 @@
     matched = ids_part == expert
     routed = jnp.any(matched, axis=1)
     weight = jnp.sum(jnp.where(matched, weights_part, 0.0), axis=1)
-    position = jnp.cumsum(routed.astype(jnp.int32)) - 1
+    row_ids = jnp.arange(quarter, dtype=jnp.int32)
+    earlier = row_ids[:, None] < row_ids[None, :]
+    position = jnp.sum((earlier & routed[:, None]).astype(jnp.int32), axis=0)
     select = (position[None, :] == slot_ids) & routed[None, :]
     select_mat = select.astype(jnp.bfloat16)
     slot_in = jnp.dot(select_mat, normed, preferred_element_type=jnp.float32).astype(jnp.bfloat16)

time: 741 us -> 741 us (level)
  no operation moved by 1% of the time
where the time goes in v1:
time: 741 us; the launch traced here: 739 us
  waiting for transfers between devices  519 us (70%)
  blocking collectives  60.2 us (8%)
  starting transfers between devices  56.1 us (8%)
  local copies, waits for them, and re-layouts  42.7 us (6%)
  matrix products  38.3 us (5%)
  between operations  15.7 us (2%)
    unnamed x15, waiting for transfers between devices  130 us
    all_gather x1, waiting for transfers between devices, per_device(): gathered = lax.all_gather(grad_share, ('exp', 'head'), axis=0, tiled=True)  85.8 us
    all_gather x1, waiting for transfers between devices, per_device(): rows_grad = lax.all_gather(slot_grad, 'seq', axis=0, tiled=True)  83.6 us
    all_gather x1, waiting for transfers between devices, per_device(): key_piece = lax.all_gather(keys, 'seq', axis=0, tiled=True)  78 us
    all_gather x1, waiting for transfers between devices, per_device(): value_piece = lax.all_gather(values, 'seq', axis=0, tiled=True)  73.8 us
    all_gather x1, waiting for transfers between devices, per_device(): rows_in = lax.all_gather(slot_in, 'seq', axis=0, tiled=True)  67.6 us
    unnamed x1, blocking collectives  60.2 us
    unnamed x9, starting transfers between devices  55.7 us
  transfers between devices with their start and end apart: 14, of which 7 were waited for; matrix products, arithmetic and copies ran while one was open for 4% of the time, Pallas kernels for 0%

profile of v1, /device:TPU:1, one launch (start us, length us, event | category | flops | bytes accessed | tf_op | source)
XLA Modules:
  0.0 739.3 jit_solution(8778688209886295671)
XLA Ops:
  7.2 0.9 fusion.74
  8.2 0.8 fusion.71
  9.0 1.8 fusion.2
  10.9 0.7 convert_element_type.56
  11.6 1.1 fusion.33
  12.7 1.9 fusion.3
  14.7 83.6 %all-gather.13.cloned.1.call-done = bf16[32,12,4096]{2,1,0:T(8,128)(2,1)} async-done(((bf16[1,12,4096]{2,1,0:T(8,128)(2,1)}), bf16[32,12,4096]{2,1,0:T(8,128)(2,1)}) %all-gather.13.cloned.1.call-update) | async-done | bytes 3145744 | tf_op jit(solution)/shard_map/all_gather | solution.py:74
  98.3 5.6 reshape.112
  103.8 3.6 fusion.11
  107.4 67.6 %all-gather.15.cloned.1.call-done = bf16[32,12,4096]{2,1,0:T(8,128)(2,1)} async-done(((bf16[1,12,4096]{2,1,0:T(8,128)(2,1)}), bf16[32,12,4096]{2,1,0:T(8,128)(2,1)}) %all-gather.15.cloned.1.call-update) | async-done | bytes 3145744 | tf_op jit(solution)/shard_map/all_gather | solution.py:73
  175.0 5.6 reshape.114
  180.6 3.6 fusion.6
  184.2 7.5 %fusion.4 = f32[384,4096]{1,0:T(8,128)} fusion(bf16[1,4096,200]{1,2,0:T(8,128)(2,1)} %param.17, f32[384,200]{0,1:T(8,128)S(1)} %fusion.11, bf16[384,4096]{1,0:T(8,128)(2,1)} %reshape.114, bf16[1,4096,200]{1,2,0:T(8,128)(2,1)S(1)} %copy-done, f32[384,200]{0,1:T(8,128)S(1)} %fusion.6), kind=kOutput, calls=%fused_computation.10 | convolution fusion | flops 1259059200 | bytes 13328384 | tf_op jit(solution)/shard_map/dot_general | solution.py:83
  191.6 6.5 convolution_add_fusion
  198.1 60.2 %fusion = f32[16,4096]{1,0:T(8,128)S(1)} fusion(f32[384,4096]{1,0:T(8,128)} %convolution_add_fusion), kind=kCustom, calls=%all-reduce-scatter | all-reduce-scatter fusion | flops 2097153 | bytes 6557696
  258.3 2.2 collective-permute-start
  260.5 1.3 collective-permute-start.1
  261.9 4.7 collective-permute-start.7
  266.6 5.4 collective-permute-start.2
  272.0 4.5 collective-permute-start.3
  276.6 26.5 %collective-permute-start.4 = (f32[16,4096]{1,0:T(8,128)S(1)}, f32[16,4096]{1,0:T(8,128)S(1)}, u32[]{:S(2)}, u32[]{:S(2)}) collective-permute-start(f32[16,4096]{1,0:T(8,128)S(1)} %fusion), channel_id=1, source_target_pairs={{0,160},{32,192},{64,224},{96,256},{128,288},{160,320},{192,352},{... | collective-permute-start | bytes 786440
  303.1 2.8 collective-permute-start.5
  305.9 8.1 %collective-permute-start.6 = (f32[16,4096]{1,0:T(8,128)S(1)}, f32[16,4096]{1,0:T(8,128)}, u32[]{:S(2)}, u32[]{:S(2)}) collective-permute-start(f32[16,4096]{1,0:T(8,128)S(1)} %fusion), channel_id=1, source_target_pairs={{0,224},{32,256},{64,288},{96,320},{128,352},{160,384},{192,416},{... | collective-permute-start | bytes 786440
  314.1 1.3 dynamic-slice.6
  316.0 1.6 collective-permute-done.6
  317.7 22.0 %concatenate = f32[140,4096]{1,0:T(8,128)} concatenate(f32[12,4096]{1,0:T(8,128)S(1)} %collective-permute-done.7, f32[16,4096]{1,0:T(8,128)} %collective-permute-done.6, f32[16,4096]{1,0:T(8,128)} %collective-permute-done.5, f32[16,4096]{1,0:T(8,128)S(1)} %collective-permute-done.4, f32[16,4096]{1,0:T(8,128)S(1)} %collective-permute-done.3, ...), dimensions={0} | concatenate | bytes 4587520
  339.7 2.2 fusion.40
  342.0 0.5 all-gather.9.cloned.1.call-update
  342.6 1.3 dynamic-slice.2
  344.5 127.7 %all-reduce.5.cloned.1.call-done = f32[32,4096]{1,0:T(8,128)} async-done(((f32[32,4096]{1,0:T(8,128)}), f32[32,4096]{1,0:T(8,128)}) %all-reduce.5.cloned.1.call-update) | async-done | bytes 524304
  472.2 1.2 fusion.49
  473.4 1.8 fusion.54
  475.4 0.3 all-gather.11.cloned.1.call-update
  475.8 78.0 %all-gather.9.cloned.1.call-done = bf16[4096,128]{1,0:T(8,128)(2,1)} async-done(((bf16[128,128]{1,0:T(8,128)(2,1)}), bf16[4096,128]{1,0:T(8,128)(2,1)}) %all-gather.9.cloned.1.call-update) | async-done | bytes 1048592 | tf_op jit(solution)/shard_map/all_gather | solution.py:113
  553.8 1.8 fusion.76
  555.6 1.3 copy-done.1
  557.0 0.6 fusion.75
  557.6 85.8 %all-gather.17.cloned.1.call-done = bf16[32,4,4096]{2,1,0:T(4,128)(2,1)} async-done(((bf16[1,4,4096]{2,1,0:T(4,128)(2,1)}), bf16[32,4,4096]{2,1,0:T(4,128)(2,1)}) %all-gather.17.cloned.1.call-update) | async-done | bytes 1048592 | tf_op jit(solution)/shard_map/all_gather | solution.py:95
  643.4 2.9 copy.26
  646.2 1.3 reshape.110
  647.6 1.7 convolution_convert_fusion.2
  649.3 0.7 constant_dynamic-slice_fusion
  650.0 73.8 %all-gather.11.cloned.1.call-done = bf16[4096,128]{1,0:T(8,128)(2,1)} async-done(((bf16[128,128]{1,0:T(8,128)(2,1)}), bf16[4096,128]{1,0:T(8,128)(2,1)}) %all-gather.11.cloned.1.call-update) | async-done | bytes 1048592 | tf_op jit(solution)/shard_map/all_gather | solution.py:114
  723.8 2.8 convolution_multiply_fusion
  726.6 1.8 fusion.32
  728.5 1.4 fusion.77
  729.9 1.8 fusion.31
  731.7 0.7 copy.29
  (34 shorter events, 0.7 us)
Async XLA Ops:
  7.2 177.0 %copy-start = (bf16[1,4096,200]{1,2,0:T(8,128)(2,1)S(1)}, bf16[1,4096,200]{1,2,0:T(8,128)(2,1)}, u32[]{:S(2)}) copy-start(bf16[1,4096,200]{1,2,0:T(8,128)(2,1)} %param.18) | copy-start | bytes 4915204
  7.2 91.1 %all-gather.13.cloned.1.call-start = ((), (), s32[]{:S(2)}) async-start(), calls=%async_computation.2 | async-start | bytes 4325376 | tf_op jit(solution)/shard_map/all_gather | solution.py:74
  10.9 164.2 %all-gather.15.cloned.1.call-start = ((), (), s32[]{:S(2)}) async-start(), calls=%async_computation.3 | async-start | bytes 4325376 | tf_op jit(solution)/shard_map/all_gather | solution.py:73
  14.6 457.6 %all-reduce.5.cloned.1.call-start = ((), (), s32[]{:S(2)}) async-start(), calls=%async_computation.5 | async-start | bytes 1048576
  258.3 44.8 %collective-permute-start = (f32[16,4096]{1,0:T(8,128)S(1)}, f32[16,4096]{1,0:T(8,128)S(1)}, u32[]{:S(2)}, u32[]{:S(2)}) collective-permute-start(f32[16,4096]{1,0:T(8,128)S(1)} %fusion), channel_id=1, source_target_pairs={{0,32},{32,64},{64,96},{96,128},{128,160},{160,192},{192,224},{224... | collective-permute-start | bytes 786440
  260.5 45.4 %collective-permute-start.1 = (f32[16,4096]{1,0:T(8,128)S(1)}, f32[16,4096]{1,0:T(8,128)S(1)}, u32[]{:S(2)}, u32[]{:S(2)}) collective-permute-start(f32[16,4096]{1,0:T(8,128)S(1)} %fusion), channel_id=1, source_target_pairs={{0,64},{32,96},{64,128},{96,160},{128,192},{160,224},{192,256},{22... | collective-permute-start | bytes 786440
  261.9 14.7 %collective-permute-start.7 = (f32[12,4096]{1,0:T(8,128)S(1)}, f32[12,4096]{1,0:T(8,128)S(1)}, u32[]{:S(2)}, u32[]{:S(2)}) collective-permute-start(f32[12,4096]{1,0:T(8,128)S(1)} %slice), channel_id=1, source_target_pairs={{0,256},{32,288},{64,320},{96,352},{128,384},{160,416},{192,448},{... | collective-permute-start | bytes 589832
  266.6 49.4 %collective-permute-start.2 = (f32[16,4096]{1,0:T(8,128)S(1)}, f32[16,4096]{1,0:T(8,128)S(1)}, u32[]{:S(2)}, u32[]{:S(2)}) collective-permute-start(f32[16,4096]{1,0:T(8,128)S(1)} %fusion), channel_id=1, source_target_pairs={{0,96},{32,128},{64,160},{96,192},{128,224},{160,256},{192,288},{2... | collective-permute-start | bytes 786440
  272.0 44.0 %collective-permute-start.3 = (f32[16,4096]{1,0:T(8,128)S(1)}, f32[16,4096]{1,0:T(8,128)S(1)}, u32[]{:S(2)}, u32[]{:S(2)}) collective-permute-start(f32[16,4096]{1,0:T(8,128)S(1)} %fusion), channel_id=1, source_target_pairs={{0,128},{32,160},{64,192},{96,224},{128,256},{160,288},{192,320},{... | collective-permute-start | bytes 786440
  276.6 39.5 %collective-permute-start.4 = (f32[16,4096]{1,0:T(8,128)S(1)}, f32[16,4096]{1,0:T(8,128)S(1)}, u32[]{:S(2)}, u32[]{:S(2)}) collective-permute-start(f32[16,4096]{1,0:T(8,128)S(1)} %fusion), channel_id=1, source_target_pairs={{0,160},{32,192},{64,224},{96,256},{128,288},{160,320},{192,352},{... | collective-permute-start | bytes 786440
  303.1 12.9 %collective-permute-start.5 = (f32[16,4096]{1,0:T(8,128)S(1)}, f32[16,4096]{1,0:T(8,128)}, u32[]{:S(2)}, u32[]{:S(2)}) collective-permute-start(f32[16,4096]{1,0:T(8,128)S(1)} %fusion), channel_id=1, source_target_pairs={{0,192},{32,224},{64,256},{96,288},{128,320},{160,352},{192,384},{... | collective-permute-start | bytes 786440
  305.9 11.7 %collective-permute-start.6 = (f32[16,4096]{1,0:T(8,128)S(1)}, f32[16,4096]{1,0:T(8,128)}, u32[]{:S(2)}, u32[]{:S(2)}) collective-permute-start(f32[16,4096]{1,0:T(8,128)S(1)} %fusion), channel_id=1, source_target_pairs={{0,224},{32,256},{64,288},{96,320},{128,352},{160,384},{192,416},{... | collective-permute-start | bytes 786440
  316.0 237.8 %copy-start.5 = (bf16[128,128]{1,0:T(8,128)(2,1)S(1)}, bf16[128,128]{1,0:T(8,128)(2,1)}, u32[]{:S(2)}) copy-start(bf16[128,128]{1,0:T(8,128)(2,1)} %param.21) | copy-start | bytes 98308
  341.9 211.9 %all-gather.9.cloned.1.call-start = ((), (), s32[]{:S(2)}) async-start(), calls=%async_computation | async-start | bytes 1081344 | tf_op jit(solution)/shard_map/all_gather | solution.py:113
  342.5 300.9 %all-gather.17.cloned.1.call-start = ((), (), s32[]{:S(2)}) async-start(), calls=%async_computation.4 | async-start | bytes 1081344 | tf_op jit(solution)/shard_map/all_gather | solution.py:95
  475.2 248.6 %all-gather.11.cloned.1.call-start = ((), (), s32[]{:S(2)}) async-start(), calls=%async_computation.1 | async-start | bytes 1081344 | tf_op jit(solution)/shard_map/all_gather | solution.py:114
  555.6 1.3 copy-start.1
  723.8 2.8 copy-start.2
  723.8 2.8 copy-start.4
  726.6 1.8 copy-start.3
Sparse Core Ops, SparseCore 0:
  11.3 86.9 all-gather.12
  101.0 74.0 all-gather.14
  342.1 130.1 all-reduce.4
  475.1 78.6 all-gather.8
  559.3 84.0 all-gather.16
  646.3 77.4 all-gather.10

commit v2 on v1

v2 whole, which is shorter than its diff:
```python
import jax
import jax.numpy as jnp
from jax import lax
from jax.sharding import Mesh, PartitionSpec as P

HD = 128
EPSILON = 1e-05
CAP = 12
FOLD = 4

CONTRACT = (((1,), (1,)), ((), ()))


def spread(rows, axis, size, dist):
    up = [(a, (a + dist) % size) for a in range(size)]
    down = [(a, (a - dist) % size) for a in range(size)]
    if axis == "z":
        pairs = [(2 * a, 2 * b) for a, b in up] + [(2 * a + 1, 2 * b + 1) for a, b in down]
        return lax.ppermute(rows, ("z", "core"), pairs)
    pairs = up + [(size + a, size + b) for a, b in down]
    return lax.ppermute(rows, ("core", axis), pairs)


def core_swap(block):
    return lax.ppermute(block, "core", [(0, 1), (1, 0)])


def norm_back(resid_full, inv_rms, grad_rows, norm_gain, expert_grad):
    scaled_grad = norm_gain.astype(jnp.float32) * expert_grad
    cubed = inv_rms * inv_rms * inv_rms
    mean_term = jnp.mean(scaled_grad * resid_full, axis=-1, keepdims=True)
    return (grad_rows + inv_rms * scaled_grad - resid_full * cubed * mean_term).astype(jnp.bfloat16)


def per_device(
    resid,
    grad_out,
    norm_gain,
    expert_ids,
    route_weights,
    w_gate,
    w_up,
    w_down,
    w_out,
    queries,
    keys,
    values,
):
    f32, bf16 = jnp.float32, jnp.bfloat16
    tok_rows, width = resid.shape
    z_count, exp_count, head_count = (lax.axis_size(a) for a in ("z", "exp", "head"))
    z_index, core_index = lax.axis_index("z"), lax.axis_index("core")
    exp_index, head_index = lax.axis_index("exp"), lax.axis_index("head")
    quarter = tok_rows // head_count
    row_first = head_index * quarter
    resid_part = lax.dynamic_slice_in_dim(resid, row_first, quarter, 0)
    grad_part = lax.dynamic_slice_in_dim(grad_out, row_first, quarter, 0)
    ids_part = lax.dynamic_slice_in_dim(expert_ids, row_first, quarter, 0)
    weights_part = lax.dynamic_slice_in_dim(route_weights, row_first, quarter, 0)
    resid_full = resid_part.astype(f32)
    inv_rms = lax.rsqrt(jnp.mean(resid_full * resid_full, axis=-1, keepdims=True) + EPSILON)
    normed = (resid_full * inv_rms * norm_gain.astype(f32)).astype(bf16)
    grad_full = grad_part.astype(f32)

    row_ids = jnp.arange(quarter, dtype=jnp.int32)
    earlier = row_ids[:, None] < row_ids[None, :]

    def slots_of(expert):
        matched = ids_part == expert
        routed = jnp.any(matched, axis=1)
        position = jnp.sum((earlier & routed[:, None]).astype(jnp.int32), axis=0)
        weight = jnp.sum(jnp.where(matched, weights_part, 0.0), axis=1)
        return routed, position, weight

    routed, position, weight = slots_of(exp_index)
    slot_ids = jnp.arange(CAP, dtype=jnp.int32)
    select = ((position[None, :] == slot_ids[:, None]) & routed[None, :]).astype(bf16)
    scaled = (weight[:, None] * grad_full).astype(bf16)
    slot_in = jnp.dot(select, normed, preferred_element_type=f32).astype(bf16)
    slot_grad = jnp.dot(select, scaled, preferred_element_type=f32).astype(bf16)
    mine = jnp.concatenate([slot_in, slot_grad], axis=0)

    rows = lax.all_gather(mine, "z", axis=0, tiled=True)
    gate_mat, up_mat, down_mat, w_mine, mine = lax.optimization_barrier(
        (w_gate[0].T, w_up[0].T, w_down[0], w_out, mine)
    )
    gate_two = jnp.concatenate([gate_mat, core_swap(gate_mat)], axis=0)
    up_two = jnp.concatenate([up_mat, core_swap(up_mat)], axis=0)
    down_two = jnp.concatenate([down_mat, core_swap(down_mat)], axis=0)
    w_near = [w_mine] + [
        lax.ppermute(w_mine, "head", [(a, (a - d) % head_count) for a in range(head_count)])
        for d in range(1, head_count)
    ]
    w_four = jnp.concatenate(w_near, axis=0)

    units = gate_two.shape[0]
    gate_all = lax.dot_general(rows, gate_two, CONTRACT, preferred_element_type=f32)
    up_all = lax.dot_general(rows, up_two, CONTRACT, preferred_element_type=f32)
    down_all = lax.dot_general(rows, down_two, CONTRACT, preferred_element_type=f32)
    gate_val = gate_all.reshape(z_count, 2 * CAP, units)[:, :CAP].reshape(-1, units)
    up_val = up_all.reshape(z_count, 2 * CAP, units)[:, :CAP].reshape(-1, units)
    hidden_grad = down_all.reshape(z_count, 2 * CAP, units)[:, CAP:].reshape(-1, units)
    sigma = jax.nn.sigmoid(gate_val)
    gate_grad = (hidden_grad * up_val * sigma * (1.0 + gate_val * (1.0 - sigma))).astype(bf16)
    up_grad = (hidden_grad * gate_val * sigma).astype(bf16)
    back = jnp.dot(gate_grad, gate_two, preferred_element_type=f32)
    back = back + jnp.dot(up_grad, up_two, preferred_element_type=f32)

    pair, rows = lax.optimization_barrier((jnp.concatenate([keys, values], axis=1), rows))
    pair_here = lax.all_gather(pair, "z", axis=0, tiled=True)
    pair_all = jnp.concatenate([pair_here, core_swap(pair_here)], axis=0)
    key_all, value_all = pair_all[:, :HD], pair_all[:, HD:]

    part = width // FOLD
    left = back.reshape(z_count, CAP, FOLD, part).transpose(0, 2, 1, 3)
    left = left.reshape(z_count, FOLD * CAP, part)
    dist = 1
    while dist < z_count:
        bit = (z_index // dist) % 2
        two = left.reshape(left.shape[0] // 2, 2, FOLD * CAP, part)
        stay = lax.dynamic_index_in_dim(two, bit, 1, keepdims=False)
        leave = lax.dynamic_index_in_dim(two, 1 - bit, 1, keepdims=False).astype(bf16)
        left = stay + spread(leave, "z", z_count, dist).astype(f32)
        dist *= 2
    slots = left.astype(bf16)
    offsets = [0]
    dist = exp_count // 2
    while dist >= 1:
        slots = jnp.concatenate([slots, spread(slots, "exp", exp_count, dist)], axis=0)
        offsets = offsets + [o + dist for o in offsets]
        dist //= 2
    toward = jnp.where(core_index == 0, -1, 1)
    picks = []
    for offset in offsets:
        routed, position, _ = slots_of((exp_index + toward * offset + exp_count) % exp_count)
        picks.append((position[:, None] == slot_ids[None, :]) & routed[:, None])
    picks = jnp.stack(picks, axis=1).astype(bf16)
    flat = slots.reshape(exp_count * FOLD * CAP, part)
    pieces = []
    for q in range(FOLD):
        there = jnp.zeros((quarter, exp_count, FOLD, CAP), bf16).at[:, :, q].set(picks)
        pieces.append(jnp.dot(there.reshape(quarter, -1), flat, preferred_element_type=f32))
    summed = jnp.concatenate(pieces, axis=1)
    grad_quarter = norm_back(resid_full, inv_rms, grad_full, norm_gain, summed)

    at_heads = lax.dot_general(grad_quarter, w_four, CONTRACT, preferred_element_type=f32)
    at_heads = at_heads.astype(bf16)
    pieces = [at_heads[:, :HD]] + [
        lax.ppermute(
            at_heads[:, d * HD : (d + 1) * HD],
            "head",
            [(a, (a + d) % head_count) for a in range(head_count)],
        )
        for d in range(1, head_count)
    ]
    stacked = jnp.stack(pieces[::-1] + pieces[::-1], axis=0).reshape(-1, HD)
    attn_grad = lax.dynamic_slice_in_dim(
        stacked, (head_count - 1 - head_index) * quarter, head_count * quarter, 0
    )

    scale = HD ** (-0.5)
    highest = lax.Precision.HIGHEST
    query_pos = (z_index * 2 + core_index) * tok_rows + jnp.arange(tok_rows, dtype=jnp.int32)
    place = jnp.arange(2 * z_count * tok_rows, dtype=jnp.int32)
    half = z_count * tok_rows
    shard = (place % half) // tok_rows * 2 + (core_index + place // half) % 2
    key_pos = shard * tok_rows + place % tok_rows
    allowed = key_pos[None, :] <= query_pos[:, None]
    scores = lax.dot_general(queries, key_all, CONTRACT, preferred_element_type=f32) * scale
    scores = jnp.where(allowed, scores, -1e30)
    row_max = jnp.max(scores, axis=-1, keepdims=True)
    expo_vals = jnp.where(allowed, jnp.exp(scores - row_max), 0.0)
    probs = expo_vals / jnp.sum(expo_vals, axis=-1, keepdims=True)
    output = jnp.dot(probs, value_all.astype(f32), precision=highest)
    delta = jnp.sum(attn_grad.astype(f32) * output, axis=-1, keepdims=True)
    prob_grad = lax.dot_general(attn_grad, value_all, CONTRACT, preferred_element_type=f32)
    mixed = probs * (prob_grad - delta)
    query_grad = (scale * jnp.dot(mixed, key_all.astype(f32), precision=highest)).astype(bf16)
    return (grad_quarter, query_grad)


def solution(mesh):
    seq, exp, head = mesh.shape["seq"], mesh.shape["exp"], mesh.shape["head"]
    fine = Mesh(mesh.devices.reshape(seq // 2, 2, exp, head), ("z", "core", "exp", "head"))
    seq_axes = ("z", "core")
    in_specs = (
        P(seq_axes, None),
        P(seq_axes, None),
        P(),
        P(seq_axes, None),
        P(seq_axes, None),
        P("exp", None, seq_axes),
        P("exp", None, seq_axes),
        P("exp", seq_axes, None),
        P(("exp", "head"), None),
        P(seq_axes, ("exp", "head")),
        P(seq_axes, ("exp", "head")),
        P(seq_axes, ("exp", "head")),
    )
    out_specs = (P(("z", "core", "head"), None), P(seq_axes, ("exp", "head")))
    return jax.shard_map(
        per_device, mesh=fine, in_specs=in_specs, out_specs=out_specs, check_vma=False
    )
```

time: 741 us -> 334 us (0.45)
  waiting for transfers between devices: 519 us -> 164 us
  blocking collectives: 60.2 us -> 0 us
  starting transfers between devices: 56.1 us -> 83.1 us
  local copies, waits for them, and re-layouts: 42.7 us -> 30.2 us
    all_gather x5 -> x2, waiting for transfers between devices: 389 us -> 106 us  [the longest x1 62.4 us: per_device(): pair_here = lax.all_gather(pair, 'z', axis=0, tiled=True)]
    unnamed x15 -> x2, waiting for transfers between devices: 130 us -> 0.03 us
    ppermute x0 -> x17, starting transfers between devices: none -> 83.1 us  [the longest x4 32.4 us: core_swap(): return lax.ppermute(block, 'core', [(0, 1), (1, 0)])]
    unnamed x1 -> x0, blocking collectives: 60.2 us -> none
    ppermute x0 -> x17, waiting for transfers between devices: none -> 58.4 us  [the longest x4 35.5 us: spread(): return lax.ppermute(rows, ('z', 'core'), pairs)]
    unnamed x9 -> x0, starting transfers between devices: 55.7 us -> none
    unnamed x19 -> x35, local copies, waits for them, and re-layouts: 37.8 us -> 5.3 us
    dot_general x13 -> x16, matrix products: 38.3 us -> 31.1 us  [the longest x1 4.82 us: per_device(): up_all = lax.dot_general(rows, up_two, CONTRACT, preferred_element_type=f32)]
  transfers between devices with their start and end apart: 14 -> 19, of which waited for: 7 -> 10; matrix products, arithmetic and copies ran while one was open for 4% -> 17% of each run, Pallas kernels for 0% -> 0%
where the time goes in v2:
time: 334 us; the launch traced here: 333 us
  waiting for transfers between devices  164 us (49%)
  starting transfers between devices  83.1 us (25%)
  matrix products  31.1 us (9%)
  local copies, waits for them, and re-layouts  30.2 us (9%)
  between operations  14.9 us (4%)
  other arithmetic  9.07 us (3%)
    all_gather x1, waiting for transfers between devices, per_device(): pair_here = lax.all_gather(pair, 'z', axis=0, tiled=True)  62.4 us
    all_gather x1, waiting for transfers between devices, per_device(): rows = lax.all_gather(mine, 'z', axis=0, tiled=True)  43.4 us
    ppermute x4, waiting for transfers between devices, spread(): return lax.ppermute(rows, ('z', 'core'), pairs)  35.5 us
    ppermute x4, starting transfers between devices, core_swap(): return lax.ppermute(block, 'core', [(0, 1), (1, 0)])  32.4 us
    ppermute x4, starting transfers between devices, spread(): return lax.ppermute(rows, ('z', 'core'), pairs)  21.6 us
    ppermute x3, waiting for transfers between devices, spread(): return lax.ppermute(rows, ('core', axis), pairs)  19.5 us
    ppermute x3, starting transfers between devices, per_device(): lax.ppermute(at_heads[:, d * HD:(d + 1) * HD], 'head', [(a, (a + d) % hea...  11.9 us
    ppermute x3, starting transfers between devices, spread(): return lax.ppermute(rows, ('core', axis), pairs)  9.69 us
  transfers between devices with their start and end apart: 19, of which 10 were waited for; matrix products, arithmetic and copies ran while one was open for 17% of the time, Pallas kernels for 0%

profile of v2, /device:TPU:1, one launch (start us, length us, event | category | flops | bytes accessed | tf_op | source)
XLA Modules:
  0.0 332.6 jit_solution(8975604809416566709)
XLA Ops:
  10.1 1.2 convolution_convert_fusion.1
  11.3 1.2 convolution_convert_fusion
  13.3 16.1 %collective-permute-start.2 = (bf16[200,4096]{1,0:T(8,128)(2,1)}, bf16[200,4096]{1,0:T(8,128)(2,1)}, u32[]{:S(2)}, u32[]{:S(2)}) collective-permute-start(bf16[200,4096]{1,0:T(8,128)(2,1)} %bitcast.9), channel_id=1, source_target_pairs={{0,32},{32,0},{1,33},{33,1},{2,34},{34,2},{3,35},{35,3},{4,36},{36... | collective-permute-start | bytes 4915208 | tf_op jit(solution)/shard_map/ppermute | solution.py:25
  29.4 1.9 collective-permute-start.1
  31.3 1.9 collective-permute-start.11
  33.2 1.9 collective-permute-start.12
  35.1 2.4 collective-permute-start
  37.7 3.4 %constant_dynamic-update-slice_fusion.9 = (bf16[400,4096]{1,0:T(8,128)(2,1)}, bf16[400,4096]{1,0:T(8,128)(2,1)S(1)}) fusion(bf16[200,4096]{1,0:T(8,128)(2,1)} %bitcast.11, bf16[200,4096]{1,0:T(8,128)(2,1)} %bitcast.9), kind=kLoop, calls=%fused_computation.84 | loop fusion | bytes 6553600
  41.2 3.6 %collective-permute-start.13 = (bf16[128,4096]{1,0:T(8,128)(2,1)}, bf16[128,4096]{1,0:T(8,128)(2,1)}, u32[]{:S(2)}, u32[]{:S(2)}) collective-permute-start(bf16[128,4096]{1,0:T(8,128)(2,1)} %param.28), channel_id=1, source_target_pairs={{0,1},{1,2},{2,3},{3,0},{4,5},{5,6},{6,7},{7,4},{8,9},{9,10},{10,1... | collective-permute-start | bytes 3145736 | tf_op jit(solution)/shard_map/ppermute | solution.py:91
  44.9 1.5 constant_dynamic-update-slice_fusion.10
  46.4 4.0 %constant_dynamic-update-slice_fusion.8 = bf16[400,4096]{1,0:T(8,128)(2,1)} fusion(bf16[400,4096]{1,0:T(8,128)(2,1)} %get-tuple-element.90, bf16[200,4096]{1,0:T(8,128)(2,1)} %collective-permute-done.1), kind=kLoop, calls=%fused_computation.83 | loop fusion | bytes 3276800 | tf_op jit(solution)/shard_map/concatenate | solution.py:88
  50.4 43.4 %all-gather.3.cloned.1.call-done = bf16[384,4096]{1,0:T(8,128)(2,1)} async-done(((bf16[24,4096]{1,0:T(8,128)(2,1)}), bf16[384,4096]{1,0:T(8,128)(2,1)}) %all-gather.3.cloned.1.call-update) | async-done | bytes 3145744 | tf_op jit(solution)/shard_map/all_gather | solution.py:83
  93.8 3.7 %fusion.109 = f32[384,400]{1,0:T(8,128)S(1)} fusion(bf16[384,4096]{1,0:T(8,128)(2,1)} %all-gather.3.cloned.1.call-done, bf16[400,4096]{1,0:T(8,128)(2,1)S(1)} %constant_dynamic-update-slice_fusion.10), kind=kOutput, calls=%fused_computation.209 | convolution fusion | flops 1258291200 | bytes 7036928 | tf_op jit(solution)/shard_map/dot_general | solution.py:97
  97.6 4.8 %fusion.11 = f32[384,400]{1,0:T(8,128)S(1)} fusion(bf16[384,4096]{1,0:T(8,128)(2,1)} %all-gather.3.cloned.1.call-done, bf16[200,4096]{1,0:T(8,128)(2,1)} %collective-permute-done, bf16[200,4096]{1,0:T(8,128)(2,1)} %bitcast.12), kind=kOutput, calls=%fused_computation.16 | convolution fusion | flops 1264844800 | bytes 7036928 | tf_op jit(solution)/shard_map/dot_general | solution.py:99
  102.6 4.8 %fusion.108 = f32[384,400]{1,0:T(8,128)S(1)} fusion(bf16[384,4096]{1,0:T(8,128)(2,1)} %all-gather.3.cloned.1.call-done, bf16[400,4096]{1,0:T(8,128)(2,1)} %constant_dynamic-update-slice_fusion.8), kind=kOutput, calls=%fused_computation.208 | convolution fusion | flops 1258291200 | bytes 7036928 | tf_op jit(solution)/shard_map/dot_general | solution.py:98
  108.3 3.1 fusion.41
  111.4 2.2 convolution_add_fusion
  113.6 3.4 %reshape.745 = f32[16,12,4,1024]{3,2,1,0:T(4,128)} reshape(f32[192,4096]{1,0:T(8,128)S(1)} %convolution_add_fusion) | data formatting | bytes 6291456 | tf_op jit(solution)/shard_map/reshape | solution.py:115
  117.0 3.7 %copy.57 = f32[16,12,4,1024]{3,0,1,2:T(8,128)S(1)} copy(f32[16,12,4,1024]{3,2,1,0:T(4,128)} %reshape.745) | data formatting | bytes 6291456 | tf_op jit(solution)/shard_map/reshape | solution.py:115
  120.7 3.2 reshape_reshape.3
  123.9 3.7 %dynamic-slice_convert_fusion = bf16[8,1,48,1024]{3,1,0,2:T(2,128)(2,1)S(1)} fusion(f32[8,2,48,1024]{3,1,0,2:T(2,128)} %reshape_reshape.3, s32[]{:T(128)S(6)} %select_n.169), kind=kLoop, calls=%fused_computation.25 | loop fusion | bytes 1572868 | tf_op jit(solution)/shard_map/convert_element_type | solution.py:122
  128.5 3.7 %collective-permute-start.3 = (bf16[8,48,1024]{2,1,0:T(8,128)(2,1)S(1)}, bf16[8,48,1024]{2,1,0:T(8,128)(2,1)S(1)}, u32[]{:S(2)}, u32[]{:S(2)}) collective-permute-start(bf16[8,48,1024]{2,1,0:T(8,128)(2,1)S(1)} %bitcast.129), channel_id=1, source_target_pairs={{0,64},{64,128},{128,192},{192,256},{256,320},{320,384},{384,448},... | collective-permute-start | bytes 2359304 | tf_op jit(solution)/shard_map/ppermute | solution.py:19
  132.3 1.7 constant_dynamic-slice_fusion.1
  134.0 7.3 %collective-permute-done.3 = bf16[8,48,1024]{2,1,0:T(8,128)(2,1)S(1)} collective-permute-done((bf16[8,48,1024]{2,1,0:T(8,128)(2,1)S(1)}, bf16[8,48,1024]{2,1,0:T(8,128)(2,1)S(1)}, u32[]{:S(2)}, u32[]{:S(2)}) %collective-permute-start.3) | collective-permute-done | bytes 786464 | tf_op jit(solution)/shard_map/ppermute | solution.py:19
  142.2 3.5 %collective-permute-start.4 = (bf16[4,48,1024]{2,1,0:T(8,128)(2,1)S(1)}, bf16[4,48,1024]{2,1,0:T(8,128)(2,1)S(1)}, u32[]{:S(2)}, u32[]{:S(2)}) collective-permute-start(bf16[4,48,1024]{2,1,0:T(8,128)(2,1)S(1)} %fusion.34), channel_id=1, source_target_pairs={{0,128},{64,192},{128,256},{192,320},{256,384},{320,448},{384,512}... | collective-permute-start | bytes 1179656 | tf_op jit(solution)/shard_map/ppermute | solution.py:19
  146.0 8.2 %collective-permute-done.4 = bf16[4,48,1024]{2,1,0:T(8,128)(2,1)S(1)} collective-permute-done((bf16[4,48,1024]{2,1,0:T(8,128)(2,1)S(1)}, bf16[4,48,1024]{2,1,0:T(8,128)(2,1)S(1)}, u32[]{:S(2)}, u32[]{:S(2)}) %collective-permute-start.4) | collective-permute-done | bytes 393248 | tf_op jit(solution)/shard_map/ppermute | solution.py:19
  154.4 4.9 %collective-permute-start.5 = (bf16[2,48,1024]{2,1,0:T(8,128)(2,1)S(1)}, bf16[2,48,1024]{2,1,0:T(8,128)(2,1)S(1)}, u32[]{:S(2)}, u32[]{:S(2)}) collective-permute-start(bf16[2,48,1024]{2,1,0:T(8,128)(2,1)S(1)} %fusion.42), channel_id=1, source_target_pairs={{0,256},{64,320},{128,384},{192,448},{256,512},{320,576},{384,640}... | collective-permute-start | bytes 589832 | tf_op jit(solution)/shard_map/ppermute | solution.py:19
  159.3 6.5 %collective-permute-done.5 = bf16[2,48,1024]{2,1,0:T(8,128)(2,1)S(1)} collective-permute-done((bf16[2,48,1024]{2,1,0:T(8,128)(2,1)S(1)}, bf16[2,48,1024]{2,1,0:T(8,128)(2,1)S(1)}, u32[]{:S(2)}, u32[]{:S(2)}) %collective-permute-start.5) | collective-permute-done | bytes 196640 | tf_op jit(solution)/shard_map/ppermute | solution.py:19
  165.9 9.4 %collective-permute-start.6 = (bf16[1,48,1024]{2,1,0:T(8,128)(2,1)S(1)}, bf16[1,48,1024]{2,1,0:T(8,128)(2,1)S(1)}, u32[]{:S(2)}, u32[]{:S(2)}) collective-permute-start(bf16[1,48,1024]{2,1,0:T(8,128)(2,1)S(1)} %dynamic-slice_convert_fusion.1), channel_id=1, source_target_pairs={{0,512},{64,576},{128,640},{192,704},{256,768},{320,832},{384,896}... | collective-permute-start | bytes 294920 | tf_op jit(solution)/shard_map/ppermute | solution.py:19
  175.4 13.4 %collective-permute-done.6 = bf16[1,48,1024]{2,1,0:T(8,128)(2,1)S(1)} collective-permute-done((bf16[1,48,1024]{2,1,0:T(8,128)(2,1)S(1)}, bf16[1,48,1024]{2,1,0:T(8,128)(2,1)S(1)}, u32[]{:S(2)}, u32[]{:S(2)}) %collective-permute-start.6) | collective-permute-done | bytes 98336 | tf_op jit(solution)/shard_map/ppermute | solution.py:19
  188.9 5.5 %collective-permute-start.7 = (bf16[1,48,1024]{2,1,0:T(8,128)(2,1)S(1)}, bf16[1,48,1024]{2,1,0:T(8,128)(2,1)S(1)}, u32[]{:S(2)}, u32[]{:S(2)}) collective-permute-start(bf16[1,48,1024]{2,1,0:T(8,128)(2,1)S(1)} %add_convert_fusion), channel_id=1, source_target_pairs={{0,16},{4,20},{8,24},{12,28},{16,0},{20,4},{24,8},{28,12},{32,48},... | collective-permute-start | bytes 294920 | tf_op jit(solution)/shard_map/ppermute | solution.py:21
  194.4 4.6 %collective-permute-done.7 = bf16[1,48,1024]{2,1,0:T(8,128)(2,1)S(1)} collective-permute-done((bf16[1,48,1024]{2,1,0:T(8,128)(2,1)S(1)}, bf16[1,48,1024]{2,1,0:T(8,128)(2,1)S(1)}, u32[]{:S(2)}, u32[]{:S(2)}) %collective-permute-start.7) | collective-permute-done | bytes 98336 | tf_op jit(solution)/shard_map/ppermute | solution.py:21
  199.1 1.9 collective-permute-start.8
  201.1 7.5 %collective-permute-done.8 = bf16[2,48,1024]{2,1,0:T(8,128)(2,1)S(1)} collective-permute-done((bf16[2,48,1024]{2,1,0:T(8,128)(2,1)S(1)}, bf16[2,48,1024]{2,1,0:T(8,128)(2,1)S(1)}, u32[]{:S(2)}, u32[]{:S(2)}) %collective-permute-start.8) | collective-permute-done | bytes 196640 | tf_op jit(solution)/shard_map/ppermute | solution.py:21
  208.6 2.2 collective-permute-start.9
  211.9 7.4 %collective-permute-done.9 = bf16[4,48,1024]{2,1,0:T(8,128)(2,1)S(1)} collective-permute-done((bf16[4,48,1024]{2,1,0:T(8,128)(2,1)S(1)}, bf16[4,48,1024]{2,1,0:T(8,128)(2,1)S(1)}, u32[]{:S(2)}, u32[]{:S(2)}) %collective-permute-start.9) | collective-permute-done | bytes 393248 | tf_op jit(solution)/shard_map/ppermute | solution.py:21
  222.0 3.1 fusion.18
  225.1 5.1 %collective-permute-start.14 = (bf16[32,128]{1,0:T(8,128)(2,1)S(1)}, bf16[32,128]{1,0:T(8,128)(2,1)S(1)}, u32[]{:S(2)}, u32[]{:S(2)}) collective-permute-start(bf16[32,128]{1,0:T(8,128)(2,1)S(1)} %get-tuple-element.73), channel_id=1, source_target_pairs={{0,3},{1,0},{2,1},{3,2},{4,7},{5,4},{6,5},{7,6},{8,11},{9,8},{10,9... | collective-permute-start | bytes 24584 | tf_op jit(solution)/shard_map/ppermute | solution.py:149
  230.2 62.4 %all-gather.5.cloned.1.call-done = bf16[2048,256]{1,0:T(8,128)(2,1)} async-done(((bf16[128,256]{1,0:T(8,128)(2,1)}), bf16[2048,256]{1,0:T(8,128)(2,1)}) %all-gather.5.cloned.1.call-update) | async-done | bytes 1048592 | tf_op jit(solution)/shard_map/all_gather | solution.py:110
  292.6 1.4 constant_dynamic-update-slice_fusion.13
  294.1 12.0 %collective-permute-start.10 = (bf16[2048,256]{1,0:T(8,128)(2,1)S(1)}, bf16[2048,256]{1,0:T(8,128)(2,1)}, u32[]{:S(2)}, u32[]{:S(2)}) collective-permute-start(bf16[2048,256]{1,0:T(8,128)(2,1)S(1)} %copy-done.7), channel_id=1, source_target_pairs={{0,32},{32,0},{1,33},{33,1},{2,34},{34,2},{3,35},{35,3},{4,36},{36... | collective-permute-start | bytes 3145736 | tf_op jit(solution)/shard_map/ppermute | solution.py:25
  306.1 4.6 %collective-permute-start.15 = (bf16[32,128]{1,0:T(8,128)(2,1)S(1)}, bf16[32,128]{1,0:T(8,128)(2,1)S(1)}, u32[]{:S(2)}, u32[]{:S(2)}) collective-permute-start(bf16[32,128]{1,0:T(8,128)(2,1)S(1)} %get-tuple-element.72), channel_id=1, source_target_pairs={{0,2},{1,3},{2,0},{3,1},{4,6},{5,7},{6,4},{7,5},{8,10},{9,11},{10,... | collective-permute-start | bytes 24584 | tf_op jit(solution)/shard_map/ppermute | solution.py:149
  310.8 2.2 collective-permute-start.16
  313.0 3.4 %collective-permute-done.16 = bf16[32,128]{1,0:T(8,128)(2,1)S(1)} collective-permute-done((bf16[32,128]{1,0:T(8,128)(2,1)S(1)}, bf16[32,128]{1,0:T(8,128)(2,1)S(1)}, u32[]{:S(2)}, u32[]{:S(2)}) %collective-permute-start.16) | collective-permute-done | bytes 8224 | tf_op jit(solution)/shard_map/ppermute | solution.py:149
  316.6 1.3 constant_dynamic-update-slice_fusion.12
  318.8 1.9 fusion.16
  320.7 1.9 fusion.21
  323.3 2.5 fusion.17
  (102 shorter events, 12.8 us)
Async XLA Ops:
  7.2 310.7 %copy-start = (bf16[128,128]{1,0:T(8,128)(2,1)S(1)}, bf16[128,128]{1,0:T(8,128)(2,1)}, u32[]{:S(2)}) copy-start(bf16[128,128]{1,0:T(8,128)(2,1)} %param.29) | copy-start | bytes 98308
  7.2 86.6 %all-gather.3.cloned.1.call-start = ((), (), s32[]{:S(2)}) async-start(), calls=%async_computation | async-start | bytes 3342336 | tf_op jit(solution)/shard_map/all_gather | solution.py:83
  13.2 279.3 %all-gather.5.cloned.1.call-start = ((), (), s32[]{:S(2)}) async-start(), calls=%async_computation.1 | async-start | bytes 1114112 | tf_op jit(solution)/shard_map/all_gather | solution.py:110
  13.3 27.9 %collective-permute-start.2 = (bf16[200,4096]{1,0:T(8,128)(2,1)}, bf16[200,4096]{1,0:T(8,128)(2,1)}, u32[]{:S(2)}, u32[]{:S(2)}) collective-permute-start(bf16[200,4096]{1,0:T(8,128)(2,1)} %bitcast.9), channel_id=1, source_target_pairs={{0,32},{32,0},{1,33},{33,1},{2,34},{34,2},{3,35},{35,3},{4,36},{36... | collective-permute-start | bytes 4915208 | tf_op jit(solution)/shard_map/ppermute | solution.py:25
  29.4 17.1 %collective-permute-start.1 = (bf16[200,4096]{1,0:T(8,128)(2,1)}, bf16[200,4096]{1,0:T(8,128)(2,1)}, u32[]{:S(2)}, u32[]{:S(2)}) collective-permute-start(bf16[200,4096]{1,0:T(8,128)(2,1)} %bitcast.11), channel_id=1, source_target_pairs={{0,32},{32,0},{1,33},{33,1},{2,34},{34,2},{3,35},{35,3},{4,36},{36... | collective-permute-start | bytes 4915208 | tf_op jit(solution)/shard_map/ppermute | solution.py:25
  31.3 190.6 %collective-permute-start.11 = (bf16[128,4096]{1,0:T(8,128)(2,1)}, bf16[128,4096]{1,0:T(8,128)(2,1)}, u32[]{:S(2)}, u32[]{:S(2)}) collective-permute-start(bf16[128,4096]{1,0:T(8,128)(2,1)} %param.28), channel_id=1, source_target_pairs={{0,3},{1,0},{2,1},{3,2},{4,7},{5,4},{6,5},{7,6},{8,11},{9,8},{10,9... | collective-permute-start | bytes 3145736 | tf_op jit(solution)/shard_map/ppermute | solution.py:91
  33.2 188.7 %collective-permute-start.12 = (bf16[128,4096]{1,0:T(8,128)(2,1)}, bf16[128,4096]{1,0:T(8,128)(2,1)}, u32[]{:S(2)}, u32[]{:S(2)}) collective-permute-start(bf16[128,4096]{1,0:T(8,128)(2,1)} %param.28), channel_id=1, source_target_pairs={{0,2},{1,3},{2,0},{3,1},{4,6},{5,7},{6,4},{7,5},{8,10},{9,11},{10,... | collective-permute-start | bytes 3145736 | tf_op jit(solution)/shard_map/ppermute | solution.py:91
  35.1 62.5 %collective-permute-start = (bf16[200,4096]{1,0:T(8,128)(2,1)}, bf16[200,4096]{1,0:T(8,128)(2,1)}, u32[]{:S(2)}, u32[]{:S(2)}) collective-permute-start(bf16[200,4096]{1,0:T(8,128)(2,1)} %bitcast.12), channel_id=1, source_target_pairs={{0,32},{32,0},{1,33},{33,1},{2,34},{34,2},{3,35},{35,3},{4,36},{36... | collective-permute-start | bytes 4915208 | tf_op jit(solution)/shard_map/ppermute | solution.py:25
  41.2 180.8 %collective-permute-start.13 = (bf16[128,4096]{1,0:T(8,128)(2,1)}, bf16[128,4096]{1,0:T(8,128)(2,1)}, u32[]{:S(2)}, u32[]{:S(2)}) collective-permute-start(bf16[128,4096]{1,0:T(8,128)(2,1)} %param.28), channel_id=1, source_target_pairs={{0,1},{1,2},{2,3},{3,0},{4,5},{5,6},{6,7},{7,4},{8,9},{9,10},{10,1... | collective-permute-start | bytes 3145736 | tf_op jit(solution)/shard_map/ppermute | solution.py:91
  46.4 51.1 %copy-start.2 = (bf16[400,4096]{1,0:T(8,128)(2,1)}, bf16[400,4096]{1,0:T(8,128)(2,1)S(1)}, u32[]{:S(2)}) copy-start(bf16[400,4096]{1,0:T(8,128)(2,1)S(1)} %constant_dynamic-update-slice_fusion.10) | copy-start | bytes 9830404
  97.6 10.7 %copy-start.4 = (f32[192,400]{1,0:T(8,128)}, f32[192,400]{1,0:T(8,128)S(1)}, u32[]{:S(2)}) copy-start(f32[192,400]{1,0:T(8,128)S(1)} %reshape.744) | copy-start | bytes 921604
  102.6 5.7 %copy-start.5 = (f32[192,400]{1,0:T(8,128)}, f32[192,400]{1,0:T(8,128)S(1)}, u32[]{:S(2)}) copy-start(f32[192,400]{1,0:T(8,128)S(1)} %reshape.740) | copy-start | bytes 921604
  108.3 3.1 copy-start.3
  108.3 3.1 copy-start.6
  123.9 8.4 %copy-start.1 = (f32[8,2,48,1024]{3,1,0,2:T(2,128)S(1)}, f32[8,2,48,1024]{3,1,0,2:T(2,128)}, u32[]{:S(2)}) copy-start(f32[8,2,48,1024]{3,1,0,2:T(2,128)} %reshape_reshape.3) | copy-start | bytes 9437188
  128.5 12.7 %collective-permute-start.3 = (bf16[8,48,1024]{2,1,0:T(8,128)(2,1)S(1)}, bf16[8,48,1024]{2,1,0:T(8,128)(2,1)S(1)}, u32[]{:S(2)}, u32[]{:S(2)}) collective-permute-start(bf16[8,48,1024]{2,1,0:T(8,128)(2,1)S(1)} %bitcast.129), channel_id=1, source_target_pairs={{0,64},{64,128},{128,192},{192,256},{256,320},{320,384},{384,448},... | collective-permute-start | bytes 2359304 | tf_op jit(solution)/shard_map/ppermute | solution.py:19
  142.2 12.0 %collective-permute-start.4 = (bf16[4,48,1024]{2,1,0:T(8,128)(2,1)S(1)}, bf16[4,48,1024]{2,1,0:T(8,128)(2,1)S(1)}, u32[]{:S(2)}, u32[]{:S(2)}) collective-permute-start(bf16[4,48,1024]{2,1,0:T(8,128)(2,1)S(1)} %fusion.34), channel_id=1, source_target_pairs={{0,128},{64,192},{128,256},{192,320},{256,384},{320,448},{384,512}... | collective-permute-start | bytes 1179656 | tf_op jit(solution)/shard_map/ppermute | solution.py:19
  154.4 11.4 %collective-permute-start.5 = (bf16[2,48,1024]{2,1,0:T(8,128)(2,1)S(1)}, bf16[2,48,1024]{2,1,0:T(8,128)(2,1)S(1)}, u32[]{:S(2)}, u32[]{:S(2)}) collective-permute-start(bf16[2,48,1024]{2,1,0:T(8,128)(2,1)S(1)} %fusion.42), channel_id=1, source_target_pairs={{0,256},{64,320},{128,384},{192,448},{256,512},{320,576},{384,640}... | collective-permute-start | bytes 589832 | tf_op jit(solution)/shard_map/ppermute | solution.py:19
  159.2 52.0 %copy-start.10 = (bf16[128,128]{1,0:T(8,128)(2,1)S(1)}, bf16[128,128]{1,0:T(8,128)(2,1)}, u32[]{:S(2)}) copy-start(bf16[128,128]{1,0:T(8,128)(2,1)} %param.31) | copy-start | bytes 98308
  159.3 52.0 %copy-start.11 = (bf16[128,128]{1,0:T(8,128)(2,1)S(1)}, bf16[128,128]{1,0:T(8,128)(2,1)}, u32[]{:S(2)}) copy-start(bf16[128,128]{1,0:T(8,128)(2,1)} %param.30) | copy-start | bytes 98308
  165.9 23.0 %collective-permute-start.6 = (bf16[1,48,1024]{2,1,0:T(8,128)(2,1)S(1)}, bf16[1,48,1024]{2,1,0:T(8,128)(2,1)S(1)}, u32[]{:S(2)}, u32[]{:S(2)}) collective-permute-start(bf16[1,48,1024]{2,1,0:T(8,128)(2,1)S(1)} %dynamic-slice_convert_fusion.1), channel_id=1, source_target_pairs={{0,512},{64,576},{128,640},{192,704},{256,768},{320,832},{384,896}... | collective-permute-start | bytes 294920 | tf_op jit(solution)/shard_map/ppermute | solution.py:19
  188.9 10.2 %collective-permute-start.7 = (bf16[1,48,1024]{2,1,0:T(8,128)(2,1)S(1)}, bf16[1,48,1024]{2,1,0:T(8,128)(2,1)S(1)}, u32[]{:S(2)}, u32[]{:S(2)}) collective-permute-start(bf16[1,48,1024]{2,1,0:T(8,128)(2,1)S(1)} %add_convert_fusion), channel_id=1, source_target_pairs={{0,16},{4,20},{8,24},{12,28},{16,0},{20,4},{24,8},{28,12},{32,48},... | collective-permute-start | bytes 294920 | tf_op jit(solution)/shard_map/ppermute | solution.py:21
  199.1 9.5 %collective-permute-start.8 = (bf16[2,48,1024]{2,1,0:T(8,128)(2,1)S(1)}, bf16[2,48,1024]{2,1,0:T(8,128)(2,1)S(1)}, u32[]{:S(2)}, u32[]{:S(2)}) collective-permute-start(bf16[2,48,1024]{2,1,0:T(8,128)(2,1)S(1)} %pad_maximum_fusion.3), channel_id=1, source_target_pairs={{0,8},{4,12},{8,16},{12,20},{16,24},{20,28},{24,0},{28,4},{32,56},... | collective-permute-start | bytes 589832 | tf_op jit(solution)/shard_map/ppermute | solution.py:21
  208.6 10.6 %collective-permute-start.9 = (bf16[4,48,1024]{2,1,0:T(8,128)(2,1)S(1)}, bf16[4,48,1024]{2,1,0:T(8,128)(2,1)S(1)}, u32[]{:S(2)}, u32[]{:S(2)}) collective-permute-start(bf16[4,48,1024]{2,1,0:T(8,128)(2,1)S(1)} %pad_maximum_fusion.1), channel_id=1, source_target_pairs={{0,4},{4,8},{8,12},{12,16},{16,20},{20,24},{24,28},{28,0},{32,60},... | collective-permute-start | bytes 1179656 | tf_op jit(solution)/shard_map/ppermute | solution.py:21
  219.3 1.2 copy-start.8
  221.9 3.1 copy-start.9
  225.1 87.9 %collective-permute-start.14 = (bf16[32,128]{1,0:T(8,128)(2,1)S(1)}, bf16[32,128]{1,0:T(8,128)(2,1)S(1)}, u32[]{:S(2)}, u32[]{:S(2)}) collective-permute-start(bf16[32,128]{1,0:T(8,128)(2,1)S(1)} %get-tuple-element.73), channel_id=1, source_target_pairs={{0,3},{1,0},{2,1},{3,2},{4,7},{5,4},{6,5},{7,6},{8,11},{9,8},{10,9... | collective-permute-start | bytes 24584 | tf_op jit(solution)/shard_map/ppermute | solution.py:149
  292.6 1.5 copy-start.7
  294.1 22.4 %collective-permute-start.10 = (bf16[2048,256]{1,0:T(8,128)(2,1)S(1)}, bf16[2048,256]{1,0:T(8,128)(2,1)}, u32[]{:S(2)}, u32[]{:S(2)}) collective-permute-start(bf16[2048,256]{1,0:T(8,128)(2,1)S(1)} %copy-done.7), channel_id=1, source_target_pairs={{0,32},{32,0},{1,33},{33,1},{2,34},{34,2},{3,35},{35,3},{4,36},{36... | collective-permute-start | bytes 3145736 | tf_op jit(solution)/shard_map/ppermute | solution.py:25
  306.1 6.8 %collective-permute-start.15 = (bf16[32,128]{1,0:T(8,128)(2,1)S(1)}, bf16[32,128]{1,0:T(8,128)(2,1)S(1)}, u32[]{:S(2)}, u32[]{:S(2)}) collective-permute-start(bf16[32,128]{1,0:T(8,128)(2,1)S(1)} %get-tuple-element.72), channel_id=1, source_target_pairs={{0,2},{1,3},{2,0},{3,1},{4,6},{5,7},{6,4},{7,5},{8,10},{9,11},{10,... | collective-permute-start | bytes 24584 | tf_op jit(solution)/shard_map/ppermute | solution.py:149
  310.8 5.6 %collective-permute-start.16 = (bf16[32,128]{1,0:T(8,128)(2,1)S(1)}, bf16[32,128]{1,0:T(8,128)(2,1)S(1)}, u32[]{:S(2)}, u32[]{:S(2)}) collective-permute-start(bf16[32,128]{1,0:T(8,128)(2,1)S(1)} %get-tuple-element.71), channel_id=1, source_target_pairs={{0,1},{1,2},{2,3},{3,0},{4,5},{5,6},{6,7},{7,4},{8,9},{9,10},{10,1... | collective-permute-start | bytes 24584 | tf_op jit(solution)/shard_map/ppermute | solution.py:149
Sparse Core Ops, SparseCore 0:
  13.4 80.4 all-gather.2
  212.0 80.5 all-gather.4

commit v3 on v2

v3 whole, which is shorter than its diff:
```python
import functools

import jax
import jax.numpy as jnp
from jax import lax
from jax.experimental import pallas as pl
from jax.experimental.pallas import tpu as pltpu
from jax.sharding import Mesh, PartitionSpec as P

HD = 128
EPSILON = 1e-05
CAP = 12
FOLD = 4
ROOM = 16
UNITS = 256
MIB = 2**20

CONTRACT = (((1,), (1,)), ((), ()))


def across(left, right):
    return lax.dot_general(left, right, CONTRACT, preferred_element_type=jnp.float32)


def two_terms(full):
    high = full.astype(jnp.bfloat16)
    return high, (full - high.astype(jnp.float32)).astype(jnp.bfloat16)


def expert_kernel(bit_ref, rows_ref, w_ref, stay_ref, leave_ref, back_ref):
    step = pl.program_id(0)
    shards, _, width = rows_ref.shape
    part = width // FOLD
    ins = rows_ref[:, :ROOM, :].reshape(shards * ROOM, width)
    grads = rows_ref[:, ROOM:, :].reshape(shards * ROOM, width)
    gate_val = across(ins, w_ref[0, 0])
    up_val = across(ins, w_ref[0, 1])
    hidden_grad = across(grads, w_ref[0, 2])
    sigma = jax.nn.sigmoid(gate_val)
    gate_grad = (hidden_grad * up_val * sigma * (1.0 + gate_val * (1.0 - sigma))).astype(jnp.bfloat16)
    up_grad = (hidden_grad * gate_val * sigma).astype(jnp.bfloat16)
    for q in range(FOLD):
        at = slice(q * part, (q + 1) * part)
        piece = jnp.dot(gate_grad, w_ref[0, 0, :, at], preferred_element_type=jnp.float32)
        piece = piece + jnp.dot(up_grad, w_ref[0, 1, :, at], preferred_element_type=jnp.float32)
        piece = piece.reshape(shards, ROOM, part)

        @pl.when(step == 0)
        def _():
            back_ref[:, :, at] = piece

        @pl.when(step == 1)
        def _():
            back_ref[:, :, at] += piece

    @pl.when(step == 1)
    def _():
        bit = bit_ref[0]

        def folded(shard):
            block = back_ref[shard]
            return jnp.concatenate([block[:CAP, q * part : (q + 1) * part] for q in range(FOLD)], axis=0)

        for k in range(shards // 2):
            stay_ref[k] = folded(2 * k + bit)
            leave_ref[k] = folded(2 * k + 1 - bit).astype(jnp.bfloat16)


def expert_block(bit, rows, weights):
    shards, depth, width = rows.shape
    out = (shards // 2, FOLD * CAP, width // FOLD)
    return pl.pallas_call(
        expert_kernel,
        grid=(2,),
        in_specs=[
            pl.BlockSpec(memory_space=pltpu.SMEM),
            pl.BlockSpec((shards, depth, width), lambda i: (0, 0, 0)),
            pl.BlockSpec((1, 3, UNITS, width), lambda i: (i, 0, 0, 0)),
        ],
        out_specs=[pl.BlockSpec(out, lambda i: (0, 0, 0))] * 2,
        out_shape=[
            jax.ShapeDtypeStruct(out, jnp.float32),
            jax.ShapeDtypeStruct(out, jnp.bfloat16),
        ],
        scratch_shapes=[pltpu.VMEM((shards, ROOM, width), jnp.float32)],
        compiler_params=pltpu.CompilerParams(vmem_limit_bytes=48 * MIB),
        cost_estimate=pl.CostEstimate(
            flops=2 * 5 * shards * ROOM * 2 * UNITS * width,
            bytes_accessed=2 * weights.size + 2 * rows.size,
            transcendentals=0,
        ),
        name="expert_block",
    )(bit, rows, weights)


def early_kernel(scale, query_ref, key_ref, value_ref, qpos_ref, kpos_ref, prob_ref, out_ref):
    allowed = kpos_ref[...] <= qpos_ref[...]
    scores = jnp.where(allowed, across(query_ref[...], key_ref[...]) * scale, -1e30)
    row_max = jnp.max(scores, axis=-1, keepdims=True)
    expo_vals = jnp.where(allowed, jnp.exp(scores - row_max), 0.0)
    probs = expo_vals / jnp.sum(expo_vals, axis=-1, keepdims=True)
    prob_ref[...] = probs
    high, low = two_terms(probs)
    values = value_ref[...]
    out_ref[...] = jnp.dot(high, values, preferred_element_type=jnp.float32) + jnp.dot(
        low, values, preferred_element_type=jnp.float32
    )


def late_kernel(scale, grad_ref, key_ref, value_ref, prob_ref, out_ref, back_ref):
    grads = grad_ref[...]
    delta = jnp.sum(grads.astype(jnp.float32) * out_ref[...], axis=-1, keepdims=True)
    mixed = prob_ref[...] * (across(grads, value_ref[...]) - delta)
    high, low = two_terms(mixed)
    keys = key_ref[...]
    total = jnp.dot(high, keys, preferred_element_type=jnp.float32) + jnp.dot(
        low, keys, preferred_element_type=jnp.float32
    )
    back_ref[...] = (scale * total).astype(jnp.bfloat16)


def in_vmem(kernel, out_shape, name, flops, *args):
    return pl.pallas_call(
        kernel,
        in_specs=[pl.BlockSpec(memory_space=pltpu.VMEM)] * len(args),
        out_specs=jax.tree.map(lambda _: pl.BlockSpec(memory_space=pltpu.VMEM), out_shape),
        out_shape=out_shape,
        compiler_params=pltpu.CompilerParams(vmem_limit_bytes=32 * MIB),
        cost_estimate=pl.CostEstimate(flops=flops, bytes_accessed=4 * MIB, transcendentals=0),
        name=name,
    )(*args)


def core_swap(block):
    return lax.ppermute(block, "core", [(0, 1), (1, 0)])


def norm_back(resid_full, inv_rms, grad_rows, norm_gain, expert_grad):
    scaled_grad = norm_gain.astype(jnp.float32) * expert_grad
    cubed = inv_rms * inv_rms * inv_rms
    mean_term = jnp.mean(scaled_grad * resid_full, axis=-1, keepdims=True)
    return (grad_rows + inv_rms * scaled_grad - resid_full * cubed * mean_term).astype(jnp.bfloat16)


def per_device(
    resid,
    grad_out,
    norm_gain,
    expert_ids,
    route_weights,
    w_gate,
    w_up,
    w_down,
    w_out,
    queries,
    keys,
    values,
):
    f32, bf16 = jnp.float32, jnp.bfloat16
    tok_rows, width = resid.shape
    z_count, exp_count, head_count = (lax.axis_size(a) for a in ("z", "exp", "head"))
    z_index, core_index = lax.axis_index("z"), lax.axis_index("core")
    exp_index, head_index = lax.axis_index("exp"), lax.axis_index("head")
    quarter = tok_rows // head_count
    row_first = head_index * quarter
    resid_part = lax.dynamic_slice_in_dim(resid, row_first, quarter, 0)
    grad_part = lax.dynamic_slice_in_dim(grad_out, row_first, quarter, 0)
    ids_part = lax.dynamic_slice_in_dim(expert_ids, row_first, quarter, 0)
    weights_part = lax.dynamic_slice_in_dim(route_weights, row_first, quarter, 0)
    resid_full = resid_part.astype(f32)
    inv_rms = lax.rsqrt(jnp.mean(resid_full * resid_full, axis=-1, keepdims=True) + EPSILON)
    normed = (resid_full * inv_rms * norm_gain.astype(f32)).astype(bf16)
    grad_full = grad_part.astype(f32)

    row_ids = jnp.arange(quarter, dtype=jnp.int32)
    earlier = row_ids[:, None] < row_ids[None, :]

    def slots_of(expert):
        matched = ids_part == expert
        routed = jnp.any(matched, axis=1)
        position = jnp.sum((earlier & routed[:, None]).astype(jnp.int32), axis=0)
        weight = jnp.sum(jnp.where(matched, weights_part, 0.0), axis=1)
        return routed, position, weight

    routed, position, weight = slots_of(exp_index)
    slot_ids = jnp.arange(ROOM, dtype=jnp.int32)
    select = ((position[None, :] == slot_ids[:CAP, None]) & routed[None, :]).astype(bf16)
    scaled = (weight[:, None] * grad_full).astype(bf16)
    slot_in = jnp.dot(select, normed, preferred_element_type=f32).astype(bf16)
    slot_grad = jnp.dot(select, scaled, preferred_element_type=f32).astype(bf16)
    spare = ROOM - CAP
    mine = jnp.concatenate(
        [slot_in, keys.reshape(spare, -1), slot_grad, values.reshape(spare, -1)], axis=0
    )

    rows = lax.all_gather(mine, "z", axis=0, tiled=True).reshape(z_count, 2 * ROOM, width)
    gate_mat, up_mat, down_mat, w_mine, mine = lax.optimization_barrier(
        (w_gate[0].T, w_up[0].T, w_down[0], w_out, mine)
    )
    fill = ((0, UNITS - gate_mat.shape[0]), (0, 0))
    own = jnp.stack([jnp.pad(w, fill) for w in (gate_mat, up_mat, down_mat)], axis=0)
    weights = jnp.stack([own, core_swap(own)], axis=0)
    w_near = [w_mine] + [
        lax.ppermute(w_mine, "head", [(a, (a - d) % head_count) for a in range(head_count)])
        for d in range(1, head_count)
    ]
    w_four = jnp.concatenate(w_near, axis=0)
    weights, w_four = lax.optimization_barrier((weights, w_four))

    packed = rows.reshape(z_count, 2, ROOM, width)[:, :, CAP:]
    packed = jnp.stack([packed, core_swap(packed)], axis=0)
    key_all = packed[:, :, 0].reshape(-1, HD)
    value_all = packed[:, :, 1].reshape(-1, HD)
    query_pos = (z_index * 2 + core_index) * tok_rows + jnp.arange(tok_rows, dtype=jnp.int32)
    place = jnp.arange(2 * z_count * tok_rows, dtype=jnp.int32)
    half = z_count * tok_rows
    shard = (place % half) // tok_rows * 2 + (core_index + place // half) % 2
    key_pos = shard * tok_rows + place % tok_rows
    scale = HD ** (-0.5)
    attn_flops = 2 * tok_rows * HD * 2 * half
    probs, output = in_vmem(
        functools.partial(early_kernel, scale),
        [
            jax.ShapeDtypeStruct((tok_rows, 2 * half), f32),
            jax.ShapeDtypeStruct((tok_rows, HD), f32),
        ],
        "attention_early",
        3 * attn_flops,
        queries,
        key_all,
        value_all,
        query_pos[:, None],
        key_pos[None, :],
    )

    bit = z_index % 2
    stay, leave = expert_block(bit.reshape(1), rows, weights)
    up = [(2 * a, 2 * ((a + 1) % z_count)) for a in range(z_count)]
    down = [(2 * a + 1, 2 * ((a - 1) % z_count) + 1) for a in range(z_count)]
    came = lax.ppermute(leave, ("z", "core"), up + down)
    left = (stay + came.astype(f32)).astype(bf16)
    same = [list(range(r, z_count, 2)) for r in range(2)]
    left = lax.all_to_all(left, "z", 0, 0, tiled=True, axis_index_groups=same)
    slots = jnp.sum(left.astype(f32), axis=0).astype(bf16)
    slots = lax.all_to_all(
        jnp.broadcast_to(slots[None], (exp_count, *slots.shape)), "exp", 0, 0, tiled=True
    )
    picks = []
    for expert in range(exp_count):
        routed, position, _ = slots_of(expert)
        picks.append((position[:, None] == slot_ids[None, :CAP]) & routed[:, None])
    picks = jnp.stack(picks, axis=1).astype(bf16)
    flat = slots.reshape(exp_count * FOLD * CAP, -1)
    pieces = []
    for q in range(FOLD):
        there = jnp.zeros((quarter, exp_count, FOLD, CAP), bf16).at[:, :, q].set(picks)
        pieces.append(jnp.dot(there.reshape(quarter, -1), flat, preferred_element_type=f32))
    summed = jnp.concatenate(pieces, axis=1)
    grad_quarter = norm_back(resid_full, inv_rms, grad_full, norm_gain, summed)

    at_heads = lax.dot_general(grad_quarter, w_four, CONTRACT, preferred_element_type=f32)
    at_heads = at_heads.astype(bf16).reshape(quarter, head_count, HD).transpose(1, 0, 2)
    at_heads = jnp.roll(at_heads, head_index, axis=0)
    attn_grad = lax.all_to_all(at_heads, "head", 0, 0, tiled=True).reshape(tok_rows, HD)
    query_grad = in_vmem(
        functools.partial(late_kernel, scale),
        jax.ShapeDtypeStruct((tok_rows, HD), bf16),
        "attention_late",
        3 * attn_flops,
        attn_grad,
        key_all,
        value_all,
        probs,
        output,
    )
    return (grad_quarter, query_grad)


def solution(mesh):
    seq, exp, head = mesh.shape["seq"], mesh.shape["exp"], mesh.shape["head"]
    fine = Mesh(mesh.devices.reshape(seq // 2, 2, exp, head), ("z", "core", "exp", "head"))
    seq_axes = ("z", "core")
    in_specs = (
        P(seq_axes, None),
        P(seq_axes, None),
        P(),
        P(seq_axes, None),
        P(seq_axes, None),
        P("exp", None, seq_axes),
        P("exp", None, seq_axes),
        P("exp", seq_axes, None),
        P(("exp", "head"), None),
        P(seq_axes, ("exp", "head")),
        P(seq_axes, ("exp", "head")),
        P(seq_axes, ("exp", "head")),
    )
    out_specs = (P(("z", "core", "head"), None), P(seq_axes, ("exp", "head")))
    return jax.shard_map(
        per_device, mesh=fine, in_specs=in_specs, out_specs=out_specs, check_vma=False
    )
```

time: 334 us -> 237 us (0.71)
  the two profiles are of different devices: /device:TPU:1 before, /device:TPU:64 now
where the time goes in v3:
time: 237 us; the launch traced here: 236 us
  waiting for transfers between devices  122 us (51%)
  starting transfers between devices  32.7 us (14%)
  other arithmetic  29.2 us (12%)
  Pallas kernels  17.3 us (7%)
  local copies, waits for them, and re-layouts  15 us (6%)
  between operations  14.4 us (6%)
  matrix products  4.79 us (2%)
    ppermute x3, waiting for transfers between devices, per_device(): lax.ppermute(w_mine, 'head', [(a, (a - d) % head_count) for a in range(he...  45.7 us
    all_to_all x1, waiting for transfers between devices, per_device(): left = lax.all_to_all(left, 'z', 0, 0, tiled=True, axis_index_groups=same)  36.2 us
    all_to_all x1, waiting for transfers between devices, per_device(): lax.all_to_all(jnp.broadcast_to(slots[None], (exp_count, *slots.shape)),...  14.8 us
    pallas_call x1, Pallas kernels, expert_block(): pl.pallas_call(expert_kernel, grid=(2,), in_specs=[pl.BlockSpec(memory_sp...  13.8 us
    another operation x2, other arithmetic, per_device(): weights = jnp.stack([own, core_swap(own)], axis=0)  13.3 us
    all_gather x1, waiting for transfers between devices, per_device(): lax.all_gather(mine, 'z', axis=0, tiled=True)  12.4 us
    ppermute x1, waiting for transfers between devices, per_device(): came = lax.ppermute(leave, ('z', 'core'), up + down)  11.1 us
    ppermute x3, starting transfers between devices, per_device(): lax.ppermute(w_mine, 'head', [(a, (a - d) % head_count) for a in range(he...  10.2 us
  transfers between devices with their start and end apart: 10, of which 7 were waited for; matrix products, arithmetic and copies ran while one was open for 13% of the time, Pallas kernels for 1%

profile of v3, /device:TPU:64, one launch (start us, length us, event | category | flops | bytes accessed | tf_op | source)
XLA Modules:
  0.0 235.7 jit_solution(3131072073542057281)
XLA Ops:
  7.2 0.8 fusion.40
  8.1 1.1 fusion.5
  9.3 0.7 convert_element_type.81
  10.0 0.8 reshape.883
  10.7 0.8 reshape.884
  11.5 1.2 convolution_convert_fusion
  12.7 1.2 convolution_convert_fusion.1
  13.9 0.8 pad_maximum_fusion.4
  14.8 2.4 %pad_bitcast_fusion = (bf16[1,256,4096]{2,1,0:T(8,128)(2,1)S(1)}, bf16[1,256,4096]{2,1,0:T(8,128)(2,1)S(1)}) fusion(bf16[200,4096]{1,0:T(8,128)(2,1)} %bitcast.78, bf16[200,4096]{1,0:T(8,128)(2,1)} %bitcast.79), kind=kLoop, calls=%fused_computation.7 | loop fusion | bytes 7471104 | tf_op jit(solution)/shard_map/stack | solution.py:201
  17.4 4.9 %fusion.42 = (bf16[1,3,256,4096]{3,2,1,0:T(8,128)(2,1)}, bf16[3,256,4096]{2,1,0:T(8,128)(2,1)}) fusion(bf16[1,256,4096]{2,1,0:T(8,128)(2,1)S(1)} %get-tuple-element.101, bf16[1,256,4096]{2,1,0:T(8,128)(2,1)S(1)} %get-tuple-element.102, bf16[1,256,4096]{2,1,0:T(8,128)(2,1)S(1)} %pad_bitcast_fusion.2), kind=kLoop, calls=%fused_computation.111 | loop fusion | flops 6291456 | bytes 18874368 | tf_op jit(solution)/shard_map/stack | solution.py:202
  22.3 1.9 collective-permute-start
  24.2 4.7 %collective-permute-start.1 = (bf16[128,4096]{1,0:T(8,128)(2,1)S(1)}, bf16[128,4096]{1,0:T(8,128)(2,1)S(1)}, u32[]{:S(2)}, u32[]{:S(2)}) collective-permute-start(bf16[128,4096]{1,0:T(8,128)(2,1)S(1)} %copy-done.7), channel_id=1, source_target_pairs={{0,3},{1,0},{2,1},{3,2},{4,7},{5,4},{6,5},{7,6},{8,11},{9,8},{10,9... | collective-permute-start | bytes 3145736 | tf_op jit(solution)/shard_map/ppermute | solution.py:204
  28.9 2.7 %collective-permute-start.2 = (bf16[128,4096]{1,0:T(8,128)(2,1)S(1)}, bf16[128,4096]{1,0:T(8,128)(2,1)S(1)}, u32[]{:S(2)}, u32[]{:S(2)}) collective-permute-start(bf16[128,4096]{1,0:T(8,128)(2,1)S(1)} %copy-done.7), channel_id=1, source_target_pairs={{0,2},{1,3},{2,0},{3,1},{4,6},{5,7},{6,4},{7,5},{8,10},{9,11},{10,... | collective-permute-start | bytes 3145736 | tf_op jit(solution)/shard_map/ppermute | solution.py:204
  31.6 2.8 %collective-permute-start.3 = (bf16[128,4096]{1,0:T(8,128)(2,1)S(1)}, bf16[128,4096]{1,0:T(8,128)(2,1)}, u32[]{:S(2)}, u32[]{:S(2)}) collective-permute-start(bf16[128,4096]{1,0:T(8,128)(2,1)S(1)} %copy-done.7), channel_id=1, source_target_pairs={{0,1},{1,2},{2,3},{3,0},{4,5},{5,6},{6,7},{7,4},{8,9},{9,10},{10,1... | collective-permute-start | bytes 3145736 | tf_op jit(solution)/shard_map/ppermute | solution.py:204
  34.4 40.0 %collective-permute-done.1 = bf16[128,4096]{1,0:T(8,128)(2,1)S(1)} collective-permute-done((bf16[128,4096]{1,0:T(8,128)(2,1)S(1)}, bf16[128,4096]{1,0:T(8,128)(2,1)S(1)}, u32[]{:S(2)}, u32[]{:S(2)}) %collective-permute-start.1) | collective-permute-done | bytes 1048608 | tf_op jit(solution)/shard_map/ppermute | solution.py:204
  74.4 5.7 %collective-permute-done.3 = bf16[128,4096]{1,0:T(8,128)(2,1)} collective-permute-done((bf16[128,4096]{1,0:T(8,128)(2,1)S(1)}, bf16[128,4096]{1,0:T(8,128)(2,1)}, u32[]{:S(2)}, u32[]{:S(2)}) %collective-permute-start.3) | collective-permute-done | bytes 1048608 | tf_op jit(solution)/shard_map/ppermute | solution.py:204
  80.1 3.2 %pad_maximum_fusion.2 = bf16[512,4096]{1,0:T(8,128)(2,1)} fusion(bf16[128,4096]{1,0:T(8,128)(2,1)} %collective-permute-done.3, bf16[128,4096]{1,0:T(8,128)(2,1)S(1)} %collective-permute-done.2, bf16[128,4096]{1,0:T(8,128)(2,1)S(1)} %collective-permute-done.1, bf16[128,4096]{1,0:T(8,128)(2,1)S(1)} %copy-done.7), kind=kLoop, calls=%fused_computation.4 | loop fusion | flops 16777216 | bytes 8388608 | tf_op jit(solution)/shard_map/concatenate | solution.py:207
  83.4 8.4 %pad_maximum_fusion.w_ref = bf16[2,3,256,4096]{3,2,1,0:T(8,128)(2,1)} fusion(bf16[1,3,256,4096]{3,2,1,0:T(8,128)(2,1)} %bitcast.19, bf16[1,3,256,4096]{3,2,1,0:T(8,128)(2,1)S(1)} %copy-done.3), kind=kLoop, calls=%fused_computation | loop fusion | flops 6291456 | bytes 25165824 | tf_op jit(solution)/shard_map/stack | solution.py:202
  91.7 12.4 %all-gather.2.cloned.1.call-done = bf16[512,4096]{1,0:T(8,128)(2,1)} async-done(((bf16[32,4096]{1,0:T(8,128)(2,1)}), bf16[512,4096]{1,0:T(8,128)(2,1)}) %all-gather.2.cloned.1.call-update) | async-done | bytes 4194320 | tf_op jit(solution)/shard_map/all_gather | solution.py:196
  104.1 13.8 %expert_block.1 = (f32[8,48,1024]{2,1,0:T(8,128)S(1)}, bf16[8,48,1024]{2,1,0:T(8,128)(2,1)S(1)}) custom-call(s32[1]{0:T(128)} %bitcast.8.bit_ref, bf16[16,32,4096]{2,1,0:T(8,128)(2,1)} %bitcast.81, bf16[2,3,256,4096]{3,2,1,0:T(8,128)(2,1)} %pad_maximum_fusion.w_ref), custom_call_target="tpu_custom_call" | custom-call | flops 5368709120 | bytes 16777216 | tf_op jit(solution)/shard_map/expert_block/pallas_call | solution.py:72
  118.0 2.5 %collective-permute-start.4 = (bf16[8,48,1024]{2,1,0:T(8,128)(2,1)S(1)}, bf16[8,48,1024]{2,1,0:T(8,128)(2,1)S(1)}, u32[]{:S(2)}, u32[]{:S(2)}) collective-permute-start(bf16[8,48,1024]{2,1,0:T(8,128)(2,1)S(1)} %get-tuple-element.66), channel_id=1, source_target_pairs={{0,64},{64,128},{128,192},{192,256},{256,320},{320,384},{384,448},... | collective-permute-start | bytes 2359304 | tf_op jit(solution)/shard_map/ppermute | solution.py:240
  120.7 11.1 %collective-permute-done.4 = bf16[8,48,1024]{2,1,0:T(8,128)(2,1)S(1)} collective-permute-done((bf16[8,48,1024]{2,1,0:T(8,128)(2,1)S(1)}, bf16[8,48,1024]{2,1,0:T(8,128)(2,1)S(1)}, u32[]{:S(2)}, u32[]{:S(2)}) %collective-permute-start.4) | collective-permute-done | bytes 786464 | tf_op jit(solution)/shard_map/ppermute | solution.py:240
  131.9 1.2 add_convert_fusion
  133.0 6.6 %all-to-all-start = ((bf16[8,48,1024]{2,1,0:T(8,128)(2,1)}), bf16[8,48,1024]{2,1,0:T(8,128)(2,1)S(1)}, u32[]{:S(2)}, u32[]{:S(2)}) async-start(bf16[8,48,1024]{2,1,0:T(8,128)(2,1)} %add_convert_fusion), calls=%async_computation | async-start | bytes 1572864 | tf_op jit(solution)/shard_map/all_to_all | solution.py:243
  140.3 2.7 %fusion.43 = (bf16[16,2,4,4096]{3,2,0,1:T(4,128)(2,1)S(1)}, bf16[1,16,2,4,4096]{4,3,1,0,2:T(4,128)(2,1)S(1)}) fusion(bf16[16,2,16,4096]{3,2,1,0:T(8,128)(2,1)} %bitcast.82), kind=kLoop, calls=%fused_computation.112 | loop fusion | bytes 3145728
  143.0 1.9 collective-permute-start.5
  145.0 36.2 %all-to-all-done = bf16[8,48,1024]{2,1,0:T(8,128)(2,1)S(1)} async-done(((bf16[8,48,1024]{2,1,0:T(8,128)(2,1)}), bf16[8,48,1024]{2,1,0:T(8,128)(2,1)S(1)}, u32[]{:S(2)}, u32[]{:S(2)}) %all-to-all-start) | async-done | bytes 786464 | tf_op jit(solution)/shard_map/all_to_all | solution.py:243
  181.3 1.0 broadcast_in_dim.7
  182.3 6.2 %all-to-all-start.1 = ((bf16[8,48,1024]{2,1,0:T(8,128)(2,1)}), bf16[8,48,1024]{2,1,0:T(8,128)(2,1)S(1)}, u32[]{:S(2)}, u32[]{:S(2)}) async-start(bf16[8,48,1024]{2,1,0:T(8,128)(2,1)} %broadcast_in_dim.7), calls=%async_computation.1 | async-start | bytes 1572864 | tf_op jit(solution)/shard_map/all_to_all | solution.py:245
  188.7 0.7 reshape.881
  189.7 3.5 %pad_maximum_fusion.3 = (bf16[2,16,1,4,4096]{4,3,1,0,2:T(4,128)(2,1)}, bf16[2,16,1,4,4096]{4,3,1,0,2:T(4,128)(2,1)S(1)}) fusion(bf16[1,16,2,4,4096]{4,3,1,0,2:T(4,128)(2,1)} %bitcast.26, bf16[1,16,2,4,4096]{4,3,1,0,2:T(4,128)(2,1)S(1)} %get-tuple-element.86), kind=kLoop, calls=%fused_computation.14 | loop fusion | flops 1048576 | bytes 4194304 | tf_op jit(solution)/shard_map/stack | solution.py:211
  193.2 1.1 reshape_squeeze.6.key_ref
  194.3 2.2 reshape_squeeze.7.value_ref
  196.5 14.8 %all-to-all-done.1 = bf16[8,48,1024]{2,1,0:T(8,128)(2,1)S(1)} async-done(((bf16[8,48,1024]{2,1,0:T(8,128)(2,1)}), bf16[8,48,1024]{2,1,0:T(8,128)(2,1)S(1)}, u32[]{:S(2)}, u32[]{:S(2)}) %all-to-all-start.1) | async-done | bytes 786464 | tf_op jit(solution)/shard_map/all_to_all | solution.py:245
  211.2 0.3 fusion.45
  211.5 0.3 fusion.46
  211.8 0.3 fusion.47
  212.0 0.3 fusion.48
  212.3 1.3 fusion.9
  213.6 1.2 fusion.4
  214.9 1.4 fusion
  216.3 0.7 fusion.17
  216.9 3.3 %all-to-all-start.2 = ((bf16[4,32,128]{2,1,0:T(8,128)(2,1)}), bf16[4,32,128]{2,1,0:T(8,128)(2,1)S(1)}, u32[]{:S(2)}, u32[]{:S(2)}) async-start(bf16[4,32,128]{2,1,0:T(8,128)(2,1)} %fusion.17), calls=%async_computation.2 | async-start | bytes 65536 | tf_op jit(solution)/shard_map/all_to_all | solution.py:264
  220.2 1.8 attention_early.1
  222.1 1.3 copy-done
  223.4 2.2 all-to-all-done.2
  225.6 1.6 copy-done.1
  227.2 1.7 attention_late.1
  (48 shorter events, 2.0 us)
Async XLA Ops:
  7.2 97.0 %all-gather.2.cloned.1.call-start = ((), (), s32[]{:S(2)}) async-start(), calls=%async_computation.3 | async-start | bytes 4456448 | tf_op jit(solution)/shard_map/all_gather | solution.py:196
  13.9 3.2 %copy-start.5 = (bf16[1,4096,200]{1,2,0:T(8,128)(2,1)S(1)}, bf16[1,4096,200]{1,2,0:T(8,128)(2,1)}, u32[]{:S(2)}) copy-start(bf16[1,4096,200]{1,2,0:T(8,128)(2,1)} %param.25) | copy-start | bytes 4915204
  17.4 6.8 %copy-start.7 = (bf16[128,4096]{1,0:T(8,128)(2,1)S(1)}, bf16[128,4096]{1,0:T(8,128)(2,1)}, u32[]{:S(2)}) copy-start(bf16[128,4096]{1,0:T(8,128)(2,1)} %param.28) | copy-start | bytes 3145732
  22.3 61.1 %collective-permute-start = (bf16[3,256,4096]{2,1,0:T(8,128)(2,1)}, bf16[3,256,4096]{2,1,0:T(8,128)(2,1)}, u32[]{:S(2)}, u32[]{:S(2)}) collective-permute-start(bf16[3,256,4096]{2,1,0:T(8,128)(2,1)} %get-tuple-element.82), channel_id=1, source_target_pairs={{0,32},{32,0},{1,33},{33,1},{2,34},{34,2},{3,35},{35,3},{4,36},{36... | collective-permute-start | bytes 18874376 | tf_op jit(solution)/shard_map/ppermute | solution.py:135
  24.2 50.2 %collective-permute-start.1 = (bf16[128,4096]{1,0:T(8,128)(2,1)S(1)}, bf16[128,4096]{1,0:T(8,128)(2,1)S(1)}, u32[]{:S(2)}, u32[]{:S(2)}) collective-permute-start(bf16[128,4096]{1,0:T(8,128)(2,1)S(1)} %copy-done.7), channel_id=1, source_target_pairs={{0,3},{1,0},{2,1},{3,2},{4,7},{5,4},{6,5},{7,6},{8,11},{9,8},{10,9... | collective-permute-start | bytes 3145736 | tf_op jit(solution)/shard_map/ppermute | solution.py:204
  28.9 45.6 %collective-permute-start.2 = (bf16[128,4096]{1,0:T(8,128)(2,1)S(1)}, bf16[128,4096]{1,0:T(8,128)(2,1)S(1)}, u32[]{:S(2)}, u32[]{:S(2)}) collective-permute-start(bf16[128,4096]{1,0:T(8,128)(2,1)S(1)} %copy-done.7), channel_id=1, source_target_pairs={{0,2},{1,3},{2,0},{3,1},{4,6},{5,7},{6,4},{7,5},{8,10},{9,11},{10,... | collective-permute-start | bytes 3145736 | tf_op jit(solution)/shard_map/ppermute | solution.py:204
  31.6 48.5 %collective-permute-start.3 = (bf16[128,4096]{1,0:T(8,128)(2,1)S(1)}, bf16[128,4096]{1,0:T(8,128)(2,1)}, u32[]{:S(2)}, u32[]{:S(2)}) collective-permute-start(bf16[128,4096]{1,0:T(8,128)(2,1)S(1)} %copy-done.7), channel_id=1, source_target_pairs={{0,1},{1,2},{2,3},{3,0},{4,5},{5,6},{6,7},{7,4},{8,9},{9,10},{10,1... | collective-permute-start | bytes 3145736 | tf_op jit(solution)/shard_map/ppermute | solution.py:204
  34.4 49.0 %copy-start.3 = (bf16[1,3,256,4096]{3,2,1,0:T(8,128)(2,1)S(1)}, bf16[1,3,256,4096]{3,2,1,0:T(8,128)(2,1)}, u32[]{:S(2)}) copy-start(bf16[1,3,256,4096]{3,2,1,0:T(8,128)(2,1)} %get-tuple-element.81) | copy-start | bytes 18874372
  118.0 13.9 %collective-permute-start.4 = (bf16[8,48,1024]{2,1,0:T(8,128)(2,1)S(1)}, bf16[8,48,1024]{2,1,0:T(8,128)(2,1)S(1)}, u32[]{:S(2)}, u32[]{:S(2)}) collective-permute-start(bf16[8,48,1024]{2,1,0:T(8,128)(2,1)S(1)} %get-tuple-element.66), channel_id=1, source_target_pairs={{0,64},{64,128},{128,192},{192,256},{256,320},{320,384},{384,448},... | collective-permute-start | bytes 2359304 | tf_op jit(solution)/shard_map/ppermute | solution.py:240
  133.0 48.1 %all-to-all-start = ((bf16[8,48,1024]{2,1,0:T(8,128)(2,1)}), bf16[8,48,1024]{2,1,0:T(8,128)(2,1)S(1)}, u32[]{:S(2)}, u32[]{:S(2)}) async-start(bf16[8,48,1024]{2,1,0:T(8,128)(2,1)} %add_convert_fusion), calls=%async_computation | async-start | bytes 1572864 | tf_op jit(solution)/shard_map/all_to_all | solution.py:243
  143.0 46.7 %collective-permute-start.5 = (bf16[16,2,4,4096]{3,2,0,1:T(4,128)(2,1)S(1)}, bf16[16,2,4,4096]{3,2,0,1:T(4,128)(2,1)}, u32[]{:S(2)}, u32[]{:S(2)}) collective-permute-start(bf16[16,2,4,4096]{3,2,0,1:T(4,128)(2,1)S(1)} %get-tuple-element.85), channel_id=1, source_target_pairs={{0,32},{32,0},{1,33},{33,1},{2,34},{34,2},{3,35},{35,3},{4,36},{36... | collective-permute-start | bytes 3145736 | tf_op jit(solution)/shard_map/ppermute | solution.py:135
  182.3 28.9 %all-to-all-start.1 = ((bf16[8,48,1024]{2,1,0:T(8,128)(2,1)}), bf16[8,48,1024]{2,1,0:T(8,128)(2,1)S(1)}, u32[]{:S(2)}, u32[]{:S(2)}) async-start(bf16[8,48,1024]{2,1,0:T(8,128)(2,1)} %broadcast_in_dim.7), calls=%async_computation.1 | async-start | bytes 1572864 | tf_op jit(solution)/shard_map/all_to_all | solution.py:245
  189.7 21.5 %copy-start.8 = (bf16[32,384]{0,1:T(8,128)(2,1)S(1)}, bf16[32,384]{0,1:T(8,128)(2,1)}, u32[]{:S(2)}) copy-start(bf16[32,384]{0,1:T(8,128)(2,1)} %reshape.881) | copy-start | bytes 73732
  211.2 3.7 %copy-start.4 = (bf16[512,4096]{1,0:T(8,128)(2,1)S(1)}, bf16[512,4096]{1,0:T(8,128)(2,1)}, u32[]{:S(2)}) copy-start(bf16[512,4096]{1,0:T(8,128)(2,1)} %pad_maximum_fusion.2) | copy-start | bytes 12582916
  211.8 8.5 %copy-start.2 = (bf16[128,128]{1,0:T(8,128)(2,1)S(1)}, bf16[128,128]{1,0:T(8,128)(2,1)}, u32[]{:S(2)}) copy-start(bf16[128,128]{1,0:T(8,128)(2,1)} %query_ref.1) | copy-start | bytes 98308
  214.9 14.0 %copy-start.6 = (bf16[32,4096]{1,0:T(8,128)(2,1)}, bf16[32,4096]{1,0:T(8,128)(2,1)S(1)}, u32[]{:S(2)}) copy-start(bf16[32,4096]{1,0:T(8,128)(2,1)S(1)} %fusion.4) | copy-start | bytes 786436
  216.9 8.7 %all-to-all-start.2 = ((bf16[4,32,128]{2,1,0:T(8,128)(2,1)}), bf16[4,32,128]{2,1,0:T(8,128)(2,1)S(1)}, u32[]{:S(2)}, u32[]{:S(2)}) async-start(bf16[4,32,128]{2,1,0:T(8,128)(2,1)} %fusion.17), calls=%async_computation.2 | async-start | bytes 65536 | tf_op jit(solution)/shard_map/all_to_all | solution.py:264
  222.1 1.4 copy-start
  225.6 1.6 copy-start.1
Sparse Core Ops, SparseCore 0:
  14.9 89.1 all-gather.1

commit v4 on v3

--- a/solution.py
+++ b/solution.py
@@ -27,70 +27,111 @@
     return high, (full - high.astype(jnp.float32)).astype(jnp.bfloat16)
 
 
-def expert_kernel(bit_ref, rows_ref, w_ref, stay_ref, leave_ref, back_ref):
-    step = pl.program_id(0)
+def expert_kernel(rows_hbm, own_hbm, other_hbm, out_ref, rows_ref, w_ref, back_ref, sems):
     shards, _, width = rows_ref.shape
     part = width // FOLD
-    ins = rows_ref[:, :ROOM, :].reshape(shards * ROOM, width)
-    grads = rows_ref[:, ROOM:, :].reshape(shards * ROOM, width)
-    gate_val = across(ins, w_ref[0, 0])
-    up_val = across(ins, w_ref[0, 1])
-    hidden_grad = across(grads, w_ref[0, 2])
-    sigma = jax.nn.sigmoid(gate_val)
-    gate_grad = (hidden_grad * up_val * sigma * (1.0 + gate_val * (1.0 - sigma))).astype(jnp.bfloat16)
-    up_grad = (hidden_grad * gate_val * sigma).astype(jnp.bfloat16)
-    for q in range(FOLD):
-        at = slice(q * part, (q + 1) * part)
-        piece = jnp.dot(gate_grad, w_ref[0, 0, :, at], preferred_element_type=jnp.float32)
-        piece = piece + jnp.dot(up_grad, w_ref[0, 1, :, at], preferred_element_type=jnp.float32)
-        piece = piece.reshape(shards, ROOM, part)
-
-        @pl.when(step == 0)
-        def _():
-            back_ref[:, :, at] = piece
-
-        @pl.when(step == 1)
-        def _():
-            back_ref[:, :, at] += piece
-
-    @pl.when(step == 1)
-    def _():
-        bit = bit_ref[0]
-
-        def folded(shard):
-            block = back_ref[shard]
-            return jnp.concatenate([block[:CAP, q * part : (q + 1) * part] for q in range(FOLD)], axis=0)
-
-        for k in range(shards // 2):
-            stay_ref[k] = folded(2 * k + bit)
-            leave_ref[k] = folded(2 * k + 1 - bit).astype(jnp.bfloat16)
-
-
-def expert_block(bit, rows, weights):
+    arrive = pltpu.make_async_copy(rows_hbm, rows_ref, sems.at[0])
+    fetch = [
+        [pltpu.make_async_copy(hbm.at[k], w_ref.at[c, k], sems.at[1 + 3 * c + k]) for k in range(3)]
+        for c, hbm in enumerate((own_hbm, other_hbm))
+    ]
+    arrive.start()
+    for copy in fetch[0] + fetch[1]:
+        copy.start()
+    arrive.wait()
+    for c in range(2):
+        ins = rows_ref[:, :ROOM, :].reshape(shards * ROOM, width)
+        fetch[c][0].wait()
+        gate_val = across(ins, w_ref[c, 0])
+        fetch[c][1].wait()
+        up_val = across(ins, w_ref[c, 1])
+        fetch[c][2].wait()
+        grads = rows_ref[:, ROOM:, :].reshape(shards * ROOM, width)
+        hidden_grad = across(grads, w_ref[c, 2])
+        sigma = jax.nn.sigmoid(gate_val)
+        gate_grad = (hidden_grad * up_val * sigma * (1.0 + gate_val * (1.0 - sigma))).astype(
+            jnp.bfloat16
+        )
+        up_grad = (hidden_grad * gate_val * sigma).astype(jnp.bfloat16)
+        for q in range(FOLD):
+            at = slice(q * part, (q + 1) * part)
+            piece = jnp.dot(gate_grad, w_ref[c, 0, :, at], preferred_element_type=jnp.float32)
+            piece = piece + jnp.dot(up_grad, w_ref[c, 1, :, at], preferred_element_type=jnp.float32)
+            if c == 0:
+                back_ref[q] = piece
+            else:
+                back_ref[q] += piece
+    for shard in range(shards):
+        at = slice(shard * ROOM, shard * ROOM + CAP)
+        block = jnp.concatenate([back_ref[q, at, :] for q in range(FOLD)], axis=0)
+        out_ref[shard] = block.astype(jnp.bfloat16)
+
+
+def expert_block(rows, own, other):
     shards, depth, width = rows.shape
-    out = (shards // 2, FOLD * CAP, width // FOLD)
+    out = (shards, FOLD * CAP, width // FOLD)
     return pl.pallas_call(
         expert_kernel,
-        grid=(2,),
-        in_specs=[
-            pl.BlockSpec(memory_space=pltpu.SMEM),
-            pl.BlockSpec((shards, depth, width), lambda i: (0, 0, 0)),
-            pl.BlockSpec((1, 3, UNITS, width), lambda i: (i, 0, 0, 0)),
+        in_specs=[pl.BlockSpec(memory_space=pl.ANY)] * 3,
+        out_specs=pl.BlockSpec(memory_space=pltpu.VMEM),
+        out_shape=jax.ShapeDtypeStruct(out, jnp.bfloat16),
+        scratch_shapes=[
+            pltpu.VMEM(rows.shape, jnp.bfloat16),
+            pltpu.VMEM((2, *own.shape), jnp.bfloat16),
+            pltpu.VMEM((FOLD, shards * ROOM, width // FOLD), jnp.float32),
+            pltpu.SemaphoreType.DMA((7,)),
         ],
-        out_specs=[pl.BlockSpec(out, lambda i: (0, 0, 0))] * 2,
-        out_shape=[
-            jax.ShapeDtypeStruct(out, jnp.float32),
-            jax.ShapeDtypeStruct(out, jnp.bfloat16),
-        ],
-        scratch_shapes=[pltpu.VMEM((shards, ROOM, width), jnp.float32)],
-        compiler_params=pltpu.CompilerParams(vmem_limit_bytes=48 * MIB),
+        compiler_params=pltpu.CompilerParams(vmem_limit_bytes=58 * MIB),
         cost_estimate=pl.CostEstimate(
             flops=2 * 5 * shards * ROOM * 2 * UNITS * width,
-            bytes_accessed=2 * weights.size + 2 * rows.size,
+            bytes_accessed=4 * own.size + 2 * rows.size,
             transcendentals=0,
         ),
         name="expert_block",
-    )(bit, rows, weights)
+    )(rows, own, other)
+
+
+def sum_kernel(in_ref, out_ref):
+    total = jnp.sum(in_ref[...].astype(jnp.float32), axis=0).astype(jnp.bfloat16)
+    for copy in range(out_ref.shape[0]):
+        out_ref[copy] = total
+
+
+def rows_kernel(
+    head_ref,
+    slots_ref,
+    picks_ref,
+    fold_ref,
+    resid_ref,
+    grad_ref,
+    gain_ref,
+    *rest,
+):
+    *w_hbm, back_ref, part_ref, w_ref, sems = rest
+    fetch = [pltpu.make_async_copy(w, w_ref.at[d], sems.at[d]) for d, w in enumerate(w_hbm)]
+    for copy in fetch:
+        copy.start()
+    flat = slots_ref[...].reshape(-1, slots_ref.shape[2])
+    fold = fold_ref[...]
+    picks = picks_ref[...]
+    pieces = [
+        jnp.dot(
+            jnp.where(fold == q, picks, 0.0).astype(jnp.bfloat16),
+            flat,
+            preferred_element_type=jnp.float32,
+        )
+        for q in range(FOLD)
+    ]
+    summed = jnp.concatenate(pieces, axis=1)
+    resid_full = resid_ref[...].astype(jnp.float32)
+    inv_rms = lax.rsqrt(jnp.mean(resid_full * resid_full, axis=-1, keepdims=True) + EPSILON)
+    grad_full = grad_ref[...].astype(jnp.float32)
+    back = norm_back(resid_full, inv_rms, grad_full, gain_ref[...], summed)
+    back_ref[...] = back
+    for d, copy in enumerate(fetch):
+        copy.wait()
+        there = lax.rem(head_ref[0] + d, len(fetch))
+        part_ref[there] = across(back, w_ref[d]).astype(jnp.bfloat16)
 
 
 def early_kernel(scale, query_ref, key_ref, value_ref, qpos_ref, kpos_ref, prob_ref, out_ref):
@@ -119,16 +160,19 @@
     back_ref[...] = (scale * total).astype(jnp.bfloat16)
 
 
-def in_vmem(kernel, out_shape, name, flops, *args):
+def in_vmem(kernel, out_shape, name, flops, *args, fetched=(), scratch=(), limit=32):
+    places = [pltpu.SMEM if a.size == 1 else pltpu.VMEM for a in args]
+    places = places + [pl.ANY] * len(fetched)
     return pl.pallas_call(
         kernel,
-        in_specs=[pl.BlockSpec(memory_space=pltpu.VMEM)] * len(args),
+        in_specs=[pl.BlockSpec(memory_space=place) for place in places],
         out_specs=jax.tree.map(lambda _: pl.BlockSpec(memory_space=pltpu.VMEM), out_shape),
         out_shape=out_shape,
-        compiler_params=pltpu.CompilerParams(vmem_limit_bytes=32 * MIB),
+        compiler_params=pltpu.CompilerParams(vmem_limit_bytes=limit * MIB),
         cost_estimate=pl.CostEstimate(flops=flops, bytes_accessed=4 * MIB, transcendentals=0),
+        scratch_shapes=list(scratch),
         name=name,
-    )(*args)
+    )(*args, *fetched)
 
 
 def core_swap(block):
@@ -199,13 +243,12 @@
     )
     fill = ((0, UNITS - gate_mat.shape[0]), (0, 0))
     own = jnp.stack([jnp.pad(w, fill) for w in (gate_mat, up_mat, down_mat)], axis=0)
-    weights = jnp.stack([own, core_swap(own)], axis=0)
+    other = core_swap(own)
     w_near = [w_mine] + [
         lax.ppermute(w_mine, "head", [(a, (a - d) % head_count) for a in range(head_count)])
         for d in range(1, head_count)
     ]
-    w_four = jnp.concatenate(w_near, axis=0)
-    weights, w_four = lax.optimization_barrier((weights, w_four))
+    other, *w_near = lax.optimization_barrier((other, *w_near))
 
     packed = rows.reshape(z_count, 2, ROOM, width)[:, :, CAP:]
     packed = jnp.stack([packed, core_swap(packed)], axis=0)
@@ -233,34 +276,48 @@
         key_pos[None, :],
     )
 
-    bit = z_index % 2
-    stay, leave = expert_block(bit.reshape(1), rows, weights)
-    up = [(2 * a, 2 * ((a + 1) % z_count)) for a in range(z_count)]
-    down = [(2 * a + 1, 2 * ((a - 1) % z_count) + 1) for a in range(z_count)]
-    came = lax.ppermute(leave, ("z", "core"), up + down)
-    left = (stay + came.astype(f32)).astype(bf16)
-    same = [list(range(r, z_count, 2)) for r in range(2)]
-    left = lax.all_to_all(left, "z", 0, 0, tiled=True, axis_index_groups=same)
-    slots = jnp.sum(left.astype(f32), axis=0).astype(bf16)
-    slots = lax.all_to_all(
-        jnp.broadcast_to(slots[None], (exp_count, *slots.shape)), "exp", 0, 0, tiled=True
-    )
+    leave = expert_block(rows, own, other)
+    came = lax.all_to_all(leave, "z", 0, 0, tiled=True)
+    came, probs, output, key_all, value_all = lax.optimization_barrier(
+        (came, probs, output, key_all, value_all)
+    )
+    slots = in_vmem(
+        sum_kernel,
+        jax.ShapeDtypeStruct((exp_count, *came.shape[1:]), bf16),
+        "slot_sum",
+        came.size,
+        came,
+    )
+    slots = lax.all_to_all(slots, "exp", 0, 0, tiled=True)
     picks = []
     for expert in range(exp_count):
         routed, position, _ = slots_of(expert)
         picks.append((position[:, None] == slot_ids[None, :CAP]) & routed[:, None])
-    picks = jnp.stack(picks, axis=1).astype(bf16)
-    flat = slots.reshape(exp_count * FOLD * CAP, -1)
-    pieces = []
-    for q in range(FOLD):
-        there = jnp.zeros((quarter, exp_count, FOLD, CAP), bf16).at[:, :, q].set(picks)
-        pieces.append(jnp.dot(there.reshape(quarter, -1), flat, preferred_element_type=f32))
-    summed = jnp.concatenate(pieces, axis=1)
-    grad_quarter = norm_back(resid_full, inv_rms, grad_full, norm_gain, summed)
-
-    at_heads = lax.dot_general(grad_quarter, w_four, CONTRACT, preferred_element_type=f32)
-    at_heads = at_heads.astype(bf16).reshape(quarter, head_count, HD).transpose(1, 0, 2)
-    at_heads = jnp.roll(at_heads, head_index, axis=0)
+    picks = jnp.stack(picks, axis=1).astype(f32)[:, :, None, :]
+    picks = jnp.broadcast_to(picks, (quarter, exp_count, FOLD, CAP)).reshape(quarter, -1)
+    fold = jnp.arange(picks.shape[1], dtype=jnp.int32) // CAP % FOLD
+    grad_quarter, at_heads = in_vmem(
+        rows_kernel,
+        [
+            jax.ShapeDtypeStruct((quarter, width), bf16),
+            jax.ShapeDtypeStruct((head_count, quarter, HD), bf16),
+        ],
+        "token_rows",
+        2 * quarter * width * (picks.shape[1] + head_count * HD),
+        head_index.reshape(1),
+        slots,
+        picks,
+        fold[None, :],
+        resid_part,
+        grad_part,
+        norm_gain[None, :],
+        fetched=w_near,
+        limit=58,
+        scratch=(
+            pltpu.VMEM((head_count, *w_out.shape), bf16),
+            pltpu.SemaphoreType.DMA((head_count,)),
+        ),
+    )
     attn_grad = lax.all_to_all(at_heads, "head", 0, 0, tiled=True).reshape(tok_rows, HD)
     query_grad = in_vmem(
         functools.partial(late_kernel, scale),

time: 237 us -> 242 us (1.021)
  other arithmetic: 29.2 us -> 9.4 us
  blocking collectives: 0 us -> 9.69 us
  Pallas kernels: 17.3 us -> 26.6 us
  waiting for transfers between devices: 122 us -> 131 us
  local copies, waits for them, and re-layouts: 15 us -> 20.6 us
  matrix products: 4.79 us -> 0.5 us
  starting transfers between devices: 32.7 us -> 29.1 us
    another operation x3 -> x2, other arithmetic: 13.3 us -> 0.92 us  [the longest x1 0.83 us: per_device(): jnp.stack([jnp.pad(w, fill) for w in (gate_mat, up_mat, down_mat)], axis=0)]
    ppermute x1 -> x0, waiting for transfers between devices: 11.1 us -> none  [per_device(): came = lax.ppermute(leave, ('z', 'core'), up + down)]
    all_gather x1, waiting for transfers between devices: 12.4 us -> 23 us  [per_device(): lax.all_gather(mine, 'z', axis=0, tiled=True)]
    all_to_all x0 -> x1, blocking collectives: none -> 9.69 us  [per_device(): lax.all_to_all(at_heads, 'head', 0, 0, tiled=True).reshape(tok_rows, HD)]
    pallas_call x3 -> x5, Pallas kernels: 17.3 us -> 26.6 us  [the longest x1 15.5 us: expert_block(): pl.pallas_call(expert_kernel, in_specs=[pl.BlockSpec(memory_space=pl.ANY)...]
    all_to_all x3 -> x2, waiting for transfers between devices: 53.2 us -> 60.1 us  [the longest x1 44.4 us: per_device(): came = lax.all_to_all(leave, 'z', 0, 0, tiled=True)]
    concatenate x2 -> x0, other arithmetic: 3.89 us -> none  [the longest x1 3.23 us: per_device(): w_four = jnp.concatenate(w_near, axis=0)]
    unnamed x19 -> x27, local copies, waits for them, and re-layouts: 5.64 us -> 8.76 us
  transfers between devices with their start and end apart: 10 -> 8, of which waited for: 7 -> 6; matrix products, arithmetic and copies ran while one was open for 13% -> 7% of each run, Pallas kernels for 1% -> 1%
where the time goes in v4:
time: 242 us; the launch traced here: 241 us
  waiting for transfers between devices  131 us (54%)
  starting transfers between devices  29.1 us (12%)
  Pallas kernels  26.6 us (11%)
  local copies, waits for them, and re-layouts  20.6 us (9%)
  between operations  14.3 us (6%)
  blocking collectives  9.69 us (4%)
  other arithmetic  9.4 us (4%)
    ppermute x3, waiting for transfers between devices, per_device(): lax.ppermute(w_mine, 'head', [(a, (a - d) % head_count) for a in range(he...  45.6 us
    all_to_all x1, waiting for transfers between devices, per_device(): came = lax.all_to_all(leave, 'z', 0, 0, tiled=True)  44.4 us
    all_gather x1, waiting for transfers between devices, per_device(): lax.all_gather(mine, 'z', axis=0, tiled=True)  23 us
    all_to_all x1, waiting for transfers between devices, per_device(): slots = lax.all_to_all(slots, 'exp', 0, 0, tiled=True)  15.6 us
    pallas_call x1, Pallas kernels, expert_block(): pl.pallas_call(expert_kernel, in_specs=[pl.BlockSpec(memory_space=pl.ANY)...  15.5 us
    pallas_call x4, Pallas kernels, in_vmem(): pl.pallas_call(kernel, in_specs=[pl.BlockSpec(memory_space=place) for pla...  11.1 us
    ppermute x3, starting transfers between devices, per_device(): lax.ppermute(w_mine, 'head', [(a, (a - d) % head_count) for a in range(he...  10.2 us
    all_to_all x1, blocking collectives, per_device(): lax.all_to_all(at_heads, 'head', 0, 0, tiled=True).reshape(tok_rows, HD)  9.69 us
  transfers between devices with their start and end apart: 8, of which 6 were waited for; matrix products, arithmetic and copies ran while one was open for 7% of the time, Pallas kernels for 1%

profile of v4, /device:TPU:64, one launch (start us, length us, event | category | flops | bytes accessed | tf_op | source)
XLA Modules:
  0.0 241.0 jit_solution(13914113354990427855)
XLA Ops:
  7.2 0.9 compare_reduce_fusion
  8.1 0.1 convert_reduce_fusion.8
  8.2 0.2 copy-done
  8.4 1.2 fusion.1
  9.7 0.7 convert_element_type.62
  10.4 0.8 reshape.773
  11.2 0.8 reshape.774
  12.0 0.8 select_reduce_fusion
  12.7 0.2 convolution_convert_fusion
  13.0 0.3 convolution_convert_fusion.1
  13.3 0.8 pad_maximum_fusion.2
  14.1 1.6 pad_bitcast_fusion.2
  15.7 2.4 pad_bitcast_fusion
  18.1 0.8 pad_maximum_fusion.own_hbm
  19.0 2.7 %copy-done.5 = bf16[3,256,4096]{2,1,0:T(8,128)(2,1)} copy-done((bf16[3,256,4096]{2,1,0:T(8,128)(2,1)}, bf16[3,256,4096]{2,1,0:T(8,128)(2,1)S(1)}, u32[]{:S(2)}) %copy-start.5) | copy-done | bytes 6291480
  21.6 1.9 collective-permute-start
  23.6 4.7 %collective-permute-start.1 = (bf16[128,4096]{1,0:T(8,128)(2,1)S(1)}, bf16[128,4096]{1,0:T(8,128)(2,1)S(1)}, u32[]{:S(2)}, u32[]{:S(2)}) collective-permute-start(bf16[128,4096]{1,0:T(8,128)(2,1)S(1)} %copy-done.7), channel_id=1, source_target_pairs={{0,3},{1,0},{2,1},{3,2},{4,7},{5,4},{6,5},{7,6},{8,11},{9,8},{10,9... | collective-permute-start | bytes 3145736 | tf_op jit(solution)/shard_map/ppermute | solution.py:248
  28.2 2.7 %collective-permute-start.2 = (bf16[128,4096]{1,0:T(8,128)(2,1)S(1)}, bf16[128,4096]{1,0:T(8,128)(2,1)S(1)}, u32[]{:S(2)}, u32[]{:S(2)}) collective-permute-start(bf16[128,4096]{1,0:T(8,128)(2,1)S(1)} %copy-done.7), channel_id=1, source_target_pairs={{0,2},{1,3},{2,0},{3,1},{4,6},{5,7},{6,4},{7,5},{8,10},{9,11},{10,... | collective-permute-start | bytes 3145736 | tf_op jit(solution)/shard_map/ppermute | solution.py:248
  31.0 2.8 %collective-permute-start.3 = (bf16[128,4096]{1,0:T(8,128)(2,1)S(1)}, bf16[128,4096]{1,0:T(8,128)(2,1)S(1)}, u32[]{:S(2)}, u32[]{:S(2)}) collective-permute-start(bf16[128,4096]{1,0:T(8,128)(2,1)S(1)} %copy-done.7), channel_id=1, source_target_pairs={{0,1},{1,2},{2,3},{3,0},{4,5},{5,6},{6,7},{7,4},{8,9},{9,10},{10,1... | collective-permute-start | bytes 3145736 | tf_op jit(solution)/shard_map/ppermute | solution.py:248
  33.8 40.0 %collective-permute-done.1.rest_1_ = bf16[128,4096]{1,0:T(8,128)(2,1)S(1)} collective-permute-done((bf16[128,4096]{1,0:T(8,128)(2,1)S(1)}, bf16[128,4096]{1,0:T(8,128)(2,1)S(1)}, u32[]{:S(2)}, u32[]{:S(2)}) %collective-permute-start.1) | collective-permute-done | bytes 1048608 | tf_op jit(solution)/shard_map/ppermute | solution.py:248
  73.8 5.6 %collective-permute-done.3.rest_3_ = bf16[128,4096]{1,0:T(8,128)(2,1)S(1)} collective-permute-done((bf16[128,4096]{1,0:T(8,128)(2,1)S(1)}, bf16[128,4096]{1,0:T(8,128)(2,1)S(1)}, u32[]{:S(2)}, u32[]{:S(2)}) %collective-permute-start.3) | collective-permute-done | bytes 1048608 | tf_op jit(solution)/shard_map/ppermute | solution.py:248
  79.4 1.0 copy-done.10
  80.4 23.0 %all-gather.2.cloned.1.call-done = bf16[512,4096]{1,0:T(8,128)(2,1)} async-done(((bf16[32,4096]{1,0:T(8,128)(2,1)}), bf16[512,4096]{1,0:T(8,128)(2,1)}) %all-gather.2.cloned.1.call-update) | async-done | bytes 4194320 | tf_op jit(solution)/shard_map/all_gather | solution.py:240
  103.4 15.5 %expert_block.1 = bf16[16,48,1024]{2,1,0:T(8,128)(2,1)} custom-call(bf16[16,32,4096]{2,1,0:T(8,128)(2,1)} %bitcast.34, bf16[3,256,4096]{2,1,0:T(8,128)(2,1)} %copy-done.5, bf16[3,256,4096]{2,1,0:T(8,128)(2,1)} %collective-permute-done.other_hbm), custom_call_target="tpu_custom_call" | custom-call | flops 5368709120 | bytes 16777216 | tf_op jit(solution)/shard_map/expert_block/pallas_call | solution.py:73
  118.9 8.1 %all-to-all-start = ((bf16[16,48,1024]{2,1,0:T(8,128)(2,1)}), bf16[16,48,1024]{2,1,0:T(8,128)(2,1)}, u32[]{:S(2)}, u32[]{:S(2)}) async-start(bf16[16,48,1024]{2,1,0:T(8,128)(2,1)} %expert_block.1), calls=%async_computation | async-start | bytes 3145728 | tf_op jit(solution)/shard_map/all_to_all | solution.py:280
  127.0 0.1 convert_reduce_fusion.6
  127.2 2.7 %fusion.29 = (bf16[16,2,4,4096]{3,2,0,1:T(4,128)(2,1)S(1)}, bf16[1,16,2,4,4096]{4,3,1,0,2:T(4,128)(2,1)S(1)}) fusion(bf16[16,2,16,4096]{3,2,1,0:T(8,128)(2,1)} %bitcast.35), kind=kLoop, calls=%fused_computation.95 | loop fusion | bytes 3145728
  129.9 2.1 collective-permute-start.4
  132.0 0.1 convert_reduce_fusion.4
  132.3 0.1 fusion.9.kpos_ref
  132.4 2.1 collective-permute-done.4
  134.4 2.4 pad_maximum_fusion.1
  136.8 1.1 reshape_squeeze.6.key_ref
  137.9 2.2 reshape_squeeze.7.value_ref
  140.1 1.8 attention_early.1
  141.9 1.3 copy-done.2
  143.3 44.4 %all-to-all-done.in_ref = bf16[16,48,1024]{2,1,0:T(8,128)(2,1)} async-done(((bf16[16,48,1024]{2,1,0:T(8,128)(2,1)}), bf16[16,48,1024]{2,1,0:T(8,128)(2,1)}, u32[]{:S(2)}, u32[]{:S(2)}) %all-to-all-start) | async-done | bytes 1572896 | tf_op jit(solution)/shard_map/all_to_all | solution.py:280
  187.7 1.6 slot_sum.1
  189.3 0.9 copy-done.1
  190.2 6.7 %all-to-all-start.1 = ((bf16[8,48,1024]{2,1,0:T(8,128)(2,1)}), bf16[8,48,1024]{2,1,0:T(8,128)(2,1)}, u32[]{:S(2)}, u32[]{:S(2)}) async-start(bf16[8,48,1024]{2,1,0:T(8,128)(2,1)} %copy-done.1), calls=%async_computation.1 | async-start | bytes 1572864 | tf_op jit(solution)/shard_map/all_to_all | solution.py:291
  197.0 0.6 broadcast_in_dim.10.gain_ref
  198.2 0.7 reshape.776
  198.9 1.6 copy.21.picks_ref
  200.5 0.6 and_select_fusion.5.fold_ref
  201.1 15.6 %all-to-all-done.1.slots_ref = bf16[8,48,1024]{2,1,0:T(8,128)(2,1)} async-done(((bf16[8,48,1024]{2,1,0:T(8,128)(2,1)}), bf16[8,48,1024]{2,1,0:T(8,128)(2,1)}, u32[]{:S(2)}, u32[]{:S(2)}) %all-to-all-start.1) | async-done | bytes 786464 | tf_op jit(solution)/shard_map/all_to_all | solution.py:291
  216.8 6.0 %token_rows.1 = (bf16[32,4096]{1,0:T(8,128)(2,1)}, bf16[4,32,128]{2,1,0:T(8,128)(2,1)}) custom-call(s32[1]{0:T(128)} %bitcast.head_ref, bf16[8,48,1024]{2,1,0:T(8,128)(2,1)} %all-to-all-done.1.slots_ref, f32[32,384]{1,0:T(8,128)} %copy.21.picks_ref, s32[1,384]{1,0:T(1,128)} %and_select_fusion.5.fold_ref, bf16[32,4096]{1,0:T(8,128)(2,1)} %copy-done.11, ...), custom_call_target="tpu_custom_call" | custom-call | flops 234881024 | bytes 4194304 | tf_op jit(solution)/shard_map/token_rows/pallas_call | solution.py:166
  222.8 9.7 %all_to_all.15 = bf16[4,32,128]{2,1,0:T(8,128)(2,1)S(1)} all-to-all(bf16[4,32,128]{2,1,0:T(8,128)(2,1)} %get-tuple-element.33), channel_id=1, replica_groups=mesh['z'=16,'core'=2,'exp'=8,'head'=4] {'head'}, dimensions={0} | all-to-all | bytes 65536 | tf_op jit(solution)/shard_map/all_to_all | solution.py:321
  232.5 1.7 attention_late.1
  (41 shorter events, 1.0 us)
Async XLA Ops:
  7.2 1.2 copy-start
  7.2 96.2 %all-gather.2.cloned.1.call-start = ((), (), s32[]{:S(2)}) async-start(), calls=%async_computation.3 | async-start | bytes 4456448 | tf_op jit(solution)/shard_map/all_gather | solution.py:240
  8.4 5.6 %copy-start.6 = (bf16[32,4096]{1,0:T(8,128)(2,1)}, bf16[32,4096]{1,0:T(8,128)(2,1)S(1)}, u32[]{:S(2)}) copy-start(bf16[32,4096]{1,0:T(8,128)(2,1)S(1)} %constant_dynamic-slice_fusion.grad_ref) | copy-start | bytes 786436
  9.7 4.4 %copy-start.11 = (bf16[32,4096]{1,0:T(8,128)(2,1)}, bf16[32,4096]{1,0:T(8,128)(2,1)S(1)}, u32[]{:S(2)}) copy-start(bf16[32,4096]{1,0:T(8,128)(2,1)S(1)} %get-tuple-element.48.resid_ref) | copy-start | bytes 786436
  18.1 5.4 %copy-start.7 = (bf16[128,4096]{1,0:T(8,128)(2,1)S(1)}, bf16[128,4096]{1,0:T(8,128)(2,1)}, u32[]{:S(2)}) copy-start(bf16[128,4096]{1,0:T(8,128)(2,1)} %rest_0_) | copy-start | bytes 3145732
  19.0 2.7 %copy-start.5 = (bf16[3,256,4096]{2,1,0:T(8,128)(2,1)}, bf16[3,256,4096]{2,1,0:T(8,128)(2,1)S(1)}, u32[]{:S(2)}) copy-start(bf16[3,256,4096]{2,1,0:T(8,128)(2,1)S(1)} %pad_maximum_fusion.own_hbm) | copy-start | bytes 18874372
  21.6 58.7 %collective-permute-start = (bf16[3,256,4096]{2,1,0:T(8,128)(2,1)S(1)}, bf16[3,256,4096]{2,1,0:T(8,128)(2,1)}, u32[]{:S(2)}, u32[]{:S(2)}) collective-permute-start(bf16[3,256,4096]{2,1,0:T(8,128)(2,1)S(1)} %pad_maximum_fusion.own_hbm), channel_id=1, source_target_pairs={{0,32},{32,0},{1,33},{33,1},{2,34},{34,2},{3,35},{35,3},{4,36},{36... | collective-permute-start | bytes 18874376 | tf_op jit(solution)/shard_map/ppermute | solution.py:179
  23.6 50.2 %collective-permute-start.1 = (bf16[128,4096]{1,0:T(8,128)(2,1)S(1)}, bf16[128,4096]{1,0:T(8,128)(2,1)S(1)}, u32[]{:S(2)}, u32[]{:S(2)}) collective-permute-start(bf16[128,4096]{1,0:T(8,128)(2,1)S(1)} %copy-done.7), channel_id=1, source_target_pairs={{0,3},{1,0},{2,1},{3,2},{4,7},{5,4},{6,5},{7,6},{8,11},{9,8},{10,9... | collective-permute-start | bytes 3145736 | tf_op jit(solution)/shard_map/ppermute | solution.py:248
  28.2 45.6 %collective-permute-start.2 = (bf16[128,4096]{1,0:T(8,128)(2,1)S(1)}, bf16[128,4096]{1,0:T(8,128)(2,1)S(1)}, u32[]{:S(2)}, u32[]{:S(2)}) collective-permute-start(bf16[128,4096]{1,0:T(8,128)(2,1)S(1)} %copy-done.7), channel_id=1, source_target_pairs={{0,2},{1,3},{2,0},{3,1},{4,6},{5,7},{6,4},{7,5},{8,10},{9,11},{10,... | collective-permute-start | bytes 3145736 | tf_op jit(solution)/shard_map/ppermute | solution.py:248
  31.0 48.4 %collective-permute-start.3 = (bf16[128,4096]{1,0:T(8,128)(2,1)S(1)}, bf16[128,4096]{1,0:T(8,128)(2,1)S(1)}, u32[]{:S(2)}, u32[]{:S(2)}) collective-permute-start(bf16[128,4096]{1,0:T(8,128)(2,1)S(1)} %copy-done.7), channel_id=1, source_target_pairs={{0,1},{1,2},{2,3},{3,0},{4,5},{5,6},{6,7},{7,4},{8,9},{9,10},{10,1... | collective-permute-start | bytes 3145736 | tf_op jit(solution)/shard_map/ppermute | solution.py:248
  73.8 45.1 %copy-start.8 = (bf16[128,4096]{1,0:T(8,128)(2,1)}, bf16[128,4096]{1,0:T(8,128)(2,1)S(1)}, u32[]{:S(2)}) copy-start(bf16[128,4096]{1,0:T(8,128)(2,1)S(1)} %collective-permute-done.1.rest_1_) | copy-start | bytes 3145732
  73.8 45.1 %copy-start.9 = (bf16[128,4096]{1,0:T(8,128)(2,1)}, bf16[128,4096]{1,0:T(8,128)(2,1)S(1)}, u32[]{:S(2)}) copy-start(bf16[128,4096]{1,0:T(8,128)(2,1)S(1)} %collective-permute-done.2.rest_2_) | copy-start | bytes 3145732
  79.4 1.0 copy-start.10
  118.9 68.8 %all-to-all-start = ((bf16[16,48,1024]{2,1,0:T(8,128)(2,1)}), bf16[16,48,1024]{2,1,0:T(8,128)(2,1)}, u32[]{:S(2)}, u32[]{:S(2)}) async-start(bf16[16,48,1024]{2,1,0:T(8,128)(2,1)} %expert_block.1), calls=%async_computation | async-start | bytes 3145728 | tf_op jit(solution)/shard_map/all_to_all | solution.py:280
  129.9 4.6 %collective-permute-start.4 = (bf16[16,2,4,4096]{3,2,0,1:T(4,128)(2,1)S(1)}, bf16[16,2,4,4096]{3,2,0,1:T(4,128)(2,1)S(1)}, u32[]{:S(2)}, u32[]{:S(2)}) collective-permute-start(bf16[16,2,4,4096]{3,2,0,1:T(4,128)(2,1)S(1)} %get-tuple-element.52), channel_id=1, source_target_pairs={{0,32},{32,0},{1,33},{33,1},{2,34},{34,2},{3,35},{35,3},{4,36},{36... | collective-permute-start | bytes 3145736 | tf_op jit(solution)/shard_map/ppermute | solution.py:179
  136.8 3.3 %copy-start.4 = (bf16[128,128]{1,0:T(8,128)(2,1)S(1)}, bf16[128,128]{1,0:T(8,128)(2,1)}, u32[]{:S(2)}) copy-start(bf16[128,128]{1,0:T(8,128)(2,1)} %query_ref.1) | copy-start | bytes 98308
  141.9 1.4 copy-start.2
  143.3 53.8 %copy-start.12 = (bf16[4096]{0:T(1024)(128)(2,1)S(1)}, bf16[4096]{0:T(1024)(128)(2,1)}, u32[]{:S(2)}) copy-start(bf16[4096]{0:T(1024)(128)(2,1)} %param.14) | copy-start | bytes 24580
  189.3 0.9 copy-start.1
  190.2 26.6 %all-to-all-start.1 = ((bf16[8,48,1024]{2,1,0:T(8,128)(2,1)}), bf16[8,48,1024]{2,1,0:T(8,128)(2,1)}, u32[]{:S(2)}, u32[]{:S(2)}) async-start(bf16[8,48,1024]{2,1,0:T(8,128)(2,1)} %copy-done.1), calls=%async_computation.1 | async-start | bytes 1572864 | tf_op jit(solution)/shard_map/all_to_all | solution.py:291
  216.8 15.7 %copy-start.3 = (f32[128,4096]{1,0:T(8,128)S(1)}, f32[128,4096]{1,0:T(8,128)}, u32[]{:S(2)}) copy-start(f32[128,4096]{1,0:T(8,128)} %copy-done.2) | copy-start | bytes 6291460
Sparse Core Ops, SparseCore 0:
  14.2 89.1 all-gather.1

commit v5 on v4

--- a/solution.py
+++ b/solution.py
@@ -27,7 +27,9 @@
     return high, (full - high.astype(jnp.float32)).astype(jnp.bfloat16)
 
 
-def expert_kernel(rows_hbm, own_hbm, other_hbm, out_ref, rows_ref, w_ref, back_ref, sems):
+def expert_kernel(
+    order_ref, rows_hbm, own_hbm, other_hbm, stay_ref, leave_ref, rows_ref, w_ref, back_ref, sems
+):
     shards, _, width = rows_ref.shape
     part = width // FOLD
     arrive = pltpu.make_async_copy(rows_hbm, rows_ref, sems.at[0])
@@ -35,17 +37,23 @@
         [pltpu.make_async_copy(hbm.at[k], w_ref.at[c, k], sems.at[1 + 3 * c + k]) for k in range(3)]
         for c, hbm in enumerate((own_hbm, other_hbm))
     ]
-    arrive.start()
-    for copy in fetch[0] + fetch[1]:
+    coming = [arrive] + fetch[0] + fetch[1]
+    for copy in coming[:3]:
         copy.start()
-    arrive.wait()
+
+    def take(index):
+        coming[index].wait()
+        if index + 3 < len(coming):
+            coming[index + 3].start()
+
+    take(0)
     for c in range(2):
         ins = rows_ref[:, :ROOM, :].reshape(shards * ROOM, width)
-        fetch[c][0].wait()
+        take(3 * c + 1)
         gate_val = across(ins, w_ref[c, 0])
-        fetch[c][1].wait()
+        take(3 * c + 2)
         up_val = across(ins, w_ref[c, 1])
-        fetch[c][2].wait()
+        take(3 * c + 3)
         grads = rows_ref[:, ROOM:, :].reshape(shards * ROOM, width)
         hidden_grad = across(grads, w_ref[c, 2])
         sigma = jax.nn.sigmoid(gate_val)
@@ -61,20 +69,21 @@
                 back_ref[q] = piece
             else:
                 back_ref[q] += piece
-    for shard in range(shards):
-        at = slice(shard * ROOM, shard * ROOM + CAP)
+    for k in range(shards):
+        at = pl.ds(pl.multiple_of(order_ref[k] * ROOM, ROOM), CAP)
         block = jnp.concatenate([back_ref[q, at, :] for q in range(FOLD)], axis=0)
-        out_ref[shard] = block.astype(jnp.bfloat16)
-
-
-def expert_block(rows, own, other):
+        out_ref = stay_ref if k < shards // 2 else leave_ref
+        out_ref[k % (shards // 2)] = block.astype(jnp.bfloat16)
+
+
+def expert_block(order, rows, own, other):
     shards, depth, width = rows.shape
-    out = (shards, FOLD * CAP, width // FOLD)
+    out = (shards // 2, FOLD * CAP, width // FOLD)
     return pl.pallas_call(
         expert_kernel,
-        in_specs=[pl.BlockSpec(memory_space=pl.ANY)] * 3,
-        out_specs=pl.BlockSpec(memory_space=pltpu.VMEM),
-        out_shape=jax.ShapeDtypeStruct(out, jnp.bfloat16),
+        in_specs=[pl.BlockSpec(memory_space=pltpu.SMEM)] + [pl.BlockSpec(memory_space=pl.ANY)] * 3,
+        out_specs=[pl.BlockSpec(memory_space=pltpu.VMEM)] * 2,
+        out_shape=[jax.ShapeDtypeStruct(out, jnp.bfloat16)] * 2,
         scratch_shapes=[
             pltpu.VMEM(rows.shape, jnp.bfloat16),
             pltpu.VMEM((2, *own.shape), jnp.bfloat16),
@@ -88,7 +97,7 @@
             transcendentals=0,
         ),
         name="expert_block",
-    )(rows, own, other)
+    )(order, rows, own, other)
 
 
 def sum_kernel(in_ref, out_ref):
@@ -113,7 +122,7 @@
         copy.start()
     flat = slots_ref[...].reshape(-1, slots_ref.shape[2])
     fold = fold_ref[...]
-    picks = picks_ref[...]
+    picks = picks_ref[...].T
     pieces = [
         jnp.dot(
             jnp.where(fold == q, picks, 0.0).astype(jnp.bfloat16),
@@ -131,29 +140,31 @@
     for d, copy in enumerate(fetch):
         copy.wait()
         there = lax.rem(head_ref[0] + d, len(fetch))
-        part_ref[there] = across(back, w_ref[d]).astype(jnp.bfloat16)
-
-
-def early_kernel(scale, query_ref, key_ref, value_ref, qpos_ref, kpos_ref, prob_ref, out_ref):
+        part_ref[there] = across(w_ref[d], back).T.astype(jnp.bfloat16)
+
+
+def early_kernel(scale, query_ref, key0, key1, value0, value1, qpos_ref, kpos_ref, prob_ref, out_ref):
     allowed = kpos_ref[...] <= qpos_ref[...]
-    scores = jnp.where(allowed, across(query_ref[...], key_ref[...]) * scale, -1e30)
+    keys = jnp.concatenate([key0[...], key1[...]], axis=0)
+    scores = jnp.where(allowed, across(query_ref[...], keys) * scale, -1e30)
     row_max = jnp.max(scores, axis=-1, keepdims=True)
     expo_vals = jnp.where(allowed, jnp.exp(scores - row_max), 0.0)
     probs = expo_vals / jnp.sum(expo_vals, axis=-1, keepdims=True)
     prob_ref[...] = probs
     high, low = two_terms(probs)
-    values = value_ref[...]
+    values = jnp.concatenate([value0[...], value1[...]], axis=0)
     out_ref[...] = jnp.dot(high, values, preferred_element_type=jnp.float32) + jnp.dot(
         low, values, preferred_element_type=jnp.float32
     )
 
 
-def late_kernel(scale, grad_ref, key_ref, value_ref, prob_ref, out_ref, back_ref):
+def late_kernel(scale, grad_ref, key0, key1, value0, value1, prob_ref, out_ref, back_ref):
     grads = grad_ref[...]
     delta = jnp.sum(grads.astype(jnp.float32) * out_ref[...], axis=-1, keepdims=True)
-    mixed = prob_ref[...] * (across(grads, value_ref[...]) - delta)
+    values = jnp.concatenate([value0[...], value1[...]], axis=0)
+    mixed = prob_ref[...] * (across(grads, values) - delta)
     high, low = two_terms(mixed)
-    keys = key_ref[...]
+    keys = jnp.concatenate([key0[...], key1[...]], axis=0)
     total = jnp.dot(high, keys, preferred_element_type=jnp.float32) + jnp.dot(
         low, keys, preferred_element_type=jnp.float32
     )
@@ -248,12 +259,31 @@
         lax.ppermute(w_mine, "head", [(a, (a - d) % head_count) for a in range(head_count)])
         for d in range(1, head_count)
     ]
-    other, *w_near = lax.optimization_barrier((other, *w_near))
-
+    picks = []
+    for expert in range(exp_count):
+        routed, position, _ = slots_of(expert)
+        picks.append((position[:, None] == slot_ids[None, :CAP]) & routed[:, None])
+    picks = jnp.stack(picks, axis=1).astype(f32)[:, :, None, :]
+    picks = jnp.broadcast_to(picks, (quarter, exp_count, FOLD, CAP)).reshape(quarter, -1).T
+    fold = jnp.arange(picks.shape[0], dtype=jnp.int32) // CAP % FOLD
+    fold, gain_row = fold[None, :], norm_gain[None, :]
+    other, picks, fold, gain_row, resid_part, grad_part, *w_near = lax.optimization_barrier(
+        (other, picks, fold, gain_row, resid_part, grad_part, *w_near)
+    )
+
+    toward = 1 - 2 * core_index
+    fours = 4 * jnp.arange(z_count // 4, dtype=jnp.int32)
+    next_index = z_index + toward + z_count
+    order = jnp.concatenate(
+        [fours + p % 4 for p in (z_index, z_index + 2, next_index, next_index + 2)]
+    )
+    stay, leave = expert_block(order, rows, own, other)
+
+    leave, rows = lax.optimization_barrier((leave, rows))
     packed = rows.reshape(z_count, 2, ROOM, width)[:, :, CAP:]
-    packed = jnp.stack([packed, core_swap(packed)], axis=0)
-    key_all = packed[:, :, 0].reshape(-1, HD)
-    value_all = packed[:, :, 1].reshape(-1, HD)
+    both = (packed, core_swap(packed))
+    key_all = [block[:, 0].reshape(-1, HD) for block in both]
+    value_all = [block[:, 1].reshape(-1, HD) for block in both]
     query_pos = (z_index * 2 + core_index) * tok_rows + jnp.arange(tok_rows, dtype=jnp.int32)
     place = jnp.arange(2 * z_count * tok_rows, dtype=jnp.int32)
     half = z_count * tok_rows
@@ -270,17 +300,27 @@
         "attention_early",
         3 * attn_flops,
         queries,
-        key_all,
-        value_all,
+        *key_all,
+        *value_all,
         query_pos[:, None],
         key_pos[None, :],
     )
 
-    leave = expert_block(rows, own, other)
-    came = lax.all_to_all(leave, "z", 0, 0, tiled=True)
-    came, probs, output, key_all, value_all = lax.optimization_barrier(
-        (came, probs, output, key_all, value_all)
-    )
+    def step(block, dist):
+        up = [(2 * a, 2 * ((a + dist) % z_count)) for a in range(z_count)]
+        down = [(2 * a + 1, 2 * ((a - dist) % z_count) + 1) for a in range(z_count)]
+        return lax.ppermute(block, ("z", "core"), up + down)
+
+    few = z_count // 4
+    came = step(leave, 1)
+    far = (stay[few:].astype(f32) + came[few:].astype(f32)).astype(bf16)
+    came_far = step(far, 2)
+    near = stay[:few].astype(f32) + came[:few].astype(f32) + came_far.astype(f32)
+    near, probs, output, key_all, value_all = lax.optimization_barrier(
+        (near.astype(bf16), probs, output, key_all, value_all)
+    )
+    same = [list(range(r, z_count, 4)) for r in range(4)]
+    came = lax.all_to_all(near, "z", 0, 0, tiled=True, axis_index_groups=same)
     slots = in_vmem(
         sum_kernel,
         jax.ShapeDtypeStruct((exp_count, *came.shape[1:]), bf16),
@@ -289,13 +329,6 @@
         came,
     )
     slots = lax.all_to_all(slots, "exp", 0, 0, tiled=True)
-    picks = []
-    for expert in range(exp_count):
-        routed, position, _ = slots_of(expert)
-        picks.append((position[:, None] == slot_ids[None, :CAP]) & routed[:, None])
-    picks = jnp.stack(picks, axis=1).astype(f32)[:, :, None, :]
-    picks = jnp.broadcast_to(picks, (quarter, exp_count, FOLD, CAP)).reshape(quarter, -1)
-    fold = jnp.arange(picks.shape[1], dtype=jnp.int32) // CAP % FOLD
     grad_quarter, at_heads = in_vmem(
         rows_kernel,
         [
@@ -303,14 +336,14 @@
             jax.ShapeDtypeStruct((head_count, quarter, HD), bf16),
         ],
         "token_rows",
-        2 * quarter * width * (picks.shape[1] + head_count * HD),
+        2 * quarter * width * (picks.shape[0] + head_count * HD),
         head_index.reshape(1),
         slots,
         picks,
-        fold[None, :],
+        fold,
         resid_part,
         grad_part,
-        norm_gain[None, :],
+        gain_row,
         fetched=w_near,
         limit=58,
         scratch=(
@@ -325,8 +358,8 @@
         "attention_late",
         3 * attn_flops,
         attn_grad,
-        key_all,
-        value_all,
+        *key_all,
+        *value_all,
         probs,
         output,
     )

time: 242 us -> 242 us (level)
  blocking collectives: 9.69 us -> 68.6 us
  waiting for transfers between devices: 131 us -> 80.1 us
  starting transfers between devices: 29.1 us -> 20.8 us
  other arithmetic: 9.4 us -> 13.1 us
  local copies, waits for them, and re-layouts: 20.6 us -> 17.7 us
    all_to_all x2 -> x0, waiting for transfers between devices: 60.1 us -> none  [the longest x1 44.4 us: per_device(): came = lax.all_to_all(leave, 'z', 0, 0, tiled=True)]
    all_to_all x0 -> x2, blocking collectives: none -> 56.1 us  [the longest x1 31.8 us: per_device(): came = lax.all_to_all(near, 'z', 0, 0, tiled=True, axis_index_groups=same)]
    all_to_all x2 -> x0, starting transfers between devices: 14.9 us -> none  [the longest x1 8.13 us: per_device(): came = lax.all_to_all(leave, 'z', 0, 0, tiled=True)]
    ppermute x0 -> x2, waiting for transfers between devices: none -> 12.6 us  [step(): return lax.ppermute(block, ('z', 'core'), up + down)]
    ppermute x0 -> x2, starting transfers between devices: none -> 6.7 us  [step(): return lax.ppermute(block, ('z', 'core'), up + down)]
    slice x0 -> x2, local copies, waits for them, and re-layouts: none -> 4.86 us  [the longest x1 2.65 us: per_device(): value_all = [block[:, 1].reshape(-1, HD) for block in both]]
    unnamed x27 -> x24, local copies, waits for them, and re-layouts: 8.76 us -> 4.43 us
    ppermute x3, waiting for transfers between devices: 45.6 us -> 42.1 us  [per_device(): lax.ppermute(w_mine, 'head', [(a, (a - d) % head_count) for a in range(he...]
  transfers between devices with their start and end apart: 8 -> 8, of which waited for: 6 -> 5; matrix products, arithmetic and copies ran while one was open for 7% -> 8% of each run, Pallas kernels for 1% -> 1%
where the time goes in v5:
time: 242 us; the launch traced here: 241 us
  waiting for transfers between devices  80.1 us (33%)
  blocking collectives  68.6 us (28%)
  Pallas kernels  25.7 us (11%)
  starting transfers between devices  20.8 us (9%)
  local copies, waits for them, and re-layouts  17.7 us (7%)
  between operations  14.3 us (6%)
  other arithmetic  13.1 us (5%)
    ppermute x3, waiting for transfers between devices, per_device(): lax.ppermute(w_mine, 'head', [(a, (a - d) % head_count) for a in range(he...  42.1 us
    all_to_all x1, blocking collectives, per_device(): came = lax.all_to_all(near, 'z', 0, 0, tiled=True, axis_index_groups=same)  31.8 us
    all_gather x1, waiting for transfers between devices, per_device(): lax.all_gather(mine, 'z', axis=0, tiled=True)  25.4 us
    all_to_all x1, blocking collectives, per_device(): slots = lax.all_to_all(slots, 'exp', 0, 0, tiled=True)  24.3 us
    pallas_call x1, Pallas kernels, expert_block(): pl.pallas_call(expert_kernel, in_specs=[pl.BlockSpec(memory_space=pltpu.S...  16 us
    ppermute x2, waiting for transfers between devices, step(): return lax.ppermute(block, ('z', 'core'), up + down)  12.6 us
    all_to_all x1, blocking collectives, per_device(): lax.all_to_all(at_heads, 'head', 0, 0, tiled=True).reshape(tok_rows, HD)  12.5 us
    ppermute x3, starting transfers between devices, per_device(): lax.ppermute(w_mine, 'head', [(a, (a - d) % head_count) for a in range(he...  10.2 us
  transfers between devices with their start and end apart: 8, of which 5 were waited for; matrix products, arithmetic and copies ran while one was open for 8% of the time, Pallas kernels for 1%

profile of v5, /device:TPU:64, one launch (start us, length us, event | category | flops | bytes accessed | tf_op | source)
XLA Modules:
  0.0 240.9 jit_solution(1510238096142664568)
XLA Ops:
  7.2 0.9 compare_reduce_fusion
  8.2 0.2 copy-done
  8.4 1.2 fusion
  9.7 0.7 convert_element_type.83
  10.4 0.8 reshape.776
  11.2 0.8 reshape.777
  12.0 0.8 select_reduce_fusion
  12.7 0.2 convolution_convert_fusion
  13.0 0.3 convolution_convert_fusion.1
  13.3 0.8 pad_maximum_fusion.1
  14.1 1.8 pad_bitcast_fusion.2
  16.0 0.5 copy-done.4
  16.5 0.5 pad_bitcast_fusion
  17.0 3.1 %pad_maximum_fusion.own_hbm = bf16[3,256,4096]{2,1,0:T(8,128)(2,1)} fusion(bf16[1,256,4096]{2,1,0:T(8,128)(2,1)S(1)} %get-tuple-element.88, bf16[1,256,4096]{2,1,0:T(8,128)(2,1)S(1)} %get-tuple-element.89, bf16[1,256,4096]{2,1,0:T(8,128)(2,1)S(1)} %pad_bitcast_fusion.2), kind=kLoop, calls=%fused_computation | loop fusion | flops 6291456 | bytes 12582912 | tf_op jit(solution)/shard_map/stack | solution.py:256
  20.2 1.9 collective-permute-start
  22.1 4.7 %collective-permute-start.1 = (bf16[128,4096]{1,0:T(8,128)(2,1)S(1)}, bf16[128,4096]{1,0:T(8,128)(2,1)S(1)}, u32[]{:S(2)}, u32[]{:S(2)}) collective-permute-start(bf16[128,4096]{1,0:T(8,128)(2,1)S(1)} %copy-done.5), channel_id=1, source_target_pairs={{0,3},{1,0},{2,1},{3,2},{4,7},{5,4},{6,5},{7,6},{8,11},{9,8},{10,9... | collective-permute-start | bytes 3145736 | tf_op jit(solution)/shard_map/ppermute | solution.py:259
  26.8 2.7 %collective-permute-start.2 = (bf16[128,4096]{1,0:T(8,128)(2,1)S(1)}, bf16[128,4096]{1,0:T(8,128)(2,1)}, u32[]{:S(2)}, u32[]{:S(2)}) collective-permute-start(bf16[128,4096]{1,0:T(8,128)(2,1)S(1)} %copy-done.5), channel_id=1, source_target_pairs={{0,2},{1,3},{2,0},{3,1},{4,6},{5,7},{6,4},{7,5},{8,10},{9,11},{10,... | collective-permute-start | bytes 3145736 | tf_op jit(solution)/shard_map/ppermute | solution.py:259
  29.5 2.8 %collective-permute-start.3 = (bf16[128,4096]{1,0:T(8,128)(2,1)S(1)}, bf16[128,4096]{1,0:T(8,128)(2,1)}, u32[]{:S(2)}, u32[]{:S(2)}) collective-permute-start(bf16[128,4096]{1,0:T(8,128)(2,1)S(1)} %copy-done.5), channel_id=1, source_target_pairs={{0,1},{1,2},{2,3},{3,0},{4,5},{5,6},{6,7},{7,4},{8,9},{9,10},{10,1... | collective-permute-start | bytes 3145736 | tf_op jit(solution)/shard_map/ppermute | solution.py:259
  33.3 0.6 broadcast_in_dim.10.gain_ref
  34.0 0.7 reshape.779
  34.7 0.6 pad_add_fusion.order_ref
  35.2 0.6 and_select_fusion.5.fold_ref
  35.8 0.1 fusion.8.kpos_ref
  36.0 36.4 %collective-permute-done.1.rest_1_ = bf16[128,4096]{1,0:T(8,128)(2,1)S(1)} collective-permute-done((bf16[128,4096]{1,0:T(8,128)(2,1)S(1)}, bf16[128,4096]{1,0:T(8,128)(2,1)S(1)}, u32[]{:S(2)}, u32[]{:S(2)}) %collective-permute-start.1) | collective-permute-done | bytes 1048608 | tf_op jit(solution)/shard_map/ppermute | solution.py:259
  72.3 5.7 %collective-permute-done.3.rest_3_ = bf16[128,4096]{1,0:T(8,128)(2,1)} collective-permute-done((bf16[128,4096]{1,0:T(8,128)(2,1)S(1)}, bf16[128,4096]{1,0:T(8,128)(2,1)}, u32[]{:S(2)}, u32[]{:S(2)}) %collective-permute-start.3) | collective-permute-done | bytes 1048608 | tf_op jit(solution)/shard_map/ppermute | solution.py:259
  78.0 25.4 %all-gather.2.cloned.1.call-done = bf16[512,4096]{1,0:T(8,128)(2,1)} async-done(((bf16[32,4096]{1,0:T(8,128)(2,1)}), bf16[512,4096]{1,0:T(8,128)(2,1)}) %all-gather.2.cloned.1.call-update) | async-done | bytes 4194320 | tf_op jit(solution)/shard_map/all_gather | solution.py:251
  103.4 16.0 %expert_block.1 = (bf16[8,48,1024]{2,1,0:T(8,128)(2,1)}, bf16[8,48,1024]{2,1,0:T(8,128)(2,1)}) custom-call(s32[16]{0:T(128)} %pad_add_fusion.order_ref, bf16[16,32,4096]{2,1,0:T(8,128)(2,1)} %bitcast.37, bf16[3,256,4096]{2,1,0:T(8,128)(2,1)} %pad_maximum_fusion.own_hbm, bf16[3,256,4096]{2,1,0:T(8,128)(2,1)} %collective-permute-done.other_hbm), custom_call_target="tpu_custom_call" | custom-call | flops 5368709120 | bytes 16777216 | tf_op jit(solution)/shard_map/expert_block/pallas_call | solution.py:82
  119.5 2.2 slice.69
  121.7 1.5 copy.24
  123.2 2.0 collective-permute-start.6
  125.2 3.1 %collective-permute-start.4 = (bf16[8,48,1024]{2,1,0:T(8,128)(2,1)}, bf16[8,48,1024]{2,1,0:T(8,128)(2,1)}, u32[]{:S(2)}, u32[]{:S(2)}) collective-permute-start(bf16[8,48,1024]{2,1,0:T(8,128)(2,1)} %get-tuple-element.38), channel_id=1, source_target_pairs={{0,64},{64,128},{128,192},{192,256},{256,320},{320,384},{384,448},... | collective-permute-start | bytes 2359304 | tf_op jit(solution)/shard_map/ppermute | solution.py:312
  128.3 2.2 slice_bitcast_fusion
  130.5 0.5 reshape_squeeze.12.key0
  131.0 0.5 reshape_squeeze.14.value0
  131.5 7.9 %collective-permute-done.4 = bf16[8,48,1024]{2,1,0:T(8,128)(2,1)} collective-permute-done((bf16[8,48,1024]{2,1,0:T(8,128)(2,1)}, bf16[8,48,1024]{2,1,0:T(8,128)(2,1)}, u32[]{:S(2)}, u32[]{:S(2)}) %collective-permute-start.4) | collective-permute-done | bytes 786464 | tf_op jit(solution)/shard_map/ppermute | solution.py:312
  139.4 1.9 add_convert_fusion.1
  141.3 3.6 %collective-permute-start.5 = (bf16[4,48,1024]{2,1,0:T(8,128)(2,1)}, bf16[4,48,1024]{2,1,0:T(8,128)(2,1)}, u32[]{:S(2)}, u32[]{:S(2)}) collective-permute-start(bf16[4,48,1024]{2,1,0:T(8,128)(2,1)} %add_convert_fusion.1), channel_id=1, source_target_pairs={{0,128},{64,192},{128,256},{192,320},{256,384},{320,448},{384,512}... | collective-permute-start | bytes 1179656 | tf_op jit(solution)/shard_map/ppermute | solution.py:312
  144.9 2.6 %fusion.32 = (bf16[16,1,4,4096]{3,2,0,1:T(4,128)(2,1)}, bf16[16,1,4,4096]{3,2,0,1:T(4,128)(2,1)S(1)}) fusion(bf16[16,2,4,4096]{3,2,0,1:T(4,128)(2,1)} %collective-permute-done.6), kind=kLoop, calls=%fused_computation.100 | loop fusion | bytes 2097152 | tf_op jit(solution)/shard_map/slice | solution.py:286
  147.6 0.5 reshape_squeeze.13.key1
  148.1 1.6 reshape_squeeze.15.value1
  149.7 1.8 attention_early.1
  151.6 4.7 %collective-permute-done.5 = bf16[4,48,1024]{2,1,0:T(8,128)(2,1)} collective-permute-done((bf16[4,48,1024]{2,1,0:T(8,128)(2,1)}, bf16[4,48,1024]{2,1,0:T(8,128)(2,1)}, u32[]{:S(2)}, u32[]{:S(2)}) %collective-permute-start.5) | collective-permute-done | bytes 393248 | tf_op jit(solution)/shard_map/ppermute | solution.py:312
  156.3 1.3 add_convert_fusion
  157.6 31.8 %all_to_all.15.in_ref = bf16[4,48,1024]{2,1,0:T(8,128)(2,1)S(1)} all-to-all(bf16[4,48,1024]{2,1,0:T(8,128)(2,1)S(1)} %add_convert_fusion), channel_id=1, replica_groups={{0,256,512,768},{64,320,576,832},{128,384,640,896},{192,448,704,960},{1..., dimensions={0} | all-to-all | bytes 786432 | tf_op jit(solution)/shard_map/all_to_all | solution.py:323
  189.5 24.3 %all_to_all.16.slots_ref = bf16[8,48,1024]{2,1,0:T(8,128)(2,1)} all-to-all(bf16[8,48,1024]{2,1,0:T(8,128)(2,1)S(1)} %slot_sum.1), channel_id=1, replica_groups=mesh['z'=16,'core'=2,'exp'=8,'head'=4] {'exp'}, dimensions={0} | all-to-all | bytes 1572864 | tf_op jit(solution)/shard_map/all_to_all | solution.py:331
  213.8 6.1 %token_rows.1 = (bf16[32,4096]{1,0:T(8,128)(2,1)}, bf16[4,32,128]{2,1,0:T(8,128)(2,1)}) custom-call(s32[1]{0:T(128)} %bitcast.head_ref, bf16[8,48,1024]{2,1,0:T(8,128)(2,1)} %all_to_all.16.slots_ref, f32[384,32]{1,0:T(8,128)} %bitcast.40, s32[1,384]{1,0:T(1,128)} %and_select_fusion.5.fold_ref, bf16[32,4096]{1,0:T(8,128)(2,1)} %copy-done.7, ...), custom_call_target="tpu_custom_call" | custom-call | flops 234881024 | bytes 4194304 | tf_op jit(solution)/shard_map/token_rows/pallas_call | solution.py:177
  219.9 12.5 %all_to_all.17 = bf16[4,32,128]{2,1,0:T(8,128)(2,1)S(1)} all-to-all(bf16[4,32,128]{2,1,0:T(8,128)(2,1)} %get-tuple-element.53), channel_id=1, replica_groups=mesh['z'=16,'core'=2,'exp'=8,'head'=4] {'head'}, dimensions={0} | all-to-all | bytes 65536 | tf_op jit(solution)/shard_map/all_to_all | solution.py:354
  232.4 1.7 attention_late.1
  (47 shorter events, 1.4 us)
Async XLA Ops:
  7.2 1.2 copy-start
  7.2 96.2 %all-gather.2.cloned.1.call-start = ((), (), s32[]{:S(2)}) async-start(), calls=%async_computation.3 | async-start | bytes 4456448 | tf_op jit(solution)/shard_map/all_gather | solution.py:251
  8.4 7.5 %copy-start.2 = (bf16[32,4096]{1,0:T(8,128)(2,1)}, bf16[32,4096]{1,0:T(8,128)(2,1)S(1)}, u32[]{:S(2)}) copy-start(bf16[32,4096]{1,0:T(8,128)(2,1)S(1)} %constant_dynamic-slice_fusion.grad_ref) | copy-start | bytes 786436
  9.7 3.6 %copy-start.7 = (bf16[32,4096]{1,0:T(8,128)(2,1)}, bf16[32,4096]{1,0:T(8,128)(2,1)S(1)}, u32[]{:S(2)}) copy-start(bf16[32,4096]{1,0:T(8,128)(2,1)S(1)} %get-tuple-element.45.resid_ref) | copy-start | bytes 786436
  14.1 1.9 copy-start.3
  14.1 2.4 copy-start.4
  17.0 5.1 %copy-start.5 = (bf16[128,4096]{1,0:T(8,128)(2,1)S(1)}, bf16[128,4096]{1,0:T(8,128)(2,1)}, u32[]{:S(2)}) copy-start(bf16[128,4096]{1,0:T(8,128)(2,1)} %rest_0_) | copy-start | bytes 3145732
  17.0 16.3 %copy-start.10 = (bf16[4096]{0:T(1024)(128)(2,1)S(1)}, bf16[4096]{0:T(1024)(128)(2,1)}, u32[]{:S(2)}) copy-start(bf16[4096]{0:T(1024)(128)(2,1)} %param.14) | copy-start | bytes 24580
  20.2 57.9 %collective-permute-start = (bf16[3,256,4096]{2,1,0:T(8,128)(2,1)}, bf16[3,256,4096]{2,1,0:T(8,128)(2,1)}, u32[]{:S(2)}, u32[]{:S(2)}) collective-permute-start(bf16[3,256,4096]{2,1,0:T(8,128)(2,1)} %pad_maximum_fusion.own_hbm), channel_id=1, source_target_pairs={{0,32},{32,0},{1,33},{33,1},{2,34},{34,2},{3,35},{35,3},{4,36},{36... | collective-permute-start | bytes 18874376 | tf_op jit(solution)/shard_map/ppermute | solution.py:190
  22.1 50.2 %collective-permute-start.1 = (bf16[128,4096]{1,0:T(8,128)(2,1)S(1)}, bf16[128,4096]{1,0:T(8,128)(2,1)S(1)}, u32[]{:S(2)}, u32[]{:S(2)}) collective-permute-start(bf16[128,4096]{1,0:T(8,128)(2,1)S(1)} %copy-done.5), channel_id=1, source_target_pairs={{0,3},{1,0},{2,1},{3,2},{4,7},{5,4},{6,5},{7,6},{8,11},{9,8},{10,9... | collective-permute-start | bytes 3145736 | tf_op jit(solution)/shard_map/ppermute | solution.py:259
  26.8 45.6 %collective-permute-start.2 = (bf16[128,4096]{1,0:T(8,128)(2,1)S(1)}, bf16[128,4096]{1,0:T(8,128)(2,1)}, u32[]{:S(2)}, u32[]{:S(2)}) collective-permute-start(bf16[128,4096]{1,0:T(8,128)(2,1)S(1)} %copy-done.5), channel_id=1, source_target_pairs={{0,2},{1,3},{2,0},{3,1},{4,6},{5,7},{6,4},{7,5},{8,10},{9,11},{10,... | collective-permute-start | bytes 3145736 | tf_op jit(solution)/shard_map/ppermute | solution.py:259
  29.5 48.5 %collective-permute-start.3 = (bf16[128,4096]{1,0:T(8,128)(2,1)S(1)}, bf16[128,4096]{1,0:T(8,128)(2,1)}, u32[]{:S(2)}, u32[]{:S(2)}) collective-permute-start(bf16[128,4096]{1,0:T(8,128)(2,1)S(1)} %copy-done.5), channel_id=1, source_target_pairs={{0,1},{1,2},{2,3},{3,0},{4,5},{5,6},{6,7},{7,4},{8,9},{9,10},{10,1... | collective-permute-start | bytes 3145736 | tf_op jit(solution)/shard_map/ppermute | solution.py:259
  72.3 47.1 %copy-start.6 = (bf16[128,4096]{1,0:T(8,128)(2,1)}, bf16[128,4096]{1,0:T(8,128)(2,1)S(1)}, u32[]{:S(2)}) copy-start(bf16[128,4096]{1,0:T(8,128)(2,1)S(1)} %collective-permute-done.1.rest_1_) | copy-start | bytes 3145732
  123.2 16.3 %copy-start.8 = (bf16[8,48,1024]{2,1,0:T(8,128)(2,1)S(1)}, bf16[8,48,1024]{2,1,0:T(8,128)(2,1)}, u32[]{:S(2)}) copy-start(bf16[8,48,1024]{2,1,0:T(8,128)(2,1)} %get-tuple-element.36) | copy-start | bytes 2359300
  123.2 21.8 %collective-permute-start.6 = (bf16[16,2,4,4096]{3,2,0,1:T(4,128)(2,1)}, bf16[16,2,4,4096]{3,2,0,1:T(4,128)(2,1)}, u32[]{:S(2)}, u32[]{:S(2)}) collective-permute-start(bf16[16,2,4,4096]{3,2,0,1:T(4,128)(2,1)} %copy.24), channel_id=1, source_target_pairs={{0,32},{32,0},{1,33},{33,1},{2,34},{34,2},{3,35},{35,3},{4,36},{36... | collective-permute-start | bytes 3145736 | tf_op jit(solution)/shard_map/ppermute | solution.py:190
  125.2 14.2 %collective-permute-start.4 = (bf16[8,48,1024]{2,1,0:T(8,128)(2,1)}, bf16[8,48,1024]{2,1,0:T(8,128)(2,1)}, u32[]{:S(2)}, u32[]{:S(2)}) collective-permute-start(bf16[8,48,1024]{2,1,0:T(8,128)(2,1)} %get-tuple-element.38), channel_id=1, source_target_pairs={{0,64},{64,128},{128,192},{192,256},{256,320},{320,384},{384,448},... | collective-permute-start | bytes 2359304 | tf_op jit(solution)/shard_map/ppermute | solution.py:312
  141.3 8.4 %copy-start.1 = (bf16[128,128]{1,0:T(8,128)(2,1)S(1)}, bf16[128,128]{1,0:T(8,128)(2,1)}, u32[]{:S(2)}) copy-start(bf16[128,128]{1,0:T(8,128)(2,1)} %query_ref.1) | copy-start | bytes 98308
  141.3 15.0 %collective-permute-start.5 = (bf16[4,48,1024]{2,1,0:T(8,128)(2,1)}, bf16[4,48,1024]{2,1,0:T(8,128)(2,1)}, u32[]{:S(2)}, u32[]{:S(2)}) collective-permute-start(bf16[4,48,1024]{2,1,0:T(8,128)(2,1)} %add_convert_fusion.1), channel_id=1, source_target_pairs={{0,128},{64,192},{128,256},{192,320},{256,384},{320,448},{384,512}... | collective-permute-start | bytes 1179656 | tf_op jit(solution)/shard_map/ppermute | solution.py:312
  149.7 6.6 %copy-start.9 = (bf16[8,48,1024]{2,1,0:T(8,128)(2,1)S(1)}, bf16[8,48,1024]{2,1,0:T(8,128)(2,1)}, u32[]{:S(2)}) copy-start(bf16[8,48,1024]{2,1,0:T(8,128)(2,1)} %get-tuple-element.36) | copy-start | bytes 2359300
Sparse Core Ops, SparseCore 0:
  14.2 89.1 all-gather.1

commit v6 on v3

--- a/solution.py
+++ b/solution.py
@@ -205,7 +205,16 @@
         for d in range(1, head_count)
     ]
     w_four = jnp.concatenate(w_near, axis=0)
-    weights, w_four = lax.optimization_barrier((weights, w_four))
+    picks = []
+    for expert in range(exp_count):
+        routed, position, _ = slots_of(expert)
+        picks.append((position[:, None] == slot_ids[None, :CAP]) & routed[:, None])
+    picks = jnp.stack(picks, axis=1).astype(bf16)
+    theres = []
+    for q in range(FOLD):
+        there = jnp.zeros((quarter, exp_count, FOLD, CAP), bf16).at[:, :, q].set(picks)
+        theres.append(there.reshape(quarter, -1))
+    weights, w_four, *theres = lax.optimization_barrier((weights, w_four, *theres))
 
     packed = rows.reshape(z_count, 2, ROOM, width)[:, :, CAP:]
     packed = jnp.stack([packed, core_swap(packed)], axis=0)
@@ -241,20 +250,15 @@
     left = (stay + came.astype(f32)).astype(bf16)
     same = [list(range(r, z_count, 2)) for r in range(2)]
     left = lax.all_to_all(left, "z", 0, 0, tiled=True, axis_index_groups=same)
+    left, probs, output, key_all, value_all = lax.optimization_barrier(
+        (left, probs, output, key_all, value_all)
+    )
     slots = jnp.sum(left.astype(f32), axis=0).astype(bf16)
     slots = lax.all_to_all(
         jnp.broadcast_to(slots[None], (exp_count, *slots.shape)), "exp", 0, 0, tiled=True
     )
-    picks = []
-    for expert in range(exp_count):
-        routed, position, _ = slots_of(expert)
-        picks.append((position[:, None] == slot_ids[None, :CAP]) & routed[:, None])
-    picks = jnp.stack(picks, axis=1).astype(bf16)
     flat = slots.reshape(exp_count * FOLD * CAP, -1)
-    pieces = []
-    for q in range(FOLD):
-        there = jnp.zeros((quarter, exp_count, FOLD, CAP), bf16).at[:, :, q].set(picks)
-        pieces.append(jnp.dot(there.reshape(quarter, -1), flat, preferred_element_type=f32))
+    pieces = [jnp.dot(there, flat, preferred_element_type=f32) for there in theres]
     summed = jnp.concatenate(pieces, axis=1)
     grad_quarter = norm_back(resid_full, inv_rms, grad_full, norm_gain, summed)
 

time: 237 us -> 236 us (level)
  waiting for transfers between devices: 122 us -> 113 us
  blocking collectives: 0 us -> 7.8 us
    all_to_all x1, waiting for transfers between devices: 36.2 us -> 25 us  [per_device(): left = lax.all_to_all(left, 'z', 0, 0, tiled=True, axis_index_groups=same)]
    all_to_all x0 -> x1, blocking collectives: none -> 7.8 us  [per_device(): lax.all_to_all(at_heads, 'head', 0, 0, tiled=True).reshape(tok_rows, HD)]
    all_to_all x1, waiting for transfers between devices: 14.8 us -> 21.5 us  [per_device(): lax.all_to_all(jnp.broadcast_to(slots[None], (exp_count, *slots.shape)),...]
    ppermute x3, waiting for transfers between devices: 45.7 us -> 40.3 us  [per_device(): lax.ppermute(w_mine, 'head', [(a, (a - d) % head_count) for a in range(he...]
    all_to_all x1 -> x0, starting transfers between devices: 3.26 us -> none  [per_device(): lax.all_to_all(at_heads, 'head', 0, 0, tiled=True).reshape(tok_rows, HD)]
    reshape x4, local copies, waits for them, and re-layouts: 0.83 us -> 3.62 us  [per_device(): theres.append(there.reshape(quarter, -1))]
    unnamed x19 -> x33, local copies, waits for them, and re-layouts: 5.64 us -> 5.07 us
  transfers between devices with their start and end apart: 10 -> 9, of which waited for: 7 -> 7; matrix products, arithmetic and copies ran while one was open for 13% -> 14% of each run, Pallas kernels for 1% -> 1%
where the time goes in v6:
time: 236 us; the launch traced here: 235 us
  waiting for transfers between devices  113 us (48%)
  starting transfers between devices  30.5 us (13%)
  other arithmetic  30.4 us (13%)
  Pallas kernels  17.3 us (7%)
  local copies, waits for them, and re-layouts  16.8 us (7%)
  between operations  14.4 us (6%)
  blocking collectives  7.8 us (3%)
  matrix products  4.77 us (2%)
    ppermute x3, waiting for transfers between devices, per_device(): lax.ppermute(w_mine, 'head', [(a, (a - d) % head_count) for a in range(he...  40.3 us
    all_to_all x1, waiting for transfers between devices, per_device(): left = lax.all_to_all(left, 'z', 0, 0, tiled=True, axis_index_groups=same)  25 us
    all_to_all x1, waiting for transfers between devices, per_device(): lax.all_to_all(jnp.broadcast_to(slots[None], (exp_count, *slots.shape)),...  21.5 us
    pallas_call x1, Pallas kernels, expert_block(): pl.pallas_call(expert_kernel, grid=(2,), in_specs=[pl.BlockSpec(memory_sp...  13.8 us
    another operation x2, other arithmetic, per_device(): weights = jnp.stack([own, core_swap(own)], axis=0)  13.2 us
    all_gather x1, waiting for transfers between devices, per_device(): lax.all_gather(mine, 'z', axis=0, tiled=True)  12.6 us
    ppermute x1, waiting for transfers between devices, per_device(): came = lax.ppermute(leave, ('z', 'core'), up + down)  11.1 us
    ppermute x3, starting transfers between devices, per_device(): lax.ppermute(w_mine, 'head', [(a, (a - d) % head_count) for a in range(he...  10.2 us
  transfers between devices with their start and end apart: 9, of which 7 were waited for; matrix products, arithmetic and copies ran while one was open for 14% of the time, Pallas kernels for 1%

profile of v6, /device:TPU:64, one launch (start us, length us, event | category | flops | bytes accessed | tf_op | source)
XLA Modules:
  0.0 234.9 jit_solution(306608366742260741)
XLA Ops:
  7.2 0.8 compare_reduce_fusion
  8.1 1.1 fusion.5
  9.8 0.7 convert_element_type.81
  10.5 0.8 reshape.881
  11.2 0.8 reshape.882
  12.0 0.8 fusion.40
  12.8 1.2 convolution_convert_fusion
  14.0 1.2 convolution_convert_fusion.1
  15.2 0.8 pad_maximum_fusion.4
  16.0 2.4 %pad_bitcast_fusion = (bf16[1,256,4096]{2,1,0:T(8,128)(2,1)S(1)}, bf16[1,256,4096]{2,1,0:T(8,128)(2,1)S(1)}) fusion(bf16[200,4096]{1,0:T(8,128)(2,1)} %bitcast.78, bf16[200,4096]{1,0:T(8,128)(2,1)} %bitcast.79), kind=kLoop, calls=%fused_computation.7 | loop fusion | bytes 7471104 | tf_op jit(solution)/shard_map/stack | solution.py:201
  18.7 4.9 %fusion.42 = (bf16[1,3,256,4096]{3,2,1,0:T(8,128)(2,1)}, bf16[3,256,4096]{2,1,0:T(8,128)(2,1)}) fusion(bf16[1,256,4096]{2,1,0:T(8,128)(2,1)S(1)} %get-tuple-element.118, bf16[1,256,4096]{2,1,0:T(8,128)(2,1)S(1)} %get-tuple-element.119, bf16[1,256,4096]{2,1,0:T(8,128)(2,1)S(1)} %pad_bitcast_fusion.2), kind=kLoop, calls=%fused_computation.111 | loop fusion | flops 6291456 | bytes 18874368 | tf_op jit(solution)/shard_map/stack | solution.py:202
  23.6 1.9 collective-permute-start
  25.5 4.7 %collective-permute-start.1 = (bf16[128,4096]{1,0:T(8,128)(2,1)S(1)}, bf16[128,4096]{1,0:T(8,128)(2,1)S(1)}, u32[]{:S(2)}, u32[]{:S(2)}) collective-permute-start(bf16[128,4096]{1,0:T(8,128)(2,1)S(1)} %copy-done.8), channel_id=1, source_target_pairs={{0,3},{1,0},{2,1},{3,2},{4,7},{5,4},{6,5},{7,6},{8,11},{9,8},{10,9... | collective-permute-start | bytes 3145736 | tf_op jit(solution)/shard_map/ppermute | solution.py:204
  30.2 2.7 %collective-permute-start.2 = (bf16[128,4096]{1,0:T(8,128)(2,1)S(1)}, bf16[128,4096]{1,0:T(8,128)(2,1)S(1)}, u32[]{:S(2)}, u32[]{:S(2)}) collective-permute-start(bf16[128,4096]{1,0:T(8,128)(2,1)S(1)} %copy-done.8), channel_id=1, source_target_pairs={{0,2},{1,3},{2,0},{3,1},{4,6},{5,7},{6,4},{7,5},{8,10},{9,11},{10,... | collective-permute-start | bytes 3145736 | tf_op jit(solution)/shard_map/ppermute | solution.py:204
  32.9 2.8 %collective-permute-start.3 = (bf16[128,4096]{1,0:T(8,128)(2,1)S(1)}, bf16[128,4096]{1,0:T(8,128)(2,1)}, u32[]{:S(2)}, u32[]{:S(2)}) collective-permute-start(bf16[128,4096]{1,0:T(8,128)(2,1)S(1)} %copy-done.8), channel_id=1, source_target_pairs={{0,1},{1,2},{2,3},{3,0},{4,5},{5,6},{6,7},{7,4},{8,9},{9,10},{10,1... | collective-permute-start | bytes 3145736 | tf_op jit(solution)/shard_map/ppermute | solution.py:204
  36.7 0.7 fusion.44
  37.5 1.6 reshape.883
  39.0 0.7 reshape.884
  40.4 0.7 reshape.886
  41.1 34.6 %collective-permute-done.1 = bf16[128,4096]{1,0:T(8,128)(2,1)S(1)} collective-permute-done((bf16[128,4096]{1,0:T(8,128)(2,1)S(1)}, bf16[128,4096]{1,0:T(8,128)(2,1)S(1)}, u32[]{:S(2)}, u32[]{:S(2)}) %collective-permute-start.1) | collective-permute-done | bytes 1048608 | tf_op jit(solution)/shard_map/ppermute | solution.py:204
  75.7 5.7 %collective-permute-done.3 = bf16[128,4096]{1,0:T(8,128)(2,1)} collective-permute-done((bf16[128,4096]{1,0:T(8,128)(2,1)S(1)}, bf16[128,4096]{1,0:T(8,128)(2,1)}, u32[]{:S(2)}, u32[]{:S(2)}) %collective-permute-start.3) | collective-permute-done | bytes 1048608 | tf_op jit(solution)/shard_map/ppermute | solution.py:204
  81.4 3.2 %pad_maximum_fusion.2 = bf16[512,4096]{1,0:T(8,128)(2,1)} fusion(bf16[128,4096]{1,0:T(8,128)(2,1)} %collective-permute-done.3, bf16[128,4096]{1,0:T(8,128)(2,1)S(1)} %collective-permute-done.2, bf16[128,4096]{1,0:T(8,128)(2,1)S(1)} %collective-permute-done.1, bf16[128,4096]{1,0:T(8,128)(2,1)S(1)} %copy-done.8), kind=kLoop, calls=%fused_computation.4 | loop fusion | flops 16777216 | bytes 8388608 | tf_op jit(solution)/shard_map/concatenate | solution.py:207
  84.6 8.4 %pad_maximum_fusion.w_ref = bf16[2,3,256,4096]{3,2,1,0:T(8,128)(2,1)} fusion(bf16[1,3,256,4096]{3,2,1,0:T(8,128)(2,1)} %bitcast.9, bf16[1,3,256,4096]{3,2,1,0:T(8,128)(2,1)S(1)} %copy-done.3), kind=kLoop, calls=%fused_computation | loop fusion | flops 6291456 | bytes 25165824 | tf_op jit(solution)/shard_map/stack | solution.py:202
  93.0 12.6 %all-gather.2.cloned.1.call-done = bf16[512,4096]{1,0:T(8,128)(2,1)} async-done(((bf16[32,4096]{1,0:T(8,128)(2,1)}), bf16[512,4096]{1,0:T(8,128)(2,1)}) %all-gather.2.cloned.1.call-update) | async-done | bytes 4194320 | tf_op jit(solution)/shard_map/all_gather | solution.py:196
  105.6 13.8 %expert_block.1 = (f32[8,48,1024]{2,1,0:T(8,128)S(1)}, bf16[8,48,1024]{2,1,0:T(8,128)(2,1)S(1)}) custom-call(s32[1]{0:T(128)} %bitcast.18.bit_ref, bf16[16,32,4096]{2,1,0:T(8,128)(2,1)} %bitcast.82, bf16[2,3,256,4096]{3,2,1,0:T(8,128)(2,1)} %pad_maximum_fusion.w_ref), custom_call_target="tpu_custom_call" | custom-call | flops 5368709120 | bytes 16777216 | tf_op jit(solution)/shard_map/expert_block/pallas_call | solution.py:72
  119.5 2.7 %collective-permute-start.4 = (bf16[8,48,1024]{2,1,0:T(8,128)(2,1)S(1)}, bf16[8,48,1024]{2,1,0:T(8,128)(2,1)S(1)}, u32[]{:S(2)}, u32[]{:S(2)}) collective-permute-start(bf16[8,48,1024]{2,1,0:T(8,128)(2,1)S(1)} %get-tuple-element.76), channel_id=1, source_target_pairs={{0,64},{64,128},{128,192},{192,256},{256,320},{320,384},{384,448},... | collective-permute-start | bytes 2359304 | tf_op jit(solution)/shard_map/ppermute | solution.py:249
  122.2 11.1 %collective-permute-done.4 = bf16[8,48,1024]{2,1,0:T(8,128)(2,1)S(1)} collective-permute-done((bf16[8,48,1024]{2,1,0:T(8,128)(2,1)S(1)}, bf16[8,48,1024]{2,1,0:T(8,128)(2,1)S(1)}, u32[]{:S(2)}, u32[]{:S(2)}) %collective-permute-start.4) | collective-permute-done | bytes 786464 | tf_op jit(solution)/shard_map/ppermute | solution.py:249
  133.4 1.1 add_convert_fusion
  134.5 6.6 %all-to-all-start = ((bf16[8,48,1024]{2,1,0:T(8,128)(2,1)}), bf16[8,48,1024]{2,1,0:T(8,128)(2,1)}, u32[]{:S(2)}, u32[]{:S(2)}) async-start(bf16[8,48,1024]{2,1,0:T(8,128)(2,1)} %add_convert_fusion), calls=%async_computation | async-start | bytes 1572864 | tf_op jit(solution)/shard_map/all_to_all | solution.py:252
  141.1 2.7 %fusion.43 = (bf16[16,2,4,4096]{3,2,0,1:T(4,128)(2,1)S(1)}, bf16[1,16,2,4,4096]{4,3,1,0,2:T(4,128)(2,1)S(1)}) fusion(bf16[16,2,16,4096]{3,2,1,0:T(8,128)(2,1)} %bitcast.83), kind=kLoop, calls=%fused_computation.112 | loop fusion | bytes 3145728
  143.8 2.1 collective-permute-start.5
  146.1 2.3 collective-permute-done.5
  148.4 1.0 copy-done.7
  149.4 2.6 %pad_maximum_fusion.3 = (bf16[2,16,1,4,4096]{4,3,1,0,2:T(4,128)(2,1)S(1)}, bf16[2,16,1,4,4096]{4,3,1,0,2:T(4,128)(2,1)S(1)}) fusion(bf16[1,16,2,4,4096]{4,3,1,0,2:T(4,128)(2,1)} %bitcast.81, bf16[1,16,2,4,4096]{4,3,1,0,2:T(4,128)(2,1)S(1)} %get-tuple-element.103), kind=kLoop, calls=%fused_computation.14 | loop fusion | flops 1048576 | bytes 4194304 | tf_op jit(solution)/shard_map/stack | solution.py:220
  152.0 1.1 reshape_squeeze.6.key_ref
  153.1 1.1 reshape_squeeze.7.value_ref
  154.3 1.8 attention_early.1
  156.1 1.3 copy-done
  157.5 25.0 %all-to-all-done = bf16[8,48,1024]{2,1,0:T(8,128)(2,1)} async-done(((bf16[8,48,1024]{2,1,0:T(8,128)(2,1)}), bf16[8,48,1024]{2,1,0:T(8,128)(2,1)}, u32[]{:S(2)}, u32[]{:S(2)}) %all-to-all-start) | async-done | bytes 786464 | tf_op jit(solution)/shard_map/all_to_all | solution.py:252
  182.4 1.3 reduce_sum.131
  183.7 1.0 broadcast_in_dim.7
  184.7 6.9 %all-to-all-start.1 = ((bf16[8,48,1024]{2,1,0:T(8,128)(2,1)}), bf16[8,48,1024]{2,1,0:T(8,128)(2,1)S(1)}, u32[]{:S(2)}, u32[]{:S(2)}) async-start(bf16[8,48,1024]{2,1,0:T(8,128)(2,1)} %broadcast_in_dim.7), calls=%async_computation.1 | async-start | bytes 1572864 | tf_op jit(solution)/shard_map/all_to_all | solution.py:257
  191.6 21.5 %all-to-all-done.1 = bf16[8,48,1024]{2,1,0:T(8,128)(2,1)S(1)} async-done(((bf16[8,48,1024]{2,1,0:T(8,128)(2,1)}), bf16[8,48,1024]{2,1,0:T(8,128)(2,1)S(1)}, u32[]{:S(2)}, u32[]{:S(2)}) %all-to-all-start.1) | async-done | bytes 786464 | tf_op jit(solution)/shard_map/all_to_all | solution.py:257
  214.1 1.7 fusion.9
  215.8 1.2 fusion.4
  217.1 1.4 fusion
  218.5 7.8 %all_to_all.15 = bf16[4,32,128]{2,1,0:T(8,128)(2,1)S(1)} all-to-all(bf16[4,32,128]{2,1,0:T(8,128)(2,1)S(1)} %fusion.17), channel_id=1, replica_groups=mesh['z'=16,'core'=2,'exp'=8,'head'=4] {'head'}, dimensions={0} | all-to-all | bytes 65536 | tf_op jit(solution)/shard_map/all_to_all | solution.py:268
  226.3 1.7 attention_late.1
  (61 shorter events, 3.9 us)
Async XLA Ops:
  7.2 98.5 %all-gather.2.cloned.1.call-start = ((), (), s32[]{:S(2)}) async-start(), calls=%async_computation.3 | async-start | bytes 4456448 | tf_op jit(solution)/shard_map/all_gather | solution.py:196
  9.8 8.7 %copy-start.14 = (f32[32]{0:T(128)}, f32[32]{0:T(128)S(1)}, u32[]{:S(2)}) copy-start(f32[32]{0:T(128)S(1)} %get-tuple-element.109) | copy-start | bytes 388
  15.2 3.2 %copy-start.5 = (bf16[1,4096,200]{1,2,0:T(8,128)(2,1)S(1)}, bf16[1,4096,200]{1,2,0:T(8,128)(2,1)}, u32[]{:S(2)}) copy-start(bf16[1,4096,200]{1,2,0:T(8,128)(2,1)} %param.25) | copy-start | bytes 4915204
  18.7 6.8 %copy-start.8 = (bf16[128,4096]{1,0:T(8,128)(2,1)S(1)}, bf16[128,4096]{1,0:T(8,128)(2,1)}, u32[]{:S(2)}) copy-start(bf16[128,4096]{1,0:T(8,128)(2,1)} %param.28) | copy-start | bytes 3145732
  23.6 61.1 %collective-permute-start = (bf16[3,256,4096]{2,1,0:T(8,128)(2,1)}, bf16[3,256,4096]{2,1,0:T(8,128)(2,1)}, u32[]{:S(2)}, u32[]{:S(2)}) collective-permute-start(bf16[3,256,4096]{2,1,0:T(8,128)(2,1)} %get-tuple-element.99), channel_id=1, source_target_pairs={{0,32},{32,0},{1,33},{33,1},{2,34},{34,2},{3,35},{35,3},{4,36},{36... | collective-permute-start | bytes 18874376 | tf_op jit(solution)/shard_map/ppermute | solution.py:135
  25.5 50.2 %collective-permute-start.1 = (bf16[128,4096]{1,0:T(8,128)(2,1)S(1)}, bf16[128,4096]{1,0:T(8,128)(2,1)S(1)}, u32[]{:S(2)}, u32[]{:S(2)}) collective-permute-start(bf16[128,4096]{1,0:T(8,128)(2,1)S(1)} %copy-done.8), channel_id=1, source_target_pairs={{0,3},{1,0},{2,1},{3,2},{4,7},{5,4},{6,5},{7,6},{8,11},{9,8},{10,9... | collective-permute-start | bytes 3145736 | tf_op jit(solution)/shard_map/ppermute | solution.py:204
  30.2 45.6 %collective-permute-start.2 = (bf16[128,4096]{1,0:T(8,128)(2,1)S(1)}, bf16[128,4096]{1,0:T(8,128)(2,1)S(1)}, u32[]{:S(2)}, u32[]{:S(2)}) collective-permute-start(bf16[128,4096]{1,0:T(8,128)(2,1)S(1)} %copy-done.8), channel_id=1, source_target_pairs={{0,2},{1,3},{2,0},{3,1},{4,6},{5,7},{6,4},{7,5},{8,10},{9,11},{10,... | collective-permute-start | bytes 3145736 | tf_op jit(solution)/shard_map/ppermute | solution.py:204
  32.9 48.5 %collective-permute-start.3 = (bf16[128,4096]{1,0:T(8,128)(2,1)S(1)}, bf16[128,4096]{1,0:T(8,128)(2,1)}, u32[]{:S(2)}, u32[]{:S(2)}) collective-permute-start(bf16[128,4096]{1,0:T(8,128)(2,1)S(1)} %copy-done.8), channel_id=1, source_target_pairs={{0,1},{1,2},{2,3},{3,0},{4,5},{5,6},{6,7},{7,4},{8,9},{9,10},{10,1... | collective-permute-start | bytes 3145736 | tf_op jit(solution)/shard_map/ppermute | solution.py:204
  41.1 43.6 %copy-start.3 = (bf16[1,3,256,4096]{3,2,1,0:T(8,128)(2,1)S(1)}, bf16[1,3,256,4096]{3,2,1,0:T(8,128)(2,1)}, u32[]{:S(2)}) copy-start(bf16[1,3,256,4096]{3,2,1,0:T(8,128)(2,1)} %get-tuple-element.98) | copy-start | bytes 18874372
  119.5 13.9 %collective-permute-start.4 = (bf16[8,48,1024]{2,1,0:T(8,128)(2,1)S(1)}, bf16[8,48,1024]{2,1,0:T(8,128)(2,1)S(1)}, u32[]{:S(2)}, u32[]{:S(2)}) collective-permute-start(bf16[8,48,1024]{2,1,0:T(8,128)(2,1)S(1)} %get-tuple-element.76), channel_id=1, source_target_pairs={{0,64},{64,128},{128,192},{192,256},{256,320},{320,384},{384,448},... | collective-permute-start | bytes 2359304 | tf_op jit(solution)/shard_map/ppermute | solution.py:249
  134.5 47.9 %all-to-all-start = ((bf16[8,48,1024]{2,1,0:T(8,128)(2,1)}), bf16[8,48,1024]{2,1,0:T(8,128)(2,1)}, u32[]{:S(2)}, u32[]{:S(2)}) async-start(bf16[8,48,1024]{2,1,0:T(8,128)(2,1)} %add_convert_fusion), calls=%async_computation | async-start | bytes 1572864 | tf_op jit(solution)/shard_map/all_to_all | solution.py:252
  143.8 4.6 %collective-permute-start.5 = (bf16[16,2,4,4096]{3,2,0,1:T(4,128)(2,1)S(1)}, bf16[16,2,4,4096]{3,2,0,1:T(4,128)(2,1)S(1)}, u32[]{:S(2)}, u32[]{:S(2)}) collective-permute-start(bf16[16,2,4,4096]{3,2,0,1:T(4,128)(2,1)S(1)} %get-tuple-element.102), channel_id=1, source_target_pairs={{0,32},{32,0},{1,33},{33,1},{2,34},{34,2},{3,35},{35,3},{4,36},{36... | collective-permute-start | bytes 3145736 | tf_op jit(solution)/shard_map/ppermute | solution.py:135
  148.4 1.0 copy-start.7
  149.4 4.9 %copy-start.2 = (bf16[128,128]{1,0:T(8,128)(2,1)S(1)}, bf16[128,128]{1,0:T(8,128)(2,1)}, u32[]{:S(2)}) copy-start(bf16[128,128]{1,0:T(8,128)(2,1)} %query_ref.1) | copy-start | bytes 98308
  153.1 60.0 %copy-start.9 = (bf16[32,384]{0,1:T(8,128)(2,1)S(1)}, bf16[32,384]{0,1:T(8,128)(2,1)}, u32[]{:S(2)}) copy-start(bf16[32,384]{0,1:T(8,128)(2,1)} %reshape.883) | copy-start | bytes 73732
  153.1 60.2 %copy-start.10 = (bf16[32,384]{0,1:T(8,128)(2,1)S(1)}, bf16[32,384]{0,1:T(8,128)(2,1)}, u32[]{:S(2)}) copy-start(bf16[32,384]{0,1:T(8,128)(2,1)} %reshape.884) | copy-start | bytes 73732
  154.3 59.3 %copy-start.11 = (bf16[32,384]{0,1:T(8,128)(2,1)S(1)}, bf16[32,384]{0,1:T(8,128)(2,1)}, u32[]{:S(2)}) copy-start(bf16[32,384]{0,1:T(8,128)(2,1)} %reshape.885) | copy-start | bytes 73732
  154.3 59.6 %copy-start.12 = (bf16[32,384]{0,1:T(8,128)(2,1)S(1)}, bf16[32,384]{0,1:T(8,128)(2,1)}, u32[]{:S(2)}) copy-start(bf16[32,384]{0,1:T(8,128)(2,1)} %reshape.886) | copy-start | bytes 73732
  156.1 1.4 copy-start
  157.5 58.3 %copy-start.13 = (f32[32]{0:T(128)S(1)}, f32[32]{0:T(128)}, u32[]{:S(2)}) copy-start(f32[32]{0:T(128)} %get-tuple-element.108) | copy-start | bytes 388
  157.5 58.4 %copy-start.15 = (f32[32]{0:T(128)S(1)}, f32[32]{0:T(128)}, u32[]{:S(2)}) copy-start(f32[32]{0:T(128)} %copy-done.14) | copy-start | bytes 388
  184.7 28.4 %all-to-all-start.1 = ((bf16[8,48,1024]{2,1,0:T(8,128)(2,1)}), bf16[8,48,1024]{2,1,0:T(8,128)(2,1)S(1)}, u32[]{:S(2)}, u32[]{:S(2)}) async-start(bf16[8,48,1024]{2,1,0:T(8,128)(2,1)} %broadcast_in_dim.7), calls=%async_computation.1 | async-start | bytes 1572864 | tf_op jit(solution)/shard_map/all_to_all | solution.py:257
  213.1 4.0 %copy-start.4 = (bf16[512,4096]{1,0:T(8,128)(2,1)S(1)}, bf16[512,4096]{1,0:T(8,128)(2,1)}, u32[]{:S(2)}) copy-start(bf16[512,4096]{1,0:T(8,128)(2,1)} %pad_maximum_fusion.2) | copy-start | bytes 12582916
  213.6 12.7 %copy-start.1 = (f32[128,4096]{1,0:T(8,128)S(1)}, f32[128,4096]{1,0:T(8,128)}, u32[]{:S(2)}) copy-start(f32[128,4096]{1,0:T(8,128)} %copy-done) | copy-start | bytes 6291460
  217.1 10.9 %copy-start.6 = (bf16[32,4096]{1,0:T(8,128)(2,1)}, bf16[32,4096]{1,0:T(8,128)(2,1)S(1)}, u32[]{:S(2)}) copy-start(bf16[32,4096]{1,0:T(8,128)(2,1)S(1)} %fusion.4) | copy-start | bytes 786436
Sparse Core Ops, SparseCore 0:
  16.2 89.4 all-gather.1

commit v7 on v6

--- a/solution.py
+++ b/solution.py
@@ -248,11 +248,11 @@
     down = [(2 * a + 1, 2 * ((a - 1) % z_count) + 1) for a in range(z_count)]
     came = lax.ppermute(leave, ("z", "core"), up + down)
     left = (stay + came.astype(f32)).astype(bf16)
+    left, probs, output, key_all, value_all = lax.optimization_barrier(
+        (left, probs, output, key_all, value_all)
+    )
     same = [list(range(r, z_count, 2)) for r in range(2)]
     left = lax.all_to_all(left, "z", 0, 0, tiled=True, axis_index_groups=same)
-    left, probs, output, key_all, value_all = lax.optimization_barrier(
-        (left, probs, output, key_all, value_all)
-    )
     slots = jnp.sum(left.astype(f32), axis=0).astype(bf16)
     slots = lax.all_to_all(
         jnp.broadcast_to(slots[None], (exp_count, *slots.shape)), "exp", 0, 0, tiled=True

time: 236 us -> 247 us (1.047)
  blocking collectives: 7.8 us -> 55.4 us
  waiting for transfers between devices: 113 us -> 79.9 us
  starting transfers between devices: 30.5 us -> 24.1 us
    all_to_all x0 -> x1, blocking collectives: none -> 47.6 us  [per_device(): left = lax.all_to_all(left, 'z', 0, 0, tiled=True, axis_index_groups=same)]
    all_to_all x1 -> x0, waiting for transfers between devices: 25 us -> none  [per_device(): left = lax.all_to_all(left, 'z', 0, 0, tiled=True, axis_index_groups=same)]
    all_to_all x1 -> x0, starting transfers between devices: 6.62 us -> none  [per_device(): left = lax.all_to_all(left, 'z', 0, 0, tiled=True, axis_index_groups=same)]
    ppermute x1, waiting for transfers between devices: 11.1 us -> 5.31 us  [per_device(): came = lax.ppermute(leave, ('z', 'core'), up + down)]
    unnamed x33 -> x31, local copies, waits for them, and re-layouts: 5.07 us -> 5.11 us
  transfers between devices with their start and end apart: 9 -> 8, of which waited for: 7 -> 5; matrix products, arithmetic and copies ran while one was open for 14% -> 12% of each run, Pallas kernels for 1% -> 0%
where the time goes in v7:
time: 247 us; the launch traced here: 246 us
  waiting for transfers between devices  79.9 us (32%)
  blocking collectives  55.4 us (22%)
  other arithmetic  31.4 us (13%)
  starting transfers between devices  24.1 us (10%)
  local copies, waits for them, and re-layouts  19 us (8%)
  Pallas kernels  17.3 us (7%)
  between operations  14.4 us (6%)
  matrix products  4.77 us (2%)
    all_to_all x1, blocking collectives, per_device(): left = lax.all_to_all(left, 'z', 0, 0, tiled=True, axis_index_groups=same)  47.6 us
    ppermute x3, waiting for transfers between devices, per_device(): lax.ppermute(w_mine, 'head', [(a, (a - d) % head_count) for a in range(he...  40.3 us
    all_to_all x1, waiting for transfers between devices, per_device(): lax.all_to_all(jnp.broadcast_to(slots[None], (exp_count, *slots.shape)),...  21.7 us
    pallas_call x1, Pallas kernels, expert_block(): pl.pallas_call(expert_kernel, grid=(2,), in_specs=[pl.BlockSpec(memory_sp...  13.8 us
    another operation x2, other arithmetic, per_device(): weights = jnp.stack([own, core_swap(own)], axis=0)  13.2 us
    all_gather x1, waiting for transfers between devices, per_device(): lax.all_gather(mine, 'z', axis=0, tiled=True)  12.6 us
    ppermute x3, starting transfers between devices, per_device(): lax.ppermute(w_mine, 'head', [(a, (a - d) % head_count) for a in range(he...  10.2 us
    all_to_all x1, blocking collectives, per_device(): lax.all_to_all(at_heads, 'head', 0, 0, tiled=True).reshape(tok_rows, HD)  7.8 us
  transfers between devices with their start and end apart: 8, of which 5 were waited for; matrix products, arithmetic and copies ran while one was open for 12% of the time, Pallas kernels for 0%

profile of v7, /device:TPU:64, one launch (start us, length us, event | category | flops | bytes accessed | tf_op | source)
XLA Modules:
  0.0 246.2 jit_solution(6269649548523490608)
XLA Ops:
  7.2 0.8 compare_reduce_fusion
  8.1 1.1 fusion.5
  9.2 0.6 multiply_multiply_fusion
  9.8 0.7 convert_element_type.81
  10.5 0.8 reshape.881
  11.2 0.8 reshape.882
  12.0 0.8 fusion.40
  12.8 1.2 convolution_convert_fusion
  14.0 1.2 convolution_convert_fusion.1
  15.2 0.8 pad_maximum_fusion.4
  16.0 2.4 pad_bitcast_fusion
  18.7 4.9 %fusion.42 = (bf16[1,3,256,4096]{3,2,1,0:T(8,128)(2,1)}, bf16[3,256,4096]{2,1,0:T(8,128)(2,1)}) fusion(bf16[1,256,4096]{2,1,0:T(8,128)(2,1)S(1)} %get-tuple-element.118, bf16[1,256,4096]{2,1,0:T(8,128)(2,1)S(1)} %get-tuple-element.119, bf16[1,256,4096]{2,1,0:T(8,128)(2,1)S(1)} %pad_bitcast_fusion.2), kind=kLoop, calls=%fused_computation.111 | loop fusion | flops 6291456 | bytes 18874368 | tf_op jit(solution)/shard_map/stack | solution.py:202
  23.6 1.9 collective-permute-start
  25.5 4.7 %collective-permute-start.1 = (bf16[128,4096]{1,0:T(8,128)(2,1)S(1)}, bf16[128,4096]{1,0:T(8,128)(2,1)S(1)}, u32[]{:S(2)}, u32[]{:S(2)}) collective-permute-start(bf16[128,4096]{1,0:T(8,128)(2,1)S(1)} %copy-done.7), channel_id=1, source_target_pairs={{0,3},{1,0},{2,1},{3,2},{4,7},{5,4},{6,5},{7,6},{8,11},{9,8},{10,9... | collective-permute-start | bytes 3145736 | tf_op jit(solution)/shard_map/ppermute | solution.py:204
  30.2 2.7 %collective-permute-start.2 = (bf16[128,4096]{1,0:T(8,128)(2,1)S(1)}, bf16[128,4096]{1,0:T(8,128)(2,1)S(1)}, u32[]{:S(2)}, u32[]{:S(2)}) collective-permute-start(bf16[128,4096]{1,0:T(8,128)(2,1)S(1)} %copy-done.7), channel_id=1, source_target_pairs={{0,2},{1,3},{2,0},{3,1},{4,6},{5,7},{6,4},{7,5},{8,10},{9,11},{10,... | collective-permute-start | bytes 3145736 | tf_op jit(solution)/shard_map/ppermute | solution.py:204
  32.9 2.8 %collective-permute-start.3 = (bf16[128,4096]{1,0:T(8,128)(2,1)S(1)}, bf16[128,4096]{1,0:T(8,128)(2,1)}, u32[]{:S(2)}, u32[]{:S(2)}) collective-permute-start(bf16[128,4096]{1,0:T(8,128)(2,1)S(1)} %copy-done.7), channel_id=1, source_target_pairs={{0,1},{1,2},{2,3},{3,0},{4,5},{5,6},{6,7},{7,4},{8,9},{9,10},{10,1... | collective-permute-start | bytes 3145736 | tf_op jit(solution)/shard_map/ppermute | solution.py:204
  36.7 0.7 fusion.44
  37.5 1.6 reshape.883
  39.0 0.7 reshape.884
  39.7 0.7 reshape.885
  40.4 0.7 reshape.886
  41.1 34.6 %collective-permute-done.1 = bf16[128,4096]{1,0:T(8,128)(2,1)S(1)} collective-permute-done((bf16[128,4096]{1,0:T(8,128)(2,1)S(1)}, bf16[128,4096]{1,0:T(8,128)(2,1)S(1)}, u32[]{:S(2)}, u32[]{:S(2)}) %collective-permute-start.1) | collective-permute-done | bytes 1048608 | tf_op jit(solution)/shard_map/ppermute | solution.py:204
  75.7 5.7 %collective-permute-done.3 = bf16[128,4096]{1,0:T(8,128)(2,1)} collective-permute-done((bf16[128,4096]{1,0:T(8,128)(2,1)S(1)}, bf16[128,4096]{1,0:T(8,128)(2,1)}, u32[]{:S(2)}, u32[]{:S(2)}) %collective-permute-start.3) | collective-permute-done | bytes 1048608 | tf_op jit(solution)/shard_map/ppermute | solution.py:204
  81.4 3.2 %pad_maximum_fusion.2 = bf16[512,4096]{1,0:T(8,128)(2,1)} fusion(bf16[128,4096]{1,0:T(8,128)(2,1)} %collective-permute-done.3, bf16[128,4096]{1,0:T(8,128)(2,1)S(1)} %collective-permute-done.2, bf16[128,4096]{1,0:T(8,128)(2,1)S(1)} %collective-permute-done.1, bf16[128,4096]{1,0:T(8,128)(2,1)S(1)} %copy-done.7), kind=kLoop, calls=%fused_computation.4 | loop fusion | flops 16777216 | bytes 8388608 | tf_op jit(solution)/shard_map/concatenate | solution.py:207
  84.6 8.4 %pad_maximum_fusion.w_ref = bf16[2,3,256,4096]{3,2,1,0:T(8,128)(2,1)} fusion(bf16[1,3,256,4096]{3,2,1,0:T(8,128)(2,1)} %bitcast.9, bf16[1,3,256,4096]{3,2,1,0:T(8,128)(2,1)S(1)} %copy-done.3), kind=kLoop, calls=%fused_computation | loop fusion | flops 6291456 | bytes 25165824 | tf_op jit(solution)/shard_map/stack | solution.py:202
  93.0 12.6 %all-gather.2.cloned.1.call-done = bf16[512,4096]{1,0:T(8,128)(2,1)} async-done(((bf16[32,4096]{1,0:T(8,128)(2,1)}), bf16[512,4096]{1,0:T(8,128)(2,1)}) %all-gather.2.cloned.1.call-update) | async-done | bytes 4194320 | tf_op jit(solution)/shard_map/all_gather | solution.py:196
  105.6 13.8 %expert_block.1 = (f32[8,48,1024]{2,1,0:T(8,128)S(1)}, bf16[8,48,1024]{2,1,0:T(8,128)(2,1)S(1)}) custom-call(s32[1]{0:T(128)} %bitcast.18.bit_ref, bf16[16,32,4096]{2,1,0:T(8,128)(2,1)} %bitcast.81, bf16[2,3,256,4096]{3,2,1,0:T(8,128)(2,1)} %pad_maximum_fusion.w_ref), custom_call_target="tpu_custom_call" | custom-call | flops 5368709120 | bytes 16777216 | tf_op jit(solution)/shard_map/expert_block/pallas_call | solution.py:72
  119.5 2.7 %collective-permute-start.4 = (bf16[8,48,1024]{2,1,0:T(8,128)(2,1)S(1)}, bf16[8,48,1024]{2,1,0:T(8,128)(2,1)}, u32[]{:S(2)}, u32[]{:S(2)}) collective-permute-start(bf16[8,48,1024]{2,1,0:T(8,128)(2,1)S(1)} %get-tuple-element.76), channel_id=1, source_target_pairs={{0,64},{64,128},{128,192},{192,256},{256,320},{320,384},{384,448},... | collective-permute-start | bytes 2359304 | tf_op jit(solution)/shard_map/ppermute | solution.py:249
  122.2 3.7 %fusion.43 = (bf16[16,2,4,4096]{3,2,0,1:T(4,128)(2,1)}, bf16[1,16,2,4,4096]{4,3,1,0,2:T(4,128)(2,1)S(1)}) fusion(bf16[16,2,16,4096]{3,2,1,0:T(8,128)(2,1)} %bitcast.82), kind=kLoop, calls=%fused_computation.112 | loop fusion | bytes 3145728
  125.9 2.1 collective-permute-start.5
  128.2 5.3 %collective-permute-done.4 = bf16[8,48,1024]{2,1,0:T(8,128)(2,1)} collective-permute-done((bf16[8,48,1024]{2,1,0:T(8,128)(2,1)S(1)}, bf16[8,48,1024]{2,1,0:T(8,128)(2,1)}, u32[]{:S(2)}, u32[]{:S(2)}) %collective-permute-start.4) | collective-permute-done | bytes 786464 | tf_op jit(solution)/shard_map/ppermute | solution.py:249
  133.5 2.3 add_convert_fusion
  135.7 3.6 %pad_maximum_fusion.3 = (bf16[2,16,1,4,4096]{4,3,1,0,2:T(4,128)(2,1)}, bf16[2,16,1,4,4096]{4,3,1,0,2:T(4,128)(2,1)}) fusion(bf16[1,16,2,4,4096]{4,3,1,0,2:T(4,128)(2,1)} %bitcast.23, bf16[1,16,2,4,4096]{4,3,1,0,2:T(4,128)(2,1)S(1)} %get-tuple-element.103), kind=kLoop, calls=%fused_computation.14 | loop fusion | flops 1048576 | bytes 4194304 | tf_op jit(solution)/shard_map/stack | solution.py:220
  139.3 2.1 reshape_squeeze.6.key_ref
  141.5 2.2 reshape_squeeze.7.value_ref
  143.7 1.8 attention_early.1
  145.6 1.3 copy-done
  146.9 47.6 %all_to_all.15 = bf16[8,48,1024]{2,1,0:T(8,128)(2,1)S(1)} all-to-all(bf16[8,48,1024]{2,1,0:T(8,128)(2,1)} %add_convert_fusion), channel_id=1, replica_groups={{0,128,256,384,512,640,768,896},{64,192,320,448,576,704,832,960},{1,129..., dimensions={0} | all-to-all | bytes 1572864 | tf_op jit(solution)/shard_map/all_to_all | solution.py:255
  194.6 1.0 broadcast_in_dim.7
  195.6 7.1 %all-to-all-start.1 = ((bf16[8,48,1024]{2,1,0:T(8,128)(2,1)}), bf16[8,48,1024]{2,1,0:T(8,128)(2,1)S(1)}, u32[]{:S(2)}, u32[]{:S(2)}) async-start(bf16[8,48,1024]{2,1,0:T(8,128)(2,1)} %broadcast_in_dim.7), calls=%async_computation.1 | async-start | bytes 1572864 | tf_op jit(solution)/shard_map/all_to_all | solution.py:257
  202.8 21.7 %all-to-all-done.1 = bf16[8,48,1024]{2,1,0:T(8,128)(2,1)S(1)} async-done(((bf16[8,48,1024]{2,1,0:T(8,128)(2,1)}), bf16[8,48,1024]{2,1,0:T(8,128)(2,1)S(1)}, u32[]{:S(2)}, u32[]{:S(2)}) %all-to-all-start.1) | async-done | bytes 786464 | tf_op jit(solution)/shard_map/all_to_all | solution.py:257
  224.7 0.3 fusion.46
  225.2 0.3 fusion.48
  225.5 1.7 fusion.9
  227.2 1.2 fusion.4
  228.5 1.4 fusion
  229.9 7.8 %all_to_all.16 = bf16[4,32,128]{2,1,0:T(8,128)(2,1)S(1)} all-to-all(bf16[4,32,128]{2,1,0:T(8,128)(2,1)S(1)} %fusion.17), channel_id=1, replica_groups=mesh['z'=16,'core'=2,'exp'=8,'head'=4] {'head'}, dimensions={0} | all-to-all | bytes 65536 | tf_op jit(solution)/shard_map/all_to_all | solution.py:268
  237.7 1.7 attention_late.1
  (58 shorter events, 2.3 us)
Async XLA Ops:
  7.2 98.5 %all-gather.2.cloned.1.call-start = ((), (), s32[]{:S(2)}) async-start(), calls=%async_computation.3 | async-start | bytes 4456448 | tf_op jit(solution)/shard_map/all_gather | solution.py:196
  9.8 8.7 %copy-start.13 = (f32[32]{0:T(128)}, f32[32]{0:T(128)S(1)}, u32[]{:S(2)}) copy-start(f32[32]{0:T(128)S(1)} %get-tuple-element.109) | copy-start | bytes 388
  15.2 3.2 %copy-start.5 = (bf16[1,4096,200]{1,2,0:T(8,128)(2,1)S(1)}, bf16[1,4096,200]{1,2,0:T(8,128)(2,1)}, u32[]{:S(2)}) copy-start(bf16[1,4096,200]{1,2,0:T(8,128)(2,1)} %param.25) | copy-start | bytes 4915204
  18.7 6.8 %copy-start.7 = (bf16[128,4096]{1,0:T(8,128)(2,1)S(1)}, bf16[128,4096]{1,0:T(8,128)(2,1)}, u32[]{:S(2)}) copy-start(bf16[128,4096]{1,0:T(8,128)(2,1)} %param.28) | copy-start | bytes 3145732
  23.6 61.1 %collective-permute-start = (bf16[3,256,4096]{2,1,0:T(8,128)(2,1)}, bf16[3,256,4096]{2,1,0:T(8,128)(2,1)}, u32[]{:S(2)}, u32[]{:S(2)}) collective-permute-start(bf16[3,256,4096]{2,1,0:T(8,128)(2,1)} %get-tuple-element.99), channel_id=1, source_target_pairs={{0,32},{32,0},{1,33},{33,1},{2,34},{34,2},{3,35},{35,3},{4,36},{36... | collective-permute-start | bytes 18874376 | tf_op jit(solution)/shard_map/ppermute | solution.py:135
  25.5 50.2 %collective-permute-start.1 = (bf16[128,4096]{1,0:T(8,128)(2,1)S(1)}, bf16[128,4096]{1,0:T(8,128)(2,1)S(1)}, u32[]{:S(2)}, u32[]{:S(2)}) collective-permute-start(bf16[128,4096]{1,0:T(8,128)(2,1)S(1)} %copy-done.7), channel_id=1, source_target_pairs={{0,3},{1,0},{2,1},{3,2},{4,7},{5,4},{6,5},{7,6},{8,11},{9,8},{10,9... | collective-permute-start | bytes 3145736 | tf_op jit(solution)/shard_map/ppermute | solution.py:204
  30.2 45.6 %collective-permute-start.2 = (bf16[128,4096]{1,0:T(8,128)(2,1)S(1)}, bf16[128,4096]{1,0:T(8,128)(2,1)S(1)}, u32[]{:S(2)}, u32[]{:S(2)}) collective-permute-start(bf16[128,4096]{1,0:T(8,128)(2,1)S(1)} %copy-done.7), channel_id=1, source_target_pairs={{0,2},{1,3},{2,0},{3,1},{4,6},{5,7},{6,4},{7,5},{8,10},{9,11},{10,... | collective-permute-start | bytes 3145736 | tf_op jit(solution)/shard_map/ppermute | solution.py:204
  32.9 48.5 %collective-permute-start.3 = (bf16[128,4096]{1,0:T(8,128)(2,1)S(1)}, bf16[128,4096]{1,0:T(8,128)(2,1)}, u32[]{:S(2)}, u32[]{:S(2)}) collective-permute-start(bf16[128,4096]{1,0:T(8,128)(2,1)S(1)} %copy-done.7), channel_id=1, source_target_pairs={{0,1},{1,2},{2,3},{3,0},{4,5},{5,6},{6,7},{7,4},{8,9},{9,10},{10,1... | collective-permute-start | bytes 3145736 | tf_op jit(solution)/shard_map/ppermute | solution.py:204
  41.1 43.6 %copy-start.3 = (bf16[1,3,256,4096]{3,2,1,0:T(8,128)(2,1)S(1)}, bf16[1,3,256,4096]{3,2,1,0:T(8,128)(2,1)}, u32[]{:S(2)}) copy-start(bf16[1,3,256,4096]{3,2,1,0:T(8,128)(2,1)} %get-tuple-element.98) | copy-start | bytes 18874372
  119.5 14.0 %collective-permute-start.4 = (bf16[8,48,1024]{2,1,0:T(8,128)(2,1)S(1)}, bf16[8,48,1024]{2,1,0:T(8,128)(2,1)}, u32[]{:S(2)}, u32[]{:S(2)}) collective-permute-start(bf16[8,48,1024]{2,1,0:T(8,128)(2,1)S(1)} %get-tuple-element.76), channel_id=1, source_target_pairs={{0,64},{64,128},{128,192},{192,256},{256,320},{320,384},{384,448},... | collective-permute-start | bytes 2359304 | tf_op jit(solution)/shard_map/ppermute | solution.py:249
  125.9 9.8 %collective-permute-start.5 = (bf16[16,2,4,4096]{3,2,0,1:T(4,128)(2,1)}, bf16[16,2,4,4096]{3,2,0,1:T(4,128)(2,1)}, u32[]{:S(2)}, u32[]{:S(2)}) collective-permute-start(bf16[16,2,4,4096]{3,2,0,1:T(4,128)(2,1)} %get-tuple-element.102), channel_id=1, source_target_pairs={{0,32},{32,0},{1,33},{33,1},{2,34},{34,2},{3,35},{35,3},{4,36},{36... | collective-permute-start | bytes 3145736 | tf_op jit(solution)/shard_map/ppermute | solution.py:135
  135.7 8.0 %copy-start.2 = (bf16[128,128]{1,0:T(8,128)(2,1)S(1)}, bf16[128,128]{1,0:T(8,128)(2,1)}, u32[]{:S(2)}) copy-start(bf16[128,128]{1,0:T(8,128)(2,1)} %query_ref.1) | copy-start | bytes 98308
  141.5 82.9 %copy-start.8 = (bf16[32,384]{0,1:T(8,128)(2,1)S(1)}, bf16[32,384]{0,1:T(8,128)(2,1)}, u32[]{:S(2)}) copy-start(bf16[32,384]{0,1:T(8,128)(2,1)} %reshape.883) | copy-start | bytes 73732
  143.7 81.0 %copy-start.9 = (bf16[32,384]{0,1:T(8,128)(2,1)S(1)}, bf16[32,384]{0,1:T(8,128)(2,1)}, u32[]{:S(2)}) copy-start(bf16[32,384]{0,1:T(8,128)(2,1)} %reshape.884) | copy-start | bytes 73732
  143.7 81.2 %copy-start.10 = (bf16[32,384]{0,1:T(8,128)(2,1)S(1)}, bf16[32,384]{0,1:T(8,128)(2,1)}, u32[]{:S(2)}) copy-start(bf16[32,384]{0,1:T(8,128)(2,1)} %reshape.885) | copy-start | bytes 73732
  145.6 1.4 copy-start
  146.9 78.3 %copy-start.11 = (bf16[32,384]{0,1:T(8,128)(2,1)S(1)}, bf16[32,384]{0,1:T(8,128)(2,1)}, u32[]{:S(2)}) copy-start(bf16[32,384]{0,1:T(8,128)(2,1)} %reshape.886) | copy-start | bytes 73732
  194.5 32.7 %copy-start.12 = (f32[32]{0:T(128)S(1)}, f32[32]{0:T(128)}, u32[]{:S(2)}) copy-start(f32[32]{0:T(128)} %get-tuple-element.108) | copy-start | bytes 388
  194.5 32.7 %copy-start.14 = (f32[32]{0:T(128)S(1)}, f32[32]{0:T(128)}, u32[]{:S(2)}) copy-start(f32[32]{0:T(128)} %copy-done.13) | copy-start | bytes 388
  195.6 28.8 %all-to-all-start.1 = ((bf16[8,48,1024]{2,1,0:T(8,128)(2,1)}), bf16[8,48,1024]{2,1,0:T(8,128)(2,1)S(1)}, u32[]{:S(2)}, u32[]{:S(2)}) async-start(bf16[8,48,1024]{2,1,0:T(8,128)(2,1)} %broadcast_in_dim.7), calls=%async_computation.1 | async-start | bytes 1572864 | tf_op jit(solution)/shard_map/all_to_all | solution.py:257
  224.4 4.0 %copy-start.4 = (bf16[512,4096]{1,0:T(8,128)(2,1)S(1)}, bf16[512,4096]{1,0:T(8,128)(2,1)}, u32[]{:S(2)}) copy-start(bf16[512,4096]{1,0:T(8,128)(2,1)} %pad_maximum_fusion.2) | copy-start | bytes 12582916
  225.0 12.7 %copy-start.1 = (f32[128,4096]{1,0:T(8,128)S(1)}, f32[128,4096]{1,0:T(8,128)}, u32[]{:S(2)}) copy-start(f32[128,4096]{1,0:T(8,128)} %copy-done) | copy-start | bytes 6291460
  228.4 10.9 %copy-start.6 = (bf16[32,4096]{1,0:T(8,128)(2,1)}, bf16[32,4096]{1,0:T(8,128)(2,1)S(1)}, u32[]{:S(2)}) copy-start(bf16[32,4096]{1,0:T(8,128)(2,1)S(1)} %fusion.4) | copy-start | bytes 786436
Sparse Core Ops, SparseCore 0:
  16.2 89.4 all-gather.1
